TPU v7x, 512 devices: a whole 4x8x8 slice. The times are simulated.
512 devices in a mesh: expert: 32 (over y, x), dp: 16 (over z, core).
Axes of the slice: x: 4, y: 8, z: 8, core: 2. Of those that a mesh axis runs over, the one named last changes fastest.
Arguments:
- tokens: bfloat16 [2048, 7168], P('expert', 'dp'), may hold values from -6 to 6
- cotangent: bfloat16 [2048, 7168], P('expert', 'dp'), may hold values from -6 to 6
- expert_ids: int32 [2048, 8], P('expert'), may hold values from 0 to 15, all different within a row; in each aligned block of 64 rows (0 to 63, 64 to 127, ...) at most 40 rows name the same one
- route_probs: bfloat16 [2048, 8], P('expert'), may hold values from 0.099609375 to 1
- held_before: int32 [32], replicated, may hold values from 0 to 31, each once
- partner: int32 [32], replicated, may hold values from 0 to 31, as said below
- gate_slabs: bfloat16 [32, 7168, 512], P('expert', 'dp'), may hold values from -0.0625 to 0.0625
- up_slabs: bfloat16 [32, 7168, 512], P('expert', 'dp'), may hold values from -0.0625 to 0.0625
- down_slabs: bfloat16 [32, 512, 7168], P('expert', None, 'dp'), may hold values from -0.1875 to 0.1875
Outputs:
- layer_out: bfloat16 [2048, 7168], P('expert', 'dp')
- token_grad: bfloat16 [2048, 7168], P('expert', 'dp')
- gate_grad: bfloat16 [32, 7168, 512], P('expert', 'dp')
- up_grad: bfloat16 [32, 7168, 512], P('expert', 'dp')
- down_grad: bfloat16 [32, 512, 7168], P('expert', None, 'dp')
Inputs may be any that keep to these rules, and one draw needn't show every extreme that they name: `expert_ids`: within the 64 rows of one group (aligned blocks), each row names 8 different experts and no expert is named by more than 40 rows; some expert is named by exactly 40 rows. `held_before`: each slab appears once. partner[partner[j]] == j and partner[j] != j for every j.
All inputs are finite; a program needn't handle non-finite values.
Results may differ from a plain program's by a relative error of at most 0.035.
Values may be sent and summed in bfloat16 or wider, within the bound.
No kernel may reach another device: no remote copies, remote signals or barrier semaphores. Data moves between devices by JAX's collectives and lax.ppermute only.
A program may use at most 64 MiB of HBM per device.

v0:
```python
import jax
import jax.numpy as jnp
from jax import lax
from jax.sharding import PartitionSpec as P


def for_sending(value):

    def short(part):
        return part.astype(jnp.bfloat16) if part.dtype == jnp.float32 else part

    return jax.tree.map(short, value)


def slot_tables(expert_ids, route_probs, slab_ids, capacity):
    owners = slab_ids // 2
    matches = expert_ids[:, :, None] == owners[None, None, :]
    routed = jnp.sum(matches.astype(jnp.int32), axis=1)
    weights = jnp.sum(
        jnp.where(matches, route_probs[:, :, None].astype(jnp.float32), jnp.zeros((), jnp.float32)),
        axis=1,
    )
    position = jnp.cumsum(routed, axis=0) - routed
    slot_iota = lax.broadcasted_iota(jnp.int32, (1, 1, capacity), 2)
    select = (routed[:, :, None] == 1) & (position[:, :, None] == slot_iota)
    return (select.astype(jnp.bfloat16), weights.astype(jnp.bfloat16))


def split_rows(matrix, pieces):
    return matrix.reshape(pieces, matrix.shape[0] // pieces, matrix.shape[1])


def relocate(tensors, partner):
    ordered = tuple((jnp.take(piece, partner, axis=0) for piece in tensors))
    return jax.tree.map(
        lambda part, own: part.astype(own.dtype),
        lax.all_to_all(for_sending(ordered), "expert", split_axis=0, concat_axis=0, tiled=True),
        ordered,
    )


def contract_last(lhs_rows, rhs_rows):
    return lax.dot_general(
        lhs_rows, rhs_rows, (((1,), (1,)), ((), ())), preferred_element_type=jnp.float32
    )


def contract_first(lhs_rows, rhs_rows):
    return lax.dot_general(
        lhs_rows, rhs_rows, (((0,), (0,)), ((), ())), preferred_element_type=jnp.float32
    )


def body(
    tokens,
    cotangent,
    expert_ids,
    route_probs,
    held_before,
    partner,
    gate_slabs,
    up_slabs,
    down_slabs,
):
    experts_n = lax.axis_size("expert")
    gate_mat = gate_slabs[0]
    up_mat = up_slabs[0]
    down_mat = down_slabs[0]
    features = gate_mat.shape[0]
    slab_width = gate_mat.shape[1]
    capacity = 5 * tokens.shape[0] // 8
    select, weights = slot_tables(expert_ids, route_probs, held_before, capacity)
    sent_tokens = jnp.einsum(
        "tnc,tf->ncf", select, tokens, preferred_element_type=jnp.float32
    ).astype(jnp.bfloat16)
    sent_grads = jnp.einsum(
        "tnc,tf->ncf", select, cotangent, preferred_element_type=jnp.float32
    ).astype(jnp.bfloat16)
    sent_probs = jnp.einsum(
        "tnc,tn->nc", select, weights, preferred_element_type=jnp.float32
    ).astype(jnp.bfloat16)
    got_tokens, got_grads, got_probs = (
        lax.all_to_all(sent_tokens, "expert", split_axis=0, concat_axis=0, tiled=True),
        lax.all_to_all(sent_grads, "expert", split_axis=0, concat_axis=0, tiled=True),
        lax.all_to_all(sent_probs, "expert", split_axis=0, concat_axis=0, tiled=True),
    )
    slot_rows = got_tokens.reshape(-1, features)
    grad_rows = got_grads.reshape(-1, features)
    slot_probs = got_probs.reshape(-1, 1).astype(jnp.float32)
    gate_part = jnp.dot(slot_rows, gate_mat, preferred_element_type=jnp.float32)
    up_part = jnp.dot(slot_rows, up_mat, preferred_element_type=jnp.float32)
    gate_sum, up_sum = (
        lax.psum(gate_part.astype(jnp.bfloat16), "dp").astype(jnp.float32),
        lax.psum(up_part.astype(jnp.bfloat16), "dp").astype(jnp.float32),
    )
    activated = jax.nn.silu(gate_sum)
    hidden = (activated * up_sum).astype(jnp.bfloat16)
    out_terms = (jnp.dot(hidden, down_mat, preferred_element_type=jnp.float32) * slot_probs).astype(
        jnp.bfloat16
    )
    scaled = (slot_probs * grad_rows.astype(jnp.float32)).astype(jnp.bfloat16)
    hidden_grad = lax.psum(contract_last(scaled, down_mat).astype(jnp.bfloat16), "dp").astype(
        jnp.float32
    )
    sigmoid_g = jax.nn.sigmoid(gate_sum)
    gate_back = (hidden_grad * up_sum * sigmoid_g * (1.0 + gate_sum * (1.0 - sigmoid_g))).astype(
        jnp.bfloat16
    )
    up_back = (hidden_grad * activated).astype(jnp.bfloat16)
    back_terms = (contract_last(gate_back, gate_mat) + contract_last(up_back, up_mat)).astype(
        jnp.bfloat16
    )
    gate_update = contract_first(slot_rows, gate_back).astype(jnp.bfloat16)
    up_update = contract_first(slot_rows, up_back).astype(jnp.bfloat16)
    down_update = contract_first(hidden, scaled).astype(jnp.bfloat16)
    out_back = out_terms.reshape(experts_n, capacity, features)
    grad_back = back_terms.reshape(experts_n, capacity, features)
    got_out, got_back, gate_piece, up_piece, down_piece = (
        lax.all_to_all(out_back, "expert", split_axis=0, concat_axis=0, tiled=True),
        lax.all_to_all(grad_back, "expert", split_axis=0, concat_axis=0, tiled=True),
        lax.all_to_all(
            split_rows(gate_update, experts_n), "expert", split_axis=0, concat_axis=0, tiled=True
        ),
        lax.all_to_all(
            split_rows(up_update, experts_n), "expert", split_axis=0, concat_axis=0, tiled=True
        ),
        lax.all_to_all(
            split_rows(down_update, experts_n), "expert", split_axis=0, concat_axis=0, tiled=True
        ),
    )
    gate_piece, up_piece, down_piece = relocate((gate_piece, up_piece, down_piece), partner)
    gate_update = gate_piece.reshape(features, slab_width)
    up_update = up_piece.reshape(features, slab_width)
    down_update = down_piece.reshape(slab_width, features)
    layer_out = jnp.einsum(
        "tnc,ncf->tf", select, got_out, preferred_element_type=jnp.float32
    ).astype(jnp.bfloat16)
    token_grad = jnp.einsum(
        "tnc,ncf->tf", select, got_back, preferred_element_type=jnp.float32
    ).astype(jnp.bfloat16)
    return (layer_out, token_grad, gate_update[None], up_update[None], down_update[None])


def solution(mesh):
    placed = (
        P("expert", "dp"),
        P("expert", "dp"),
        P("expert", None),
        P("expert", None),
        P(),
        P(),
        P("expert", "dp", None),
        P("expert", "dp", None),
        P("expert", None, "dp"),
    )
    return jax.shard_map(
        body,
        mesh=mesh,
        in_specs=placed,
        out_specs=(
            P("expert", "dp"),
            P("expert", "dp"),
            P("expert", "dp", None),
            P("expert", "dp", None),
            P("expert", None, "dp"),
        ),
        check_vma=False,
    )
```

profile of v0, /device:TPU:1, one launch (start us, length us, event | category | flops | bytes accessed | tf_op | source)
XLA Modules:
  0.0 452.7 jit_solution(3981748251206411547)
XLA Ops:
  11.3 10.5 %all-to-all-start.1 = ((bf16[32,1,40]{2,1,0:T(2,128)(2,1)}), bf16[32,1,40]{2,1,0:T(2,128)(2,1)S(1)}, u32[]{:S(2)}, u32[]{:S(2)}) async-start(bf16[32,1,40]{2,1,0:T(2,128)(2,1)} %copy.52), calls=%async_computation.1 | async-start | bytes 32768 | tf_op jit(solution)/shard_map/all_to_all | solution.py:85
  21.9 2.4 convolution_convert_fusion.4
  24.3 6.1 %all-to-all-done.1 = bf16[32,1,40]{2,1,0:T(2,128)(2,1)S(1)} async-done(((bf16[32,1,40]{2,1,0:T(2,128)(2,1)}), bf16[32,1,40]{2,1,0:T(2,128)(2,1)S(1)}, u32[]{:S(2)}, u32[]{:S(2)}) %all-to-all-start.1) | async-done | bytes 2592 | tf_op jit(solution)/shard_map/all_to_all | solution.py:85
  30.4 3.9 all-to-all-start
  35.9 28.9 %all-to-all-done = bf16[32,40,448]{2,1,0:T(8,128)(2,1)S(1)} async-done(((bf16[32,40,448]{2,1,0:T(8,128)(2,1)}), bf16[32,40,448]{2,1,0:T(8,128)(2,1)S(1)}, u32[]{:S(2)}, u32[]{:S(2)}) %all-to-all-start) | async-done | bytes 1146912 | tf_op jit(solution)/shard_map/all_to_all | solution.py:83
  64.8 7.0 %all-to-all-start.3 = ((bf16[32,40,448]{2,1,0:T(8,128)(2,1)}), bf16[32,40,448]{2,1,0:T(8,128)(2,1)S(1)}, u32[]{:S(2)}, u32[]{:S(2)}) async-start(bf16[32,40,448]{2,1,0:T(8,128)(2,1)} %convolution_convert_fusion.3), calls=%async_computation.3 | async-start | bytes 2621440 | tf_op jit(solution)/shard_map/all_to_all | solution.py:84
  71.9 2.9 convolution_convert_fusion.1
  76.9 25.1 %all-to-all-done.3 = bf16[32,40,448]{2,1,0:T(8,128)(2,1)S(1)} async-done(((bf16[32,40,448]{2,1,0:T(8,128)(2,1)}), bf16[32,40,448]{2,1,0:T(8,128)(2,1)S(1)}, u32[]{:S(2)}, u32[]{:S(2)}) %all-to-all-start.3) | async-done | bytes 1146912 | tf_op jit(solution)/shard_map/all_to_all | solution.py:84
  105.0 130.8 %all-reduce.3.cloned.1.call-done = (bf16[1280,512]{1,0:T(8,128)(2,1)}, bf16[1280,512]{1,0:T(8,128)(2,1)}, bf16[1280,512]{1,0:T(8,128)(2,1)}) async-done(((bf16[1280,512]{1,0:T(8,128)(2,1)}, bf16[1280,512]{1,0:T(8,128)(2,1)}, bf16[1280,512]{1,0:T(8,128)(2,1)}), (bf16[1280,512]{1,0:T(8,128)(2,1)}, bf16[1280,512]{1,0:T(8,128)(2,1)}, bf16[1280,512]{1,0:T(8,128)(2,1)})) %all-reduce.3.cloned.1.call-update) | async-done | bytes 3932176 | tf_op jit(solution)/shard_map/psum | solution.py:94
  235.8 2.8 convolution_convert_fusion.6
  239.5 9.4 %all-to-all-start.7 = ((bf16[32,14,512]{2,1,0:T(8,128)(2,1)}), bf16[32,14,512]{2,1,0:T(8,128)(2,1)}, u32[]{:S(2)}, u32[]{:S(2)}) async-start(bf16[32,14,512]{2,1,0:T(8,128)(2,1)} %reshape.84), calls=%async_computation.7 | async-start | bytes 1048576 | tf_op jit(solution)/shard_map/all_to_all | solution.py:124
  248.9 4.7 %fusion.5 = (bf16[1280,512]{1,0:T(8,128)(2,1)S(1)}, bf16[1280,512]{1,0:T(8,128)(2,1)}) fusion(bf16[1280,512]{1,0:T(8,128)(2,1)} %get-tuple-element.26, bf16[1280,512]{1,0:T(8,128)(2,1)} %get-tuple-element.28, bf16[1280,512]{1,0:T(8,128)(2,1)} %get-tuple-element.27), kind=kLoop, calls=%fused_computation.19 | loop fusion | flops 10485760 | bytes 6553600 | tf_op jit(solution)/shard_map/convert_element_type | solution.py:106
  255.4 8.8 %all-to-all-done.7 = bf16[32,14,512]{2,1,0:T(8,128)(2,1)} async-done(((bf16[32,14,512]{2,1,0:T(8,128)(2,1)}), bf16[32,14,512]{2,1,0:T(8,128)(2,1)}, u32[]{:S(2)}, u32[]{:S(2)}) %all-to-all-start.7) | async-done | bytes 458784 | tf_op jit(solution)/shard_map/all_to_all | solution.py:124
  264.2 6.3 %all-to-all-start.5 = ((bf16[32,14,512]{2,1,0:T(8,128)(2,1)}), bf16[32,14,512]{2,1,0:T(8,128)(2,1)}, u32[]{:S(2)}, u32[]{:S(2)}) async-start(bf16[32,14,512]{2,1,0:T(8,128)(2,1)} %reshape.83), calls=%async_computation.5 | async-start | bytes 1048576 | tf_op jit(solution)/shard_map/all_to_all | solution.py:121
  273.2 2.8 convolution_convert_fusion.5
  277.0 8.6 %all-to-all-done.5 = bf16[32,14,512]{2,1,0:T(8,128)(2,1)} async-done(((bf16[32,14,512]{2,1,0:T(8,128)(2,1)}), bf16[32,14,512]{2,1,0:T(8,128)(2,1)}, u32[]{:S(2)}, u32[]{:S(2)}) %all-to-all-start.5) | async-done | bytes 458784 | tf_op jit(solution)/shard_map/all_to_all | solution.py:121
  285.5 6.5 %all-to-all-start.9 = ((bf16[32,16,448]{2,1,0:T(8,128)(2,1)}), bf16[32,16,448]{2,1,0:T(8,128)(2,1)}, u32[]{:S(2)}, u32[]{:S(2)}) async-start(bf16[32,16,448]{2,1,0:T(8,128)(2,1)} %bitcast.17), calls=%async_computation.9 | async-start | bytes 1048576 | tf_op jit(solution)/shard_map/all_to_all | solution.py:127
  293.7 2.5 gather_fusion.1
  296.2 2.0 broadcast_select_fusion
  298.2 8.8 %all-to-all-done.9 = bf16[32,16,448]{2,1,0:T(8,128)(2,1)} async-done(((bf16[32,16,448]{2,1,0:T(8,128)(2,1)}), bf16[32,16,448]{2,1,0:T(8,128)(2,1)}, u32[]{:S(2)}, u32[]{:S(2)}) %all-to-all-start.9) | async-done | bytes 458784 | tf_op jit(solution)/shard_map/all_to_all | solution.py:127
  307.0 21.2 %all_to_all.59 = bf16[32,14,512]{2,1,0:T(8,128)(2,1)} all-to-all(bf16[32,14,512]{2,1,0:T(8,128)(2,1)S(1)} %get-tuple-element.31), channel_id=1, replica_groups=mesh['expert'=32,'dp'=16] {'expert'}, dimensions={0} | all-to-all | bytes 917504 | tf_op jit(solution)/shard_map/all_to_all | solution.py:37
  328.2 6.5 %all-to-all-start.6 = ((bf16[32,14,512]{2,1,0:T(8,128)(2,1)}), bf16[32,14,512]{2,1,0:T(8,128)(2,1)S(1)}, u32[]{:S(2)}, u32[]{:S(2)}) async-start(bf16[32,14,512]{2,1,0:T(8,128)(2,1)} %get-tuple-element.32), calls=%async_computation.6 | async-start | bytes 1048576 | tf_op jit(solution)/shard_map/all_to_all | solution.py:37
  337.2 12.0 %all-to-all-done.6 = bf16[32,14,512]{2,1,0:T(8,128)(2,1)S(1)} async-done(((bf16[32,14,512]{2,1,0:T(8,128)(2,1)}), bf16[32,14,512]{2,1,0:T(8,128)(2,1)S(1)}, u32[]{:S(2)}, u32[]{:S(2)}) %all-to-all-start.6) | async-done | bytes 458784 | tf_op jit(solution)/shard_map/all_to_all | solution.py:37
  349.2 6.3 %all-to-all-start.10 = ((bf16[32,16,448]{2,1,0:T(8,128)(2,1)}), bf16[32,16,448]{2,1,0:T(8,128)(2,1)S(1)}, u32[]{:S(2)}, u32[]{:S(2)}) async-start(bf16[32,16,448]{2,1,0:T(8,128)(2,1)} %broadcast_select_fusion.2), calls=%async_computation.10 | async-start | bytes 1048576 | tf_op jit(solution)/shard_map/all_to_all | solution.py:37
  360.0 10.0 %all-to-all-done.10 = bf16[32,16,448]{2,1,0:T(8,128)(2,1)S(1)} async-done(((bf16[32,16,448]{2,1,0:T(8,128)(2,1)}), bf16[32,16,448]{2,1,0:T(8,128)(2,1)S(1)}, u32[]{:S(2)}, u32[]{:S(2)}) %all-to-all-start.10) | async-done | bytes 458784 | tf_op jit(solution)/shard_map/all_to_all | solution.py:37
  370.9 6.3 %all-to-all-start.4 = ((bf16[32,40,448]{2,1,0:T(8,128)(2,1)}), bf16[32,40,448]{2,1,0:T(8,128)(2,1)S(1)}, u32[]{:S(2)}, u32[]{:S(2)}) async-start(bf16[32,40,448]{2,1,0:T(8,128)(2,1)} %bitcast.14), calls=%async_computation.4 | async-start | bytes 2621440 | tf_op jit(solution)/shard_map/all_to_all | solution.py:120
  377.2 2.8 fusion
  380.0 2.4 copy.53
  382.4 24.9 %all-to-all-done.4 = bf16[32,40,448]{2,1,0:T(8,128)(2,1)S(1)} async-done(((bf16[32,40,448]{2,1,0:T(8,128)(2,1)}), bf16[32,40,448]{2,1,0:T(8,128)(2,1)S(1)}, u32[]{:S(2)}, u32[]{:S(2)}) %all-to-all-start.4) | async-done | bytes 1146912 | tf_op jit(solution)/shard_map/all_to_all | solution.py:120
  407.4 7.4 %all-to-all-start.2 = ((bf16[32,40,448]{2,1,0:T(8,128)(2,1)}), bf16[32,40,448]{2,1,0:T(8,128)(2,1)S(1)}, u32[]{:S(2)}, u32[]{:S(2)}) async-start(bf16[32,40,448]{2,1,0:T(8,128)(2,1)} %bitcast.57), calls=%async_computation.2 | async-start | bytes 2621440 | tf_op jit(solution)/shard_map/all_to_all | solution.py:119
  414.8 2.0 copy.57
  421.6 23.2 %all-to-all-done.2 = bf16[32,40,448]{2,1,0:T(8,128)(2,1)S(1)} async-done(((bf16[32,40,448]{2,1,0:T(8,128)(2,1)}), bf16[32,40,448]{2,1,0:T(8,128)(2,1)S(1)}, u32[]{:S(2)}, u32[]{:S(2)}) %all-to-all-start.2) | async-done | bytes 1146912 | tf_op jit(solution)/shard_map/all_to_all | solution.py:119
  (69 shorter events, 32.5 us)
Async XLA Ops:
  7.2 67.7 %copy-start = (bf16[1,448,512]{2,1,0:T(8,128)(2,1)S(1)}, bf16[1,448,512]{2,1,0:T(8,128)(2,1)}, u32[]{:S(2)}) copy-start(bf16[1,448,512]{2,1,0:T(8,128)(2,1)} %param.17) | copy-start | bytes 1376260
  8.7 25.6 %copy-start.9 = (pred[64,32]{0,1:T(8,128)(4,1)}, pred[64,32]{0,1:T(8,128)(4,1)S(1)}, u32[]{:S(2)}) copy-start(pred[64,32]{0,1:T(8,128)(4,1)S(1)} %broadcast_compare_fusion) | copy-start | bytes 6148
  11.3 19.0 %all-to-all-start.1 = ((bf16[32,1,40]{2,1,0:T(2,128)(2,1)}), bf16[32,1,40]{2,1,0:T(2,128)(2,1)S(1)}, u32[]{:S(2)}, u32[]{:S(2)}) async-start(bf16[32,1,40]{2,1,0:T(2,128)(2,1)} %copy.52), calls=%async_computation.1 | async-start | bytes 32768 | tf_op jit(solution)/shard_map/all_to_all | solution.py:85
  24.3 10.1 %copy-start.11 = (bf16[64,448]{1,0:T(8,128)(2,1)S(1)}, bf16[64,448]{1,0:T(8,128)(2,1)}, u32[]{:S(2)}) copy-start(bf16[64,448]{1,0:T(8,128)(2,1)} %param.12) | copy-start | bytes 172036
  30.4 41.5 %copy-start.8 = (bf16[32,1,40]{2,1,0:T(2,128)(2,1)}, bf16[32,1,40]{2,1,0:T(2,128)(2,1)S(1)}, u32[]{:S(2)}) copy-start(bf16[32,1,40]{2,1,0:T(2,128)(2,1)S(1)} %all-to-all-done.1) | copy-start | bytes 7684
  30.4 34.4 %all-to-all-start = ((bf16[32,40,448]{2,1,0:T(8,128)(2,1)}), bf16[32,40,448]{2,1,0:T(8,128)(2,1)S(1)}, u32[]{:S(2)}, u32[]{:S(2)}) async-start(bf16[32,40,448]{2,1,0:T(8,128)(2,1)} %convolution_convert_fusion.4), calls=%async_computation | async-start | bytes 2621440 | tf_op jit(solution)/shard_map/all_to_all | solution.py:83
  64.8 170.9 %copy-start.4 = (bf16[32,40,448]{2,1,0:T(8,128)(2,1)}, bf16[32,40,448]{2,1,0:T(8,128)(2,1)S(1)}, u32[]{:S(2)}) copy-start(bf16[32,40,448]{2,1,0:T(8,128)(2,1)S(1)} %all-to-all-done) | copy-start | bytes 3440644
  64.8 37.1 %all-to-all-start.3 = ((bf16[32,40,448]{2,1,0:T(8,128)(2,1)}), bf16[32,40,448]{2,1,0:T(8,128)(2,1)S(1)}, u32[]{:S(2)}, u32[]{:S(2)}) async-start(bf16[32,40,448]{2,1,0:T(8,128)(2,1)} %convolution_convert_fusion.3), calls=%async_computation.3 | async-start | bytes 2621440 | tf_op jit(solution)/shard_map/all_to_all | solution.py:84
  71.8 163.9 %all-reduce.3.cloned.1.call-start = ((), (), s32[]{:S(2)}) async-start(), calls=%async_computation.11 | async-start | bytes 7864320 | tf_op jit(solution)/shard_map/psum | solution.py:94
  102.0 1.0 copy-start.13
  239.5 24.7 %all-to-all-start.7 = ((bf16[32,14,512]{2,1,0:T(8,128)(2,1)}), bf16[32,14,512]{2,1,0:T(8,128)(2,1)}, u32[]{:S(2)}, u32[]{:S(2)}) async-start(bf16[32,14,512]{2,1,0:T(8,128)(2,1)} %reshape.84), calls=%async_computation.7 | async-start | bytes 1048576 | tf_op jit(solution)/shard_map/all_to_all | solution.py:124
  248.9 4.7 %copy-start.5 = (bf16[32,40,448]{2,1,0:T(8,128)(2,1)S(1)}, bf16[32,40,448]{2,1,0:T(8,128)(2,1)}, u32[]{:S(2)}) copy-start(bf16[32,40,448]{2,1,0:T(8,128)(2,1)} %copy-done.4) | copy-start | bytes 3440644
  264.2 21.3 %all-to-all-start.5 = ((bf16[32,14,512]{2,1,0:T(8,128)(2,1)}), bf16[32,14,512]{2,1,0:T(8,128)(2,1)}, u32[]{:S(2)}, u32[]{:S(2)}) async-start(bf16[32,14,512]{2,1,0:T(8,128)(2,1)} %reshape.83), calls=%async_computation.5 | async-start | bytes 1048576 | tf_op jit(solution)/shard_map/all_to_all | solution.py:121
  276.0 16.1 %copy-start.14 = (s32[32]{0:T(128)S(1)}, s32[32]{0:T(128)}, u32[]{:S(2)}) copy-start(s32[32]{0:T(128)} %param.16) | copy-start | bytes 388
  285.5 21.5 %all-to-all-start.9 = ((bf16[32,16,448]{2,1,0:T(8,128)(2,1)}), bf16[32,16,448]{2,1,0:T(8,128)(2,1)}, u32[]{:S(2)}, u32[]{:S(2)}) async-start(bf16[32,16,448]{2,1,0:T(8,128)(2,1)} %bitcast.17), calls=%async_computation.9 | async-start | bytes 1048576 | tf_op jit(solution)/shard_map/all_to_all | solution.py:127
  328.2 21.0 %all-to-all-start.6 = ((bf16[32,14,512]{2,1,0:T(8,128)(2,1)}), bf16[32,14,512]{2,1,0:T(8,128)(2,1)S(1)}, u32[]{:S(2)}, u32[]{:S(2)}) async-start(bf16[32,14,512]{2,1,0:T(8,128)(2,1)} %get-tuple-element.32), calls=%async_computation.6 | async-start | bytes 1048576 | tf_op jit(solution)/shard_map/all_to_all | solution.py:37
  349.2 7.1 %copy-start.2 = (bf16[32,14,512]{2,1,0:T(8,128)(2,1)}, bf16[32,14,512]{2,1,0:T(8,128)(2,1)S(1)}, u32[]{:S(2)}) copy-start(bf16[32,14,512]{2,1,0:T(8,128)(2,1)S(1)} %all-to-all-done.6) | copy-start | bytes 1376260
  349.2 20.8 %all-to-all-start.10 = ((bf16[32,16,448]{2,1,0:T(8,128)(2,1)}), bf16[32,16,448]{2,1,0:T(8,128)(2,1)S(1)}, u32[]{:S(2)}, u32[]{:S(2)}) async-start(bf16[32,16,448]{2,1,0:T(8,128)(2,1)} %broadcast_select_fusion.2), calls=%async_computation.10 | async-start | bytes 1048576 | tf_op jit(solution)/shard_map/all_to_all | solution.py:37
  355.5 1.3 copy-start.6
  355.5 1.7 copy-start.7
  355.5 1.8 copy-start.12
  370.1 0.8 copy-start.3
  370.1 7.1 %copy-start.1 = (bf16[1280,512]{1,0:T(8,128)(2,1)S(1)}, bf16[1280,512]{1,0:T(8,128)(2,1)}, u32[]{:S(2)}) copy-start(bf16[1280,512]{1,0:T(8,128)(2,1)} %get-tuple-element.30) | copy-start | bytes 3932164
  370.9 36.5 %all-to-all-start.4 = ((bf16[32,40,448]{2,1,0:T(8,128)(2,1)}), bf16[32,40,448]{2,1,0:T(8,128)(2,1)S(1)}, u32[]{:S(2)}, u32[]{:S(2)}) async-start(bf16[32,40,448]{2,1,0:T(8,128)(2,1)} %bitcast.14), calls=%async_computation.4 | async-start | bytes 2621440 | tf_op jit(solution)/shard_map/all_to_all | solution.py:120
  407.4 37.5 %all-to-all-start.2 = ((bf16[32,40,448]{2,1,0:T(8,128)(2,1)}), bf16[32,40,448]{2,1,0:T(8,128)(2,1)S(1)}, u32[]{:S(2)}, u32[]{:S(2)}) async-start(bf16[32,40,448]{2,1,0:T(8,128)(2,1)} %bitcast.57), calls=%async_computation.2 | async-start | bytes 2621440 | tf_op jit(solution)/shard_map/all_to_all | solution.py:119
  414.8 5.9 %copy-start.10 = (pred[64,32]{0,1:T(8,128)(4,1)S(1)}, pred[64,32]{0,1:T(8,128)(4,1)}, u32[]{:S(2)}) copy-start(pred[64,32]{0,1:T(8,128)(4,1)} %copy-done.9) | copy-start | bytes 6148
Sparse Core Ops, SparseCore 0:
  105.1 130.6 all-reduce.2
where the time goes:
time: 458 us; the launch traced here: 453 us
  waiting for transfers between devices  287 us (63%)
  starting transfers between devices  70.1 us (15%)
  matrix products  24.4 us (5%)
  local copies, waits for them, and re-layouts  23.5 us (5%)
  blocking collectives  21.2 us (5%)
  between operations  14.3 us (3%)
  other arithmetic  11.9 us (3%)
    psum x1, waiting for transfers between devices, body(): lax.psum(up_part.astype(jnp.bfloat16), 'dp').astype(jnp.float32)  131 us
    all_to_all x1, waiting for transfers between devices, body(): lax.all_to_all(sent_tokens, 'expert', split_axis=0, concat_axis=0, tiled=...  28.9 us
    all_to_all x1, waiting for transfers between devices, body(): lax.all_to_all(sent_grads, 'expert', split_axis=0, concat_axis=0, tiled=T...  25.1 us
    all_to_all x1, waiting for transfers between devices, body(): lax.all_to_all(grad_back, 'expert', split_axis=0, concat_axis=0, tiled=True)  24.9 us
    all_to_all x1, waiting for transfers between devices, body(): lax.all_to_all(out_back, 'expert', split_axis=0, concat_axis=0, tiled=True)  23.2 us
    all_to_all x2, waiting for transfers between devices, relocate(): lax.all_to_all(for_sending(ordered), 'expert', split_axis=0, concat_axis=...  22.1 us
    all_to_all x1, blocking collectives, relocate(): lax.all_to_all(for_sending(ordered), 'expert', split_axis=0, concat_axis=...  21.2 us
    all_to_all x2, starting transfers between devices, relocate(): lax.all_to_all(for_sending(ordered), 'expert', split_axis=0, concat_axis=...  12.7 us
  transfers between devices with their start and end apart: 11, of which 11 were waited for; matrix products, arithmetic and copies ran while one was open for 10% of the time, Pallas kernels for 0%

commit v1 on v0

v1 whole, which is shorter than its diff:
```python
import functools

import jax
import jax.numpy as jnp
from jax import lax
from jax.experimental import pallas as pl
from jax.experimental.pallas import tpu as pltpu
from jax.sharding import Mesh, PartitionSpec as P

TOK = 64
CAP = 40
FEAT = 448
WIDE = 512
HID = 512
QUAD = 4 * TOK
QROWS = 4 * CAP
HALF = 2 * CAP
QUADS = 8
TAIL = 3
ROWS = QUADS * QROWS
BUNDLE = 256
BF = jnp.bfloat16
F32 = jnp.float32


def dot(lhs, rhs):
    return jnp.dot(lhs, rhs, preferred_element_type=F32)


def dot_last(lhs, rhs):
    return lax.dot_general(lhs, rhs, (((1,), (1,)), ((), ())), preferred_element_type=F32)


def dot_first(lhs, rhs):
    return lax.dot_general(lhs, rhs, (((0,), (0,)), ((), ())), preferred_element_type=F32)


def weight_rows(tail, experts):
    lane = lax.broadcasted_iota(jnp.int32, (8, 128), 1)
    row = lax.broadcasted_iota(jnp.int32, (8, 128), 0)
    hit = lane < 0
    for i, expert in enumerate(experts):
        hit = hit | ((row == i) & (lane == TOK + expert))
    return dot_last(jnp.where(hit, 1.0, 0.0).astype(BF), tail)


def slot_places(weights):
    count = weights.shape[1]
    routed = weights > 0.0
    source = lax.broadcasted_iota(jnp.int32, (count, count), 0)
    target = lax.broadcasted_iota(jnp.int32, (count, count), 1)
    earlier = (source < target) & ((source >> 6) == (target >> 6))
    position = dot(jnp.where(routed, 1.0, 0.0).astype(BF), jnp.where(earlier, 1.0, 0.0).astype(BF))
    group = lax.broadcasted_iota(jnp.int32, weights.shape, 1) >> 6
    return jnp.where(routed, position.astype(jnp.int32) + CAP * group, -1)


def one_hot(place, rows):
    return lax.broadcasted_iota(jnp.int32, (rows, place.shape[1]), 0) == place


def quad_select(tail, expert):
    weights = weight_rows(tail, (expert,))
    place = slot_places(weights)
    return weights[0:1], place[0:1]


def slot_weights(hit, weights):
    return jnp.sum(jnp.where(hit, weights, 0.0), axis=1, keepdims=True)


def as_matrix(hit):
    return jnp.where(hit, 1.0, 0.0).astype(BF)


def own_half_first(place, core):
    moved = place - HALF * core
    return jnp.where(place < 0, -1, jnp.where(moved < 0, moved + QROWS, moved))


def gate_up_kernel(info, tok_ref, gate_ref, up_ref, keep_ref, send_ref):
    weights, place = quad_select(tok_ref[:, TAIL * 128 :], info[0])
    pick = as_matrix(one_hot(own_half_first(place, info[1]), QROWS))
    rows = dot(pick, tok_ref[:, :FEAT]).astype(BF)
    gate = dot(rows, gate_ref[...]).astype(BF)
    up = dot(rows, up_ref[...]).astype(BF)
    keep_ref[0, :, :HID] = gate[:HALF]
    keep_ref[0, :, HID:] = up[:HALF]
    send_ref[0, :, :HID] = gate[HALF:]
    send_ref[0, :, HID:] = up[HALF:]


def hidden_grad_kernel(info, tail_ref, cot_ref, down_ref, keep_ref, send_ref):
    weights, place = quad_select(tail_ref[...], info[0])
    hit = one_hot(own_half_first(place, info[1]), QROWS)
    scaled = (slot_weights(hit, weights) * dot(as_matrix(hit), cot_ref[:, :FEAT])).astype(BF)
    grad = dot_last(scaled, down_ref[...]).astype(BF)
    keep_ref[0] = grad[:HALF]
    send_ref[0] = grad[HALF:]


def activation_kernel(gate_up_ref, grad_ref, out_ref):
    both = jnp.sum(gate_up_ref[...].astype(F32), axis=0)
    gate, up = both[:, :HID], both[:, HID:]
    grad = jnp.sum(grad_ref[...].astype(F32), axis=0)
    sig = jax.nn.sigmoid(gate)
    activated = gate * sig
    out_ref[0:HALF] = (activated * up).astype(BF)
    out_ref[HALF : 2 * HALF] = (grad * up * sig * (1.0 + gate * (1.0 - sig))).astype(BF)
    out_ref[2 * HALF : 3 * HALF] = (grad * activated).astype(BF)
    out_ref[3 * HALF :] = jnp.zeros((BUNDLE - 3 * HALF, HID), BF)


def bundle_part(acts_ref, part):
    picked = acts_ref[:, part * HALF : (part + 1) * HALF, :]
    return picked.reshape(picked.shape[0] * HALF, HID)


def terms_kernel(info, tail_ref, acts_ref, gate_ref, up_ref, down_ref, out_ref):
    weights, place = quad_select(tail_ref[...], info[0])
    factor = slot_weights(one_hot(place, QROWS), weights)
    out = (dot(bundle_part(acts_ref, 0), down_ref[...]) * factor).astype(BF)
    back = dot_last(bundle_part(acts_ref, 1), gate_ref[...]) + dot_last(bundle_part(acts_ref, 2), up_ref[...])
    out_ref[...] = jnp.concatenate([out, back.astype(BF)], axis=1)


def merge_kernel(info, tail_ref, rows_ref, out_ref):
    weights = weight_rows(tail_ref[...], tuple(info[4 + i] for i in range(4)))
    place = slot_places(weights)
    total = jnp.zeros(out_ref.shape, F32)
    for i in range(4):
        total = total + dot_first(as_matrix(one_hot(place[i : i + 1], HALF)), rows_ref[i])
    out_ref[...] = total.astype(BF)


def new_rows_kernel(info, tok_ref, cot_ref, rows_ref, scaled_ref):
    weights, place = quad_select(tok_ref[:, TAIL * 128 :], info[2])
    hit = one_hot(place, QROWS)
    pick = as_matrix(hit)
    rows_ref[...] = dot(pick, tok_ref[:, :FEAT]).astype(BF)
    scaled_ref[...] = (slot_weights(hit, weights) * dot(pick, cot_ref[:, :FEAT])).astype(BF)


def slab_grad_kernel(rows_ref, scaled_ref, acts_ref, gate_ref, up_ref, down_ref):
    gate_ref[...] = dot_first(rows_ref[...], bundle_part(acts_ref, 1)).astype(BF)
    up_ref[...] = dot_first(rows_ref[...], bundle_part(acts_ref, 2)).astype(BF)
    down_ref[...] = dot_first(bundle_part(acts_ref, 0), scaled_ref[...]).astype(BF)


def call(kernel, grid, in_specs, out_specs, out_shape, flops, moved, info, *operands):
    return pl.pallas_call(
        kernel,
        grid_spec=pltpu.PrefetchScalarGridSpec(
            num_scalar_prefetch=1, grid=grid, in_specs=in_specs, out_specs=out_specs
        ),
        out_shape=out_shape,
        compiler_params=pltpu.CompilerParams(vmem_limit_bytes=32 * 1024 * 1024),
        cost_estimate=pl.CostEstimate(flops=flops, bytes_accessed=moved, transcendentals=0),
    )(info, *operands)


def whole(*shape):
    return pl.BlockSpec(shape, lambda q, info: (0,) * len(shape))


def quad_block(*shape):
    return pl.BlockSpec(shape, lambda q, info: (q,) + (0,) * (len(shape) - 1))


def tail_block():
    return pl.BlockSpec((QUAD, 128), lambda q, info: (q, TAIL))


def shaped(*shape):
    return jax.ShapeDtypeStruct(shape, BF)


def swap(value):
    return lax.ppermute(value, "core", [(0, 1), (1, 0)])


def exchange(value, axes):
    return lax.all_to_all(value, axes, split_axis=0, concat_axis=0, tiled=True)


def dp_scatter_sum(keep, send):
    pair = (keep.astype(F32) + swap(send).astype(F32)).astype(BF)
    return exchange(pair, "z")


def body(tokens, cotangent, expert_ids, route_probs, held_before, partner, gate_slabs, up_slabs, down_slabs):
    gate, up, down = gate_slabs[0], up_slabs[0], down_slabs[0]
    here_y, here_x, core = lax.axis_index("y"), lax.axis_index("x"), lax.axis_index("core")
    here = here_y * 4 + here_x
    experts = held_before // 2
    new_expert = experts[partner[here]]
    row_experts = lax.dynamic_slice(experts, (here_y * 4,), (4,))
    info = jnp.concatenate(
        [jnp.stack([experts[here], core, new_expert, here_x]).astype(jnp.int32), row_experts.astype(jnp.int32)]
    )

    cot_all = lax.all_gather(jnp.pad(cotangent, ((0, 0), (0, WIDE - FEAT))), ("y", "x"), tiled=True)
    names = lax.broadcasted_iota(jnp.int32, (1, 1, 16), 2)
    dense = jnp.sum(
        jnp.where(expert_ids[:, :, None] == names, route_probs[:, :, None].astype(F32), 0.0), axis=1
    ).astype(BF)
    packed = jnp.concatenate([tokens, dense, jnp.zeros((TOK, WIDE - FEAT - 16), BF)], axis=1)
    column = exchange(jnp.broadcast_to(packed, (8, TOK, WIDE)), "y").reshape(8 * TOK, WIDE)
    tok_all = exchange(jnp.broadcast_to(column, (4, 8 * TOK, WIDE)), "x").reshape(32 * TOK, WIDE)

    halves = (quad_block(1, HALF, 2 * HID), quad_block(1, HALF, 2 * HID))
    keep, send = call(
        gate_up_kernel,
        (QUADS,),
        [quad_block(QUAD, WIDE), whole(FEAT, HID), whole(FEAT, HID)],
        halves,
        (shaped(QUADS, HALF, 2 * HID), shaped(QUADS, HALF, 2 * HID)),
        3_000_000_000,
        6_000_000,
        info,
        tok_all,
        gate,
        up,
    )
    gate_up = dp_scatter_sum(keep, send)

    cot_spec = pl.BlockSpec((4, 1, TOK, WIDE), lambda q, info: (q % 2, q // 2, 0, 0))
    cot_view = cot_all.reshape(2, 4, 4, TOK, WIDE)
    cot_spec = pl.BlockSpec((None, 4, None, TOK, WIDE), lambda q, info: (q % 2, 0, q // 2, 0, 0))

    def with_cot(kernel, position):
        def run(*refs):
            refs = list(refs)
            refs[position] = _Flat(refs[position])
            kernel(*refs)

        return run

    keep, send = call(
        with_cot(hidden_grad_kernel, 2),
        (QUADS,),
        [tail_block(), cot_spec, whole(HID, FEAT)],
        (quad_block(1, HALF, HID), quad_block(1, HALF, HID)),
        (shaped(QUADS, HALF, HID), shaped(QUADS, HALF, HID)),
        1_500_000_000,
        5_000_000,
        info,
        tok_all,
        cot_view,
        down,
    )
    hidden_grad = dp_scatter_sum(keep, send)

    acts = pl.pallas_call(
        activation_kernel,
        out_shape=shaped(BUNDLE, HID),
        compiler_params=pltpu.CompilerParams(vmem_limit_bytes=32 * 1024 * 1024),
        cost_estimate=pl.CostEstimate(flops=3_000_000, bytes_accessed=2_300_000, transcendentals=50_000),
    )(gate_up, hidden_grad)

    own_acts = lax.all_gather(acts, ("z", "core"), tiled=True).reshape(16, BUNDLE, HID)
    spread = exchange(acts.reshape(32, 8, HID), ("y", "x"))
    moved = exchange(jnp.take(spread, partner, axis=0), ("y", "x")).reshape(BUNDLE, HID)

    terms = call(
        terms_kernel,
        (QUADS,),
        [tail_block(), quad_block(2, BUNDLE, HID), whole(FEAT, HID), whole(FEAT, HID), whole(HID, FEAT)],
        quad_block(QROWS, 2 * FEAT),
        shaped(ROWS, 2 * FEAT),
        2_000_000_000,
        8_000_000,
        info,
        tok_all,
        own_acts,
        gate,
        up,
        down,
    )
    new_acts = lax.all_gather(moved, ("z", "core"), tiled=True).reshape(16, BUNDLE, HID)

    returned = exchange(terms.reshape(4, 8 * CAP, 2 * FEAT), "x")
    merged = call(
        merge_kernel,
        (4,),
        [
            pl.BlockSpec((2 * TOK, 128), lambda q, info: (info[3] * 4 + q, TAIL)),
            pl.BlockSpec((4, HALF, 2 * FEAT), lambda q, info: (0, q, 0)),
        ],
        quad_block(2 * TOK, 2 * FEAT),
        shaped(8 * TOK, 2 * FEAT),
        300_000_000,
        3_500_000,
        info,
        tok_all,
        returned,
    )
    home = exchange(merged.reshape(8, TOK, 2 * FEAT), "y")

    rows, scaled = call(
        with_cot(new_rows_kernel, 2),
        (QUADS,),
        [quad_block(QUAD, WIDE), cot_spec],
        (quad_block(QROWS, FEAT), quad_block(QROWS, FEAT)),
        (shaped(ROWS, FEAT), shaped(ROWS, FEAT)),
        600_000_000,
        6_500_000,
        info,
        tok_all,
        cot_view,
    )
    gate_grad, up_grad, down_grad = pl.pallas_call(
        slab_grad_kernel,
        out_shape=(shaped(FEAT, HID), shaped(FEAT, HID), shaped(HID, FEAT)),
        compiler_params=pltpu.CompilerParams(vmem_limit_bytes=32 * 1024 * 1024),
        cost_estimate=pl.CostEstimate(flops=1_800_000_000, bytes_accessed=8_000_000, transcendentals=0),
    )(rows, scaled, new_acts)

    total = jnp.sum(home.astype(F32), axis=0).astype(BF)
    return (total[:, :FEAT], total[:, FEAT:], gate_grad[None], up_grad[None], down_grad[None])


class _Flat:
    def __init__(self, ref):
        self.ref = ref

    def __getitem__(self, index):
        return self.ref[...].reshape(QUAD, WIDE)[index]


def solution(mesh):
    fine = Mesh(mesh.devices.reshape(8, 4, 8, 2), ("y", "x", "z", "core"))
    expert, dp = ("y", "x"), ("z", "core")
    return jax.shard_map(
        body,
        mesh=fine,
        in_specs=(
            P(expert, dp),
            P(expert, dp),
            P(expert, None),
            P(expert, None),
            P(),
            P(),
            P(expert, dp, None),
            P(expert, dp, None),
            P(expert, None, dp),
        ),
        out_specs=(
            P(expert, dp),
            P(expert, dp),
            P(expert, dp, None),
            P(expert, dp, None),
            P(expert, None, dp),
        ),
        check_vma=False,
    )
```

time: 458 us -> 314 us (0.69)
  waiting for transfers between devices: 287 us -> 94.6 us
  blocking collectives: 21.2 us -> 107 us
  starting transfers between devices: 70.1 us -> 33.5 us
  Pallas kernels: 0 us -> 32.1 us
  matrix products: 24.4 us -> 0 us
    psum x1 -> x0, waiting for transfers between devices: 131 us -> none  [body(): lax.psum(up_part.astype(jnp.bfloat16), 'dp').astype(jnp.float32)]
    all_to_all x10 -> x4, waiting for transfers between devices: 156 us -> 59.7 us  [exchange(): return lax.all_to_all(value, axes, split_axis=0, concat_axis=0, tiled=True)]
    all_to_all x1 -> x4, blocking collectives: 21.2 us -> 107 us  [exchange(): return lax.all_to_all(value, axes, split_axis=0, concat_axis=0, tiled=True)]
    all_to_all x10 -> x4, starting transfers between devices: 70.1 us -> 25.1 us  [exchange(): return lax.all_to_all(value, axes, split_axis=0, concat_axis=0, tiled=True)]
    all_gather x0 -> x3, waiting for transfers between devices: none -> 34.8 us  [the longest x1 32.3 us: body(): lax.all_gather(jnp.pad(cotangent, ((0, 0), (0, WIDE - FEAT))), ('y', 'x')...]
    pallas_call x0 -> x7, Pallas kernels: none -> 32.1 us  [the longest x5 28.6 us: call(): pl.pallas_call(kernel, grid_spec=pltpu.PrefetchScalarGridSpec(num_scalar_...]
    dot_general x14 -> x0, matrix products: 24.4 us -> none  [the longest x3 6.38 us: contract_first(): lax.dot_general(lhs_rows, rhs_rows, (((0,), (0,)), ((), ())), preferred_e...]
    ppermute x0 -> x2, starting transfers between devices: none -> 8.25 us  [swap(): return lax.ppermute(value, 'core', [(0, 1), (1, 0)])]
  transfers between devices with their start and end apart: 11 -> 9, of which waited for: 11 -> 6; matrix products, arithmetic and copies ran while one was open for 10% -> 5% of each run, Pallas kernels for 0% -> 8%
where the time goes in v1:
time: 314 us; the launch traced here: 313 us
  blocking collectives  107 us (34%)
  waiting for transfers between devices  94.6 us (30%)
  starting transfers between devices  33.5 us (11%)
  Pallas kernels  32.1 us (10%)
  local copies, waits for them, and re-layouts  21 us (7%)
  between operations  15.9 us (5%)
  other arithmetic  9.1 us (3%)
    all_to_all x4, blocking collectives, exchange(): return lax.all_to_all(value, axes, split_axis=0, concat_axis=0, tiled=True)  107 us
    all_to_all x4, waiting for transfers between devices, exchange(): return lax.all_to_all(value, axes, split_axis=0, concat_axis=0, tiled=True)  59.7 us
    all_gather x1, waiting for transfers between devices, body(): lax.all_gather(jnp.pad(cotangent, ((0, 0), (0, WIDE - FEAT))), ('y', 'x')...  32.3 us
    pallas_call x5, Pallas kernels, call(): pl.pallas_call(kernel, grid_spec=pltpu.PrefetchScalarGridSpec(num_scalar_...  28.6 us
    all_to_all x4, starting transfers between devices, exchange(): return lax.all_to_all(value, axes, split_axis=0, concat_axis=0, tiled=True)  25.1 us
    unnamed x30, local copies, waits for them, and re-layouts  12.2 us
    ppermute x2, starting transfers between devices, swap(): return lax.ppermute(value, 'core', [(0, 1), (1, 0)])  8.25 us
  transfers between devices with their start and end apart: 9, of which 6 were waited for; matrix products, arithmetic and copies ran while one was open for 5% of the time, Pallas kernels for 8%

profile of v1, /device:TPU:1, one launch (start us, length us, event | category | flops | bytes accessed | tf_op | source)
XLA Modules:
  0.0 313.1 jit_solution(11980622424409964304)
XLA Ops:
  7.2 1.5 pad.4
  11.3 22.2 %all_to_all.40 = bf16[8,64,512]{2,1,0:T(8,128)(2,1)S(1)} all-to-all(bf16[8,64,512]{2,1,0:T(8,128)(2,1)S(1)} %broadcast_in_dim.47), channel_id=1, replica_groups=mesh['y'=8,'x'=4,'z'=8,'core'=2] {'y'}, dimensions={0} | all-to-all | bytes 1048576 | tf_op jit(solution)/shard_map/all_to_all | solution.py:183
  33.5 1.5 broadcast_in_dim.48
  35.0 5.4 %all-to-all-start.1 = ((bf16[4,512,512]{2,1,0:T(8,128)(2,1)}), bf16[4,512,512]{2,1,0:T(8,128)(2,1)S(1)}, u32[]{:S(2)}, u32[]{:S(2)}) async-start(bf16[4,512,512]{2,1,0:T(8,128)(2,1)} %broadcast_in_dim.48), calls=%async_computation.1 | async-start | bytes 4194304 | tf_op jit(solution)/shard_map/all_to_all | solution.py:183
  43.8 1.4 concatenate.6.info.refs_0_
  45.2 19.3 %all-to-all-done.1 = bf16[4,512,512]{2,1,0:T(8,128)(2,1)S(1)} async-done(((bf16[4,512,512]{2,1,0:T(8,128)(2,1)}), bf16[4,512,512]{2,1,0:T(8,128)(2,1)S(1)}, u32[]{:S(2)}, u32[]{:S(2)}) %all-to-all-start.1) | async-done | bytes 2097184 | tf_op jit(solution)/shard_map/all_to_all | solution.py:183
  64.5 32.3 %all-gather.4.cloned.1.call-done = bf16[2048,512]{1,0:T(8,128)(2,1)} async-done(((bf16[64,512]{1,0:T(8,128)(2,1)}), bf16[2048,512]{1,0:T(8,128)(2,1)}) %all-gather.4.cloned.1.call-update) | async-done | bytes 2097168 | tf_op jit(solution)/shard_map/all_gather | solution.py:202
  96.8 1.6 copy-done.2
  98.4 6.2 %shard_map.129 = (bf16[8,80,512]{2,1,0:T(8,128)(2,1)S(1)}, bf16[8,80,512]{2,1,0:T(8,128)(2,1)S(1)}) custom-call(s32[8]{0:T(128)S(1)} %concatenate.6.info.refs_0_, bf16[2048,512]{1,0:T(8,128)(2,1)S(1)} %bitcast.18, bf16[2,4,4,64,512]{4,3,2,1,0:T(8,128)(2,1)S(1)} %bitcast.28, bf16[512,448]{1,0:T(8,128)(2,1)S(1)} %bitcast.26), custom_call_target="tpu_custom_call" | custom-call | flops 1500000000 | bytes 5000000 | tf_op jit(solution)/shard_map/pallas_call | solution.py:151
  104.6 6.3 %collective-permute-start.1 = (bf16[8,80,512]{2,1,0:T(8,128)(2,1)S(1)}, bf16[8,80,512]{2,1,0:T(8,128)(2,1)S(1)}, u32[]{:S(2)}, u32[]{:S(2)}) collective-permute-start(bf16[8,80,512]{2,1,0:T(8,128)(2,1)S(1)} %get-tuple-element.17), channel_id=1, source_target_pairs={{0,1},{1,0},{2,3},{3,2},{4,5},{5,4},{6,7},{7,6},{8,9},{9,8},{10,11... | collective-permute-start | bytes 1966088 | tf_op jit(solution)/shard_map/ppermute | solution.py:179
  111.0 6.9 %shard_map.128 = (bf16[8,80,1024]{2,1,0:T(8,128)(2,1)S(1)}, bf16[8,80,1024]{2,1,0:T(8,128)(2,1)}) custom-call(s32[8]{0:T(128)S(1)} %concatenate.6.info.refs_0_, bf16[2048,512]{1,0:T(8,128)(2,1)S(1)} %bitcast.19, bf16[448,512]{1,0:T(8,128)(2,1)S(1)} %bitcast.31, bf16[448,512]{1,0:T(8,128)(2,1)S(1)} %bitcast.33), custom_call_target="tpu_custom_call" | custom-call | flops 3000000000 | bytes 6000000 | tf_op jit(solution)/shard_map/pallas_call | solution.py:151
  119.0 1.9 collective-permute-start
  121.9 7.1 %all-to-all-start.3 = ((bf16[8,80,512]{2,1,0:T(8,128)(2,1)}), bf16[8,80,512]{2,1,0:T(8,128)(2,1)S(1)}, u32[]{:S(2)}, u32[]{:S(2)}) async-start(bf16[8,80,512]{2,1,0:T(8,128)(2,1)} %add_convert_fusion.1), calls=%async_computation.3 | async-start | bytes 1310720 | tf_op jit(solution)/shard_map/all_to_all | solution.py:183
  129.1 3.4 %add_convert_fusion = bf16[8,80,1024]{2,1,0:T(8,128)(2,1)} fusion(bf16[8,80,1024]{2,1,0:T(8,128)(2,1)} %collective-permute-done, bf16[8,80,1024]{2,1,0:T(8,128)(2,1)} %copy-done.4), kind=kLoop, calls=%fused_computation.1 | loop fusion | flops 2621440 | bytes 3932160 | tf_op jit(solution)/shard_map/convert_element_type | solution.py:187
  132.5 17.3 %all-to-all-done.3.grad_ref = bf16[8,80,512]{2,1,0:T(8,128)(2,1)S(1)} async-done(((bf16[8,80,512]{2,1,0:T(8,128)(2,1)}), bf16[8,80,512]{2,1,0:T(8,128)(2,1)S(1)}, u32[]{:S(2)}, u32[]{:S(2)}) %all-to-all-start.3) | async-done | bytes 655392 | tf_op jit(solution)/shard_map/all_to_all | solution.py:183
  149.8 38.0 %all_to_all.41.gate_up_ref = bf16[8,80,1024]{2,1,0:T(8,128)(2,1)S(1)} all-to-all(bf16[8,80,1024]{2,1,0:T(8,128)(2,1)} %add_convert_fusion), channel_id=1, replica_groups=mesh['y'=8,'x'=4,'z'=8,'core'=2] {'z'}, dimensions={0} | all-to-all | bytes 2621440 | tf_op jit(solution)/shard_map/all_to_all | solution.py:183
  188.9 5.7 %all-to-all-start.6 = ((bf16[32,8,512]{2,1,0:T(8,128)(2,1)}), bf16[32,8,512]{2,1,0:T(8,128)(2,1)}, u32[]{:S(2)}, u32[]{:S(2)}) async-start(bf16[32,8,512]{2,1,0:T(8,128)(2,1)} %bitcast.12), calls=%async_computation.6 | async-start | bytes 524288 | tf_op jit(solution)/shard_map/all_to_all | solution.py:183
  194.7 11.1 %all-to-all-done.6 = bf16[32,8,512]{2,1,0:T(8,128)(2,1)} async-done(((bf16[32,8,512]{2,1,0:T(8,128)(2,1)}), bf16[32,8,512]{2,1,0:T(8,128)(2,1)}, u32[]{:S(2)}, u32[]{:S(2)}) %all-to-all-start.6) | async-done | bytes 262176 | tf_op jit(solution)/shard_map/all_to_all | solution.py:183
  205.8 2.2 gather_fusion
  209.1 15.0 %all_to_all.42 = bf16[32,8,512]{2,1,0:T(8,128)(2,1)} all-to-all(bf16[32,8,512]{2,1,0:T(8,128)(2,1)S(1)} %broadcast_select_fusion), channel_id=1, replica_groups=mesh['y'=8,'x'=4,'z'=8,'core'=2] {'y','x'}, dimensions={0} | all-to-all | bytes 524288 | tf_op jit(solution)/shard_map/all_to_all | solution.py:183
  224.1 2.5 all-gather.6.cloned.1.call-done
  226.7 2.2 copy-done
  228.8 6.2 %shard_map.131 = bf16[1280,896]{1,0:T(8,128)(2,1)S(1)} custom-call(s32[8]{0:T(128)S(1)} %concatenate.6.info.refs_0_, bf16[2048,512]{1,0:T(8,128)(2,1)S(1)} %bitcast.20, bf16[16,256,512]{2,1,0:T(8,128)(2,1)S(1)} %bitcast.24, bf16[448,512]{1,0:T(8,128)(2,1)S(1)} %bitcast.32, bf16[448,512]{1,0:T(8,128)(2,1)S(1)} %bitcast.34, bf16[512,448]{1,0:T(8,128)(2,1)S(1)} %bitcast.27), custom_call_target="tpu_custom_call" | custom-call | flops 2000000000 | bytes 8000000 | tf_op jit(solution)/shard_map/pallas_call | solution.py:151
  235.1 31.6 %all_to_all.43.rows_ref = bf16[4,320,896]{2,1,0:T(8,128)(2,1)S(1)} all-to-all(bf16[4,320,896]{2,1,0:T(8,128)(2,1)S(1)} %bitcast.23), channel_id=1, replica_groups=mesh['y'=8,'x'=4,'z'=8,'core'=2] {'x'}, dimensions={0} | all-to-all | bytes 4587520 | tf_op jit(solution)/shard_map/all_to_all | solution.py:183
  266.7 4.3 %shard_map.132 = bf16[512,896]{1,0:T(8,128)(2,1)} custom-call(s32[8]{0:T(128)S(1)} %concatenate.6.info.refs_0_, bf16[2048,512]{1,0:T(8,128)(2,1)S(1)} %bitcast.21, bf16[4,320,896]{2,1,0:T(8,128)(2,1)S(1)} %all_to_all.43.rows_ref), custom_call_target="tpu_custom_call" | custom-call | flops 300000000 | bytes 3500000 | tf_op jit(solution)/shard_map/pallas_call | solution.py:151
  271.1 7.0 %all-to-all-start.5 = ((bf16[8,64,896]{2,1,0:T(8,128)(2,1)}), bf16[8,64,896]{2,1,0:T(8,128)(2,1)}, u32[]{:S(2)}, u32[]{:S(2)}) async-start(bf16[8,64,896]{2,1,0:T(8,128)(2,1)} %bitcast.11), calls=%async_computation.5 | async-start | bytes 1835008 | tf_op jit(solution)/shard_map/all_to_all | solution.py:183
  278.0 1.6 copy-done.3
  279.6 4.9 %shard_map.133 = (bf16[1280,448]{1,0:T(8,128)(2,1)S(1)}, bf16[1280,448]{1,0:T(8,128)(2,1)S(1)}) custom-call(s32[8]{0:T(128)S(1)} %concatenate.6.info.refs_0_, bf16[2048,512]{1,0:T(8,128)(2,1)S(1)} %bitcast.22, bf16[2,4,4,64,512]{4,3,2,1,0:T(8,128)(2,1)S(1)} %bitcast.29), custom_call_target="tpu_custom_call" | custom-call | flops 600000000 | bytes 6500000 | tf_op jit(solution)/shard_map/pallas_call | solution.py:151
  285.6 2.2 copy-done.1
  287.8 1.3 copy-done.6
  289.1 2.5 shard_map.134
  292.5 12.0 %all-to-all-done.5 = bf16[8,64,896]{2,1,0:T(8,128)(2,1)} async-done(((bf16[8,64,896]{2,1,0:T(8,128)(2,1)}), bf16[8,64,896]{2,1,0:T(8,128)(2,1)}, u32[]{:S(2)}, u32[]{:S(2)}) %all-to-all-start.5) | async-done | bytes 917536 | tf_op jit(solution)/shard_map/all_to_all | solution.py:183
  (53 shorter events, 12.5 us)
Async XLA Ops:
  7.2 89.6 %all-gather.4.cloned.1.call-start = ((), (), s32[]{:S(2)}) async-start(), calls=%async_computation.8 | async-start | bytes 2162688 | tf_op jit(solution)/shard_map/all_gather | solution.py:202
  35.0 5.4 %copy-start.13 = (s32[32]{0:T(128)S(1)}, s32[32]{0:T(128)}, u32[]{:S(2)}) copy-start(s32[32]{0:T(128)} %param.14) | copy-start | bytes 388
  35.0 7.3 %copy-start.11 = (bf16[1,512,448]{1,2,0:T(8,128)(2,1)S(1)}, bf16[1,512,448]{1,2,0:T(8,128)(2,1)}, u32[]{:S(2)}) copy-start(bf16[1,512,448]{1,2,0:T(8,128)(2,1)} %param.17) | copy-start | bytes 1376260
  35.0 8.2 %copy-start.12 = (s32[32]{0:T(128)S(1)}, s32[32]{0:T(128)}, u32[]{:S(2)}) copy-start(s32[32]{0:T(128)} %param.13) | copy-start | bytes 388
  35.0 29.5 %all-to-all-start.1 = ((bf16[4,512,512]{2,1,0:T(8,128)(2,1)}), bf16[4,512,512]{2,1,0:T(8,128)(2,1)S(1)}, u32[]{:S(2)}, u32[]{:S(2)}) async-start(bf16[4,512,512]{2,1,0:T(8,128)(2,1)} %broadcast_in_dim.48), calls=%async_computation.1 | async-start | bytes 4194304 | tf_op jit(solution)/shard_map/all_to_all | solution.py:183
  96.8 1.6 copy-start.2
  98.4 12.6 %copy-start.7 = (bf16[1,448,512]{2,1,0:T(8,128)(2,1)S(1)}, bf16[1,448,512]{2,1,0:T(8,128)(2,1)}, u32[]{:S(2)}) copy-start(bf16[1,448,512]{2,1,0:T(8,128)(2,1)} %param.15) | copy-start | bytes 1376260
  98.4 12.6 %copy-start.9 = (bf16[1,448,512]{2,1,0:T(8,128)(2,1)S(1)}, bf16[1,448,512]{2,1,0:T(8,128)(2,1)}, u32[]{:S(2)}) copy-start(bf16[1,448,512]{2,1,0:T(8,128)(2,1)} %param.16) | copy-start | bytes 1376260
  104.6 16.3 %collective-permute-start.1 = (bf16[8,80,512]{2,1,0:T(8,128)(2,1)S(1)}, bf16[8,80,512]{2,1,0:T(8,128)(2,1)S(1)}, u32[]{:S(2)}, u32[]{:S(2)}) collective-permute-start(bf16[8,80,512]{2,1,0:T(8,128)(2,1)S(1)} %get-tuple-element.17), channel_id=1, source_target_pairs={{0,1},{1,0},{2,3},{3,2},{4,5},{5,4},{6,7},{7,6},{8,9},{9,8},{10,11... | collective-permute-start | bytes 1966088 | tf_op jit(solution)/shard_map/ppermute | solution.py:179
  117.9 1.1 copy-start.4
  119.0 10.1 %collective-permute-start = (bf16[8,80,1024]{2,1,0:T(8,128)(2,1)}, bf16[8,80,1024]{2,1,0:T(8,128)(2,1)}, u32[]{:S(2)}, u32[]{:S(2)}) collective-permute-start(bf16[8,80,1024]{2,1,0:T(8,128)(2,1)} %get-tuple-element.15), channel_id=1, source_target_pairs={{0,1},{1,0},{2,3},{3,2},{4,5},{5,4},{6,7},{7,6},{8,9},{9,8},{10,11... | collective-permute-start | bytes 3932168 | tf_op jit(solution)/shard_map/ppermute | solution.py:179
  121.9 27.9 %all-to-all-start.3 = ((bf16[8,80,512]{2,1,0:T(8,128)(2,1)}), bf16[8,80,512]{2,1,0:T(8,128)(2,1)S(1)}, u32[]{:S(2)}, u32[]{:S(2)}) async-start(bf16[8,80,512]{2,1,0:T(8,128)(2,1)} %add_convert_fusion.1), calls=%async_computation.3 | async-start | bytes 1310720 | tf_op jit(solution)/shard_map/all_to_all | solution.py:183
  129.0 97.6 %all-gather.6.cloned.1.call-start = ((), (), s32[]{:S(2)}) async-start(), calls=%async_computation.9 | async-start | bytes 4456448 | tf_op jit(solution)/shard_map/all_gather | solution.py:261
  188.9 37.8 %copy-start.8 = (bf16[1,448,512]{2,1,0:T(8,128)(2,1)S(1)}, bf16[1,448,512]{2,1,0:T(8,128)(2,1)}, u32[]{:S(2)}) copy-start(bf16[1,448,512]{2,1,0:T(8,128)(2,1)} %param.15) | copy-start | bytes 1376260
  188.9 37.8 %copy-start.10 = (bf16[1,448,512]{2,1,0:T(8,128)(2,1)S(1)}, bf16[1,448,512]{2,1,0:T(8,128)(2,1)}, u32[]{:S(2)}) copy-start(bf16[1,448,512]{2,1,0:T(8,128)(2,1)} %param.16) | copy-start | bytes 1376260
  188.9 16.9 %all-to-all-start.6 = ((bf16[32,8,512]{2,1,0:T(8,128)(2,1)}), bf16[32,8,512]{2,1,0:T(8,128)(2,1)}, u32[]{:S(2)}, u32[]{:S(2)}) async-start(bf16[32,8,512]{2,1,0:T(8,128)(2,1)} %bitcast.12), calls=%async_computation.6 | async-start | bytes 524288 | tf_op jit(solution)/shard_map/all_to_all | solution.py:183
  194.6 91.0 %all-gather.8.cloned.1.call-start = ((), (), s32[]{:S(2)}) async-start(), calls=%async_computation.10 | async-start | bytes 4456448 | tf_op jit(solution)/shard_map/all_gather | solution.py:280
  226.6 2.2 copy-start
  271.1 33.5 %all-to-all-start.5 = ((bf16[8,64,896]{2,1,0:T(8,128)(2,1)}), bf16[8,64,896]{2,1,0:T(8,128)(2,1)}, u32[]{:S(2)}, u32[]{:S(2)}) async-start(bf16[8,64,896]{2,1,0:T(8,128)(2,1)} %bitcast.11), calls=%async_computation.5 | async-start | bytes 1835008 | tf_op jit(solution)/shard_map/all_to_all | solution.py:183
  278.0 1.6 copy-start.3
  284.5 1.1 copy-start.5
  285.6 2.2 copy-start.1
  287.8 1.3 copy-start.6
Sparse Core Ops, SparseCore 0:
  11.7 85.0 all-gather.3
  189.0 37.5 all-gather.5
  228.8 44.2 all-gather.7

commit v2 on v1

v2 whole, which is shorter than its diff:
```python
import jax
import jax.numpy as jnp
from jax import lax
from jax.experimental import pallas as pl
from jax.experimental.pallas import tpu as pltpu
from jax.sharding import Mesh, PartitionSpec as P

TOK = 64
CAP = 40
FEAT = 448
WIDE = 512
HID = 512
PAIR = 2 * TOK
HALF = 2 * CAP
CHUNKS = 16
ROWS = CHUNKS * HALF
BUNDLE = 256
BF = jnp.bfloat16
F32 = jnp.float32


def dot(lhs, rhs):
    return jnp.dot(lhs, rhs, preferred_element_type=F32)


def dot_last(lhs, rhs):
    return lax.dot_general(lhs, rhs, (((1,), (1,)), ((), ())), preferred_element_type=F32)


def dot_first(lhs, rhs):
    return lax.dot_general(lhs, rhs, (((0,), (0,)), ((), ())), preferred_element_type=F32)


def as_matrix(hit):
    return jnp.where(hit, 1.0, 0.0).astype(BF)


def weight_rows(tail, experts):
    lane = lax.broadcasted_iota(jnp.int32, (8, 128), 1)
    row = lax.broadcasted_iota(jnp.int32, (8, 128), 0)
    hit = lane < 0
    for i, expert in enumerate(experts):
        hit = hit | ((row == i) & (lane == TOK + expert))
    return dot_last(as_matrix(hit), tail)


def slot_places(weights):
    count = weights.shape[1]
    routed = weights > 0.0
    source = lax.broadcasted_iota(jnp.int32, (count, count), 0)
    target = lax.broadcasted_iota(jnp.int32, (count, count), 1)
    earlier = (source < target) & ((source >> 6) == (target >> 6))
    position = dot(as_matrix(routed), as_matrix(earlier))
    group = lax.broadcasted_iota(jnp.int32, weights.shape, 1) >> 6
    return jnp.where(routed, position.astype(jnp.int32) + CAP * group, -1)


def one_hot(place, rows):
    return lax.broadcasted_iota(jnp.int32, (rows, place.shape[1]), 0) == place


def chunk_hits(tail, expert):
    weights = weight_rows(tail, (expert,))
    return one_hot(slot_places(weights)[0:1], HALF), weights[0:1]


def slot_weights(hit, weights):
    return jnp.sum(jnp.where(hit, weights, 0.0), axis=1, keepdims=True)


def prep_kernel(tok_ref, cot_ref, ids_ref, probs_ref, held_ref, packed_ref, sent_ref):
    names = lax.broadcasted_iota(jnp.int32, (TOK, TOK), 1)
    probs = probs_ref[...].astype(F32)
    ids = ids_ref[...]
    dense = jnp.zeros((TOK, TOK), F32)
    for k in range(8):
        dense = dense + jnp.where(ids[:, k : k + 1] == names, probs[:, k : k + 1], 0.0)
    dense = dense.astype(BF)
    tok = jnp.concatenate([tok_ref[...], dense], axis=1)
    packed_ref[:, :WIDE] = jnp.concatenate([cot_ref[...], dense], axis=1)
    packed_ref[:, WIDE:] = tok
    slab = lax.broadcasted_iota(jnp.int32, (32, TOK), 1) == (held_ref[...] >> 1)
    place = slot_places(dot_last(as_matrix(slab), dense))
    first = lax.broadcasted_iota(jnp.int32, (HALF, TOK), 0) < CAP
    slot = lax.broadcasted_iota(jnp.int32, (HALF, TOK), 0)
    slot = jnp.where(first, slot, slot - CAP)
    for i in range(CHUNKS):
        hit = slot == jnp.where(first, place[2 * i : 2 * i + 1], place[2 * i + 1 : 2 * i + 2])
        sent_ref[i] = dot(as_matrix(hit), tok).astype(BF)


def gate_up(rows_ref, gate_ref, up_ref):
    count = rows_ref.shape[0] * HALF
    rows = rows_ref[...].reshape(count, WIDE)[:, :FEAT]
    return dot(rows, gate_ref[...]), dot(rows, up_ref[...])


def gate_up_send_kernel(info, rows_ref, gate_ref, up_ref, out_ref):
    gate, up = gate_up(rows_ref, gate_ref, up_ref)
    shape = (rows_ref.shape[0], HALF, HID)
    out_ref[:, :, :HID] = gate.astype(BF).reshape(shape)
    out_ref[:, :, HID:] = up.astype(BF).reshape(shape)


def gate_up_keep_kernel(info, rows_ref, gate_ref, up_ref, got_ref, out_ref):
    gate, up = gate_up(rows_ref, gate_ref, up_ref)
    shape = (rows_ref.shape[0], HALF, HID)
    out_ref[:, :, :HID] = (gate.reshape(shape) + got_ref[:, :, :HID].astype(F32)).astype(BF)
    out_ref[:, :, HID:] = (up.reshape(shape) + got_ref[:, :, HID:].astype(F32)).astype(BF)


def hidden_grad(info, cot_ref, down_ref):
    parts = []
    for i in range(cot_ref.shape[0]):
        hit, weights = chunk_hits(cot_ref[i, :, WIDE - 128 :], info[0])
        rows = dot(as_matrix(hit), cot_ref[i, :, :FEAT])
        parts.append((slot_weights(hit, weights) * rows).astype(BF))
    grad = dot_last(jnp.concatenate(parts, axis=0), down_ref[...])
    return grad.reshape(cot_ref.shape[0], HALF, HID)


def hidden_grad_send_kernel(info, cot_ref, down_ref, after_ref, out_ref):
    out_ref[...] = hidden_grad(info, cot_ref, down_ref).astype(BF)


def hidden_grad_keep_kernel(info, cot_ref, down_ref, got_ref, after_ref, out_ref):
    out_ref[...] = (hidden_grad(info, cot_ref, down_ref) + got_ref[...].astype(F32)).astype(BF)


def activation_kernel(gate_up_ref, grad_ref, out_ref):
    both = jnp.sum(gate_up_ref[...].astype(F32), axis=0)
    gate, up = both[:, :HID], both[:, HID:]
    grad = jnp.sum(grad_ref[...].astype(F32), axis=0)
    sig = jax.nn.sigmoid(gate)
    activated = gate * sig
    out_ref[0:HALF] = (activated * up).astype(BF)
    out_ref[HALF : 2 * HALF] = (grad * up * sig * (1.0 + gate * (1.0 - sig))).astype(BF)
    out_ref[2 * HALF : 3 * HALF] = (grad * activated).astype(BF)
    out_ref[3 * HALF :] = jnp.zeros((BUNDLE - 3 * HALF, HID), BF)


def pick_kernel(partner, pieces_ref, out_ref):
    for j in range(32):
        out_ref[j] = pieces_ref[partner[j]]


def bundle_part(acts_ref, part):
    picked = acts_ref[:, part * HALF : (part + 1) * HALF, :]
    return picked.reshape(picked.shape[0] * HALF, HID)


def terms_kernel(info, tail_ref, acts_ref, gate_ref, up_ref, down_ref, out_ref):
    lane = lax.broadcasted_iota(jnp.int32, tail_ref.shape, 1)
    factor = jnp.sum(jnp.where(lane == TOK + info[0], tail_ref[...].astype(F32), 0.0), axis=1, keepdims=True)
    out = dot(bundle_part(acts_ref, 0), down_ref[...]) * factor
    back = dot_last(bundle_part(acts_ref, 1), gate_ref[...]) + dot_last(bundle_part(acts_ref, 2), up_ref[...])
    both = jnp.concatenate([out, back], axis=1)
    for y in range(out_ref.shape[1]):
        for x in range(4):
            at = (4 * y + x) * CAP
            out_ref[x, y] = both[at : at + CAP].astype(BF)


def merge_kernel(info, tail_ref, rows_ref, out_ref):
    weights = weight_rows(tail_ref[...].reshape(PAIR, 128), tuple(info[4 + i] for i in range(4)))
    place = slot_places(weights)
    total = jnp.zeros(out_ref.shape, F32)
    for i in range(4):
        total = total + dot_first(as_matrix(one_hot(place[i : i + 1], HALF)), rows_ref[i])
    out_ref[...] = total.astype(BF)


def new_rows_kernel(info, packed_ref, rows_ref, scaled_ref):
    for i in range(packed_ref.shape[0]):
        hit, weights = chunk_hits(packed_ref[i, :, WIDE - 128 : WIDE], info[2])
        pick = as_matrix(hit)
        rows_ref[i] = dot(pick, packed_ref[i, :, WIDE : WIDE + FEAT]).astype(BF)
        scaled_ref[i] = (slot_weights(hit, weights) * dot(pick, packed_ref[i, :, :FEAT])).astype(BF)


def slab_grad_kernel(rows_ref, scaled_ref, acts_ref, gate_ref, up_ref, down_ref):
    gate_ref[...] = dot_first(rows_ref[...], bundle_part(acts_ref, 1)).astype(BF)
    up_ref[...] = dot_first(rows_ref[...], bundle_part(acts_ref, 2)).astype(BF)
    down_ref[...] = dot_first(bundle_part(acts_ref, 0), scaled_ref[...]).astype(BF)


def shaped(*shape):
    return jax.ShapeDtypeStruct(shape, BF)


def params():
    return pltpu.CompilerParams(vmem_limit_bytes=32 * 1024 * 1024)


def cost(mflop, kbytes):
    return pl.CostEstimate(flops=mflop * 1_000_000, bytes_accessed=kbytes * 1000, transcendentals=0)


def call(kernel, grid, in_specs, out_specs, out_shape, estimate, info, *operands):
    return pl.pallas_call(
        kernel,
        grid_spec=pltpu.PrefetchScalarGridSpec(
            num_scalar_prefetch=1, grid=grid, in_specs=in_specs, out_specs=out_specs
        ),
        out_shape=out_shape,
        compiler_params=params(),
        cost_estimate=estimate,
    )(info, *operands)


def local(kernel, out_shape, estimate, *operands):
    return pl.pallas_call(kernel, out_shape=out_shape, compiler_params=params(), cost_estimate=estimate)(*operands)


def whole(*shape):
    return pl.BlockSpec(shape, lambda i, info: (0,) * len(shape))


def lead_block(*shape):
    return pl.BlockSpec(shape, lambda i, info: (i,) + (0,) * (len(shape) - 1))


def core_half(count, rows, lanes, mine):
    if mine:
        return pl.BlockSpec((count, None, rows, lanes), lambda i, info: (i, info[1], 0, 0))
    return pl.BlockSpec((count, None, rows, lanes), lambda i, info: (i, 1 - info[1], 0, 0))


ANYWHERE = pl.BlockSpec(memory_space=pl.ANY)


def swap(value):
    return lax.ppermute(value, "core", [(0, 1), (1, 0)])


def exchange(value, axes):
    return lax.all_to_all(value, axes, split_axis=0, concat_axis=0, tiled=True)


def body(tokens, cotangent, expert_ids, route_probs, held_before, partner, gate_slabs, up_slabs, down_slabs):
    gate, up, down = gate_slabs[0], up_slabs[0], down_slabs[0]
    here_y, here_x, core = lax.axis_index("y"), lax.axis_index("x"), lax.axis_index("core")
    here = here_y * 4 + here_x
    experts = held_before // 2
    new_expert = experts[partner[here]]
    row_experts = lax.dynamic_slice(experts, (here_y * 4,), (4,))
    info = jnp.concatenate(
        [jnp.stack([experts[here], core, new_expert, here_x]).astype(jnp.int32), row_experts.astype(jnp.int32)]
    )

    packed, sent = local(
        prep_kernel,
        (shaped(TOK, 2 * WIDE), shaped(CHUNKS, HALF, WIDE)),
        cost(90, 1600),
        tokens,
        cotangent,
        expert_ids,
        route_probs,
        held_before.reshape(32, 1),
    )
    everyone = lax.all_gather(packed, ("y", "x"), tiled=True)
    own_rows = exchange(sent.reshape(32, CAP, WIDE), ("y", "x"))

    rows_view = own_rows.reshape(8, 2, HALF, WIDE)
    weight_specs = [whole(FEAT, HID), whole(FEAT, HID)]
    wide_out = lead_block(4, HALF, 2 * HID)
    sending = call(
        gate_up_send_kernel,
        (2,),
        [core_half(4, HALF, WIDE, False)] + weight_specs,
        wide_out,
        shaped(8, HALF, 2 * HID),
        cost(600, 2900),
        info,
        rows_view,
        gate,
        up,
    )
    pair_gate_up = call(
        gate_up_keep_kernel,
        (2,),
        [core_half(4, HALF, WIDE, True)] + weight_specs + [wide_out],
        wide_out,
        shaped(8, HALF, 2 * HID),
        cost(600, 4200),
        info,
        rows_view,
        gate,
        up,
        swap(sending),
    )
    sums_gate_up = exchange(pair_gate_up, "z")

    cot_view = everyone.reshape(8, 2, PAIR, 2 * WIDE)
    thin_out = lead_block(4, HALF, HID)
    sending = call(
        hidden_grad_send_kernel,
        (2,),
        [core_half(4, PAIR, WIDE, False), whole(HID, FEAT), ANYWHERE],
        thin_out,
        shaped(8, HALF, HID),
        cost(400, 2200),
        info,
        cot_view,
        down,
        pair_gate_up,
    )
    pair_grad = call(
        hidden_grad_keep_kernel,
        (2,),
        [core_half(4, PAIR, WIDE, True), whole(HID, FEAT), thin_out, ANYWHERE],
        thin_out,
        shaped(8, HALF, HID),
        cost(400, 2900),
        info,
        cot_view,
        down,
        swap(sending),
        sums_gate_up,
    )
    sums_grad = exchange(pair_grad, "z")

    acts = local(activation_kernel, shaped(BUNDLE, HID), cost(3, 2300), sums_gate_up, sums_grad)

    own_acts = lax.all_gather(acts, ("z", "core"), tiled=True).reshape(CHUNKS, BUNDLE, HID)
    pieces = exchange(acts.reshape(32, 8, HID), ("y", "x"))
    picked = pl.pallas_call(
        pick_kernel,
        grid_spec=pltpu.PrefetchScalarGridSpec(
            num_scalar_prefetch=1,
            grid=(1,),
            in_specs=[whole(32, 8, HID)],
            out_specs=whole(32, 8, HID),
        ),
        out_shape=shaped(32, 8, HID),
        compiler_params=params(),
        cost_estimate=cost(1, 520),
    )(partner, pieces)
    moved = exchange(picked, ("y", "x")).reshape(BUNDLE, HID)

    terms = call(
        terms_kernel,
        (4,),
        [
            pl.BlockSpec((4 * HALF, 128), lambda i, info: (i, 3)),
            lead_block(4, BUNDLE, HID),
            whole(FEAT, HID),
            whole(FEAT, HID),
            whole(HID, FEAT),
        ],
        pl.BlockSpec((4, 2, CAP, 2 * FEAT), lambda i, info: (0, i, 0, 0)),
        shaped(4, 8, CAP, 2 * FEAT),
        cost(1800, 8000),
        info,
        own_rows.reshape(ROWS, WIDE),
        own_acts,
        gate,
        up,
        down,
    )
    new_acts = lax.all_gather(moved, ("z", "core"), tiled=True).reshape(CHUNKS, BUNDLE, HID)

    returned = exchange(terms.reshape(4, 8 * CAP, 2 * FEAT), "x")
    merged = call(
        merge_kernel,
        (4,),
        [
            pl.BlockSpec((2, None, TOK, 128), lambda i, info: (i, info[3], 0, 3)),
            pl.BlockSpec((4, HALF, 2 * FEAT), lambda i, info: (0, i, 0)),
        ],
        lead_block(PAIR, 2 * FEAT),
        shaped(8 * TOK, 2 * FEAT),
        cost(300, 3500),
        info,
        everyone.reshape(8, 4, TOK, 2 * WIDE),
        returned,
    )
    home = exchange(merged.reshape(8, TOK, 2 * FEAT), "y")

    rows, scaled = call(
        new_rows_kernel,
        (4,),
        [lead_block(4, PAIR, 2 * WIDE)],
        (lead_block(4, HALF, FEAT), lead_block(4, HALF, FEAT)),
        (shaped(CHUNKS, HALF, FEAT), shaped(CHUNKS, HALF, FEAT)),
        cost(600, 6500),
        info,
        everyone.reshape(CHUNKS, PAIR, 2 * WIDE),
    )
    gate_grad, up_grad, down_grad = local(
        slab_grad_kernel,
        (shaped(FEAT, HID), shaped(FEAT, HID), shaped(HID, FEAT)),
        cost(1800, 8000),
        rows.reshape(ROWS, FEAT),
        scaled.reshape(ROWS, FEAT),
        new_acts,
    )

    total = jnp.sum(home.astype(F32), axis=0).astype(BF)
    return (total[:, :FEAT], total[:, FEAT:], gate_grad[None], up_grad[None], down_grad[None])


def solution(mesh):
    fine = Mesh(mesh.devices.reshape(8, 4, 8, 2), ("y", "x", "z", "core"))
    expert, dp = ("y", "x"), ("z", "core")
    slab = P(expert, dp, None)
    down = P(expert, None, dp)
    return jax.shard_map(
        body,
        mesh=fine,
        in_specs=(P(expert, dp), P(expert, dp), P(expert, None), P(expert, None), P(), P(), slab, slab, down),
        out_specs=(P(expert, dp), P(expert, dp), slab, slab, down),
        check_vma=False,
    )
```

time: 314 us -> 280 us (0.89)
  blocking collectives: 107 us -> 88.6 us
  waiting for transfers between devices: 94.6 us -> 80.2 us
  other arithmetic: 9.1 us -> 1.32 us
  starting transfers between devices: 33.5 us -> 38.4 us
    all_to_all x4, blocking collectives: 107 us -> 88.6 us  [exchange(): return lax.all_to_all(value, axes, split_axis=0, concat_axis=0, tiled=True)]
    all_to_all x4 -> x3, waiting for transfers between devices: 59.7 us -> 43.5 us  [exchange(): return lax.all_to_all(value, axes, split_axis=0, concat_axis=0, tiled=True)]
    convert_element_type x3 -> x0, other arithmetic: 5.09 us -> none  [the longest x2 4.4 us: dp_scatter_sum(): pair = (keep.astype(F32) + swap(send).astype(F32)).astype(BF)]
    ppermute x2, waiting for transfers between devices: 0.01 us -> 4.67 us  [swap(): return lax.ppermute(value, 'core', [(0, 1), (1, 0)])]
    unnamed x30 -> x32, local copies, waits for them, and re-layouts: 12.2 us -> 16.4 us
    all_to_all x4 -> x3, starting transfers between devices: 25.1 us -> 28.4 us  [exchange(): return lax.all_to_all(value, axes, split_axis=0, concat_axis=0, tiled=True)]
    pallas_call x5 -> x7, Pallas kernels: 28.6 us -> 27.3 us  [call(): pl.pallas_call(kernel, grid_spec=pltpu.PrefetchScalarGridSpec(num_scalar_...]
  transfers between devices with their start and end apart: 9 -> 8, of which waited for: 6 -> 6; matrix products, arithmetic and copies ran while one was open for 5% -> 2% of each run, Pallas kernels for 8% -> 9%
where the time goes in v2:
time: 280 us; the launch traced here: 279 us
  blocking collectives  88.6 us (32%)
  waiting for transfers between devices  80.2 us (29%)
  starting transfers between devices  38.4 us (14%)
  Pallas kernels  33.5 us (12%)
  local copies, waits for them, and re-layouts  20.5 us (7%)
  between operations  15.9 us (6%)
    all_to_all x4, blocking collectives, exchange(): return lax.all_to_all(value, axes, split_axis=0, concat_axis=0, tiled=True)  88.6 us
    all_to_all x3, waiting for transfers between devices, exchange(): return lax.all_to_all(value, axes, split_axis=0, concat_axis=0, tiled=True)  43.5 us
    all_to_all x3, starting transfers between devices, exchange(): return lax.all_to_all(value, axes, split_axis=0, concat_axis=0, tiled=True)  28.4 us
    pallas_call x7, Pallas kernels, call(): pl.pallas_call(kernel, grid_spec=pltpu.PrefetchScalarGridSpec(num_scalar_...  27.3 us
    all_gather x1, waiting for transfers between devices, body(): everyone = lax.all_gather(packed, ('y', 'x'), tiled=True)  23.6 us
    unnamed x32, local copies, waits for them, and re-layouts  16.4 us
    ppermute x2, starting transfers between devices, swap(): return lax.ppermute(value, 'core', [(0, 1), (1, 0)])  9.89 us
    all_gather x1, waiting for transfers between devices, body(): lax.all_gather(acts, ('z', 'core'), tiled=True).reshape(CHUNKS, BUNDLE, HID)  8.36 us
  transfers between devices with their start and end apart: 8, of which 6 were waited for; matrix products, arithmetic and copies ran while one was open for 2% of the time, Pallas kernels for 9%

profile of v2, /device:TPU:1, one launch (start us, length us, event | category | flops | bytes accessed | tf_op | source)
XLA Modules:
  0.0 278.5 jit_solution(4163215262713513059)
XLA Ops:
  11.2 2.1 shard_map.128
  13.3 10.6 %all-to-all-start = ((bf16[32,40,512]{2,1,0:T(8,128)(2,1)}), bf16[32,40,512]{2,1,0:T(8,128)(2,1)S(1)}, u32[]{:S(2)}, u32[]{:S(2)}) async-start(bf16[32,40,512]{2,1,0:T(8,128)(2,1)} %bitcast.5), calls=%async_computation | async-start | bytes 2621440 | tf_op jit(solution)/shard_map/all_to_all | solution.py:237
  27.2 1.4 concatenate.3.info
  28.6 30.9 %all-to-all-done = bf16[32,40,512]{2,1,0:T(8,128)(2,1)S(1)} async-done(((bf16[32,40,512]{2,1,0:T(8,128)(2,1)}), bf16[32,40,512]{2,1,0:T(8,128)(2,1)S(1)}, u32[]{:S(2)}, u32[]{:S(2)}) %all-to-all-start) | async-done | bytes 1310752 | tf_op jit(solution)/shard_map/all_to_all | solution.py:237
  59.5 1.6 shard_map.129
  61.2 4.7 %collective-permute-start = (bf16[8,80,1024]{2,1,0:T(8,128)(2,1)S(1)}, bf16[8,80,1024]{2,1,0:T(8,128)(2,1)S(1)}, u32[]{:S(2)}, u32[]{:S(2)}) collective-permute-start(bf16[8,80,1024]{2,1,0:T(8,128)(2,1)S(1)} %shard_map.129), channel_id=1, source_target_pairs={{0,1},{1,0},{2,3},{3,2},{4,5},{5,4},{6,7},{7,6},{8,9},{9,8},{10,11... | collective-permute-start | bytes 3932168 | tf_op jit(solution)/shard_map/ppermute | solution.py:233
  65.9 2.6 collective-permute-done.got_ref
  68.6 2.5 shard_map.130.after_ref
  71.1 11.4 %all-to-all-start.1 = ((bf16[8,80,1024]{2,1,0:T(8,128)(2,1)}), bf16[8,80,1024]{2,1,0:T(8,128)(2,1)S(1)}, u32[]{:S(2)}, u32[]{:S(2)}) async-start(bf16[8,80,1024]{2,1,0:T(8,128)(2,1)} %shard_map.130.after_ref), calls=%async_computation.1 | async-start | bytes 2621440 | tf_op jit(solution)/shard_map/all_to_all | solution.py:237
  82.5 1.2 copy.17
  83.7 23.6 %all-gather.4.cloned.1.call-done = bf16[2048,1024]{1,0:T(8,128)(2,1)} async-done(((bf16[64,1024]{1,0:T(8,128)(2,1)}), bf16[2048,1024]{1,0:T(8,128)(2,1)}) %all-gather.4.cloned.1.call-update) | async-done | bytes 4194320 | tf_op jit(solution)/shard_map/all_gather | solution.py:261
  107.3 2.2 copy-done
  109.5 4.3 %shard_map.131 = bf16[8,80,512]{2,1,0:T(8,128)(2,1)} custom-call(s32[8]{0:T(128)S(1)} %concatenate.3.info, bf16[8,2,128,1024]{3,2,1,0:T(8,128)(2,1)S(1)} %bitcast.24, bf16[512,448]{1,0:T(8,128)(2,1)S(1)} %bitcast.32, bf16[8,80,1024]{2,1,0:T(8,128)(2,1)} %shard_map.130.after_ref), custom_call_target="tpu_custom_call" | custom-call | flops 400000000 | bytes 2200000 | tf_op jit(solution)/shard_map/pallas_call | solution.py:200
  113.9 5.1 %collective-permute-start.1 = (bf16[8,80,512]{2,1,0:T(8,128)(2,1)}, bf16[8,80,512]{2,1,0:T(8,128)(2,1)}, u32[]{:S(2)}, u32[]{:S(2)}) collective-permute-start(bf16[8,80,512]{2,1,0:T(8,128)(2,1)} %shard_map.131), channel_id=1, source_target_pairs={{0,1},{1,0},{2,3},{3,2},{4,5},{5,4},{6,7},{7,6},{8,9},{9,8},{10,11... | collective-permute-start | bytes 1966088 | tf_op jit(solution)/shard_map/ppermute | solution.py:233
  119.0 2.0 collective-permute-done.1.got_ref
  121.1 2.2 copy-done.1
  123.3 4.6 %shard_map.132 = bf16[8,80,512]{2,1,0:T(8,128)(2,1)S(1)} custom-call(s32[8]{0:T(128)S(1)} %concatenate.3.info, bf16[8,2,128,1024]{3,2,1,0:T(8,128)(2,1)S(1)} %bitcast.25, bf16[512,448]{1,0:T(8,128)(2,1)S(1)} %bitcast.33, bf16[8,80,512]{2,1,0:T(8,128)(2,1)} %collective-permute-done.1.got_ref, bf16[8,80,1024]{2,1,0:T(8,128)(2,1)S(1)} %all-to-all-done.1.after_ref.gate_up_ref), custom_call_target="tpu_custom_call" | custom-call | flops 400000000 | bytes 2900000 | tf_op jit(solution)/shard_map/pallas_call | solution.py:200
  127.8 26.4 %all_to_all.35.grad_ref = bf16[8,80,512]{2,1,0:T(8,128)(2,1)S(1)} all-to-all(bf16[8,80,512]{2,1,0:T(8,128)(2,1)S(1)} %shard_map.132), channel_id=1, replica_groups=mesh['y'=8,'x'=4,'z'=8,'core'=2] {'z'}, dimensions={0} | all-to-all | bytes 1310720 | tf_op jit(solution)/shard_map/all_to_all | solution.py:237
  155.4 16.0 %all_to_all.36.pieces_ref = bf16[32,8,512]{2,1,0:T(8,128)(2,1)S(1)} all-to-all(bf16[32,8,512]{2,1,0:T(8,128)(2,1)} %bitcast.18), channel_id=1, replica_groups=mesh['y'=8,'x'=4,'z'=8,'core'=2] {'y','x'}, dimensions={0} | all-to-all | bytes 524288 | tf_op jit(solution)/shard_map/all_to_all | solution.py:237
  172.0 14.3 %all_to_all.37 = bf16[32,8,512]{2,1,0:T(8,128)(2,1)} all-to-all(bf16[32,8,512]{2,1,0:T(8,128)(2,1)S(1)} %shard_map.137), channel_id=1, replica_groups=mesh['y'=8,'x'=4,'z'=8,'core'=2] {'y','x'}, dimensions={0} | all-to-all | bytes 524288 | tf_op jit(solution)/shard_map/all_to_all | solution.py:237
  186.3 8.4 %all-gather.6.cloned.1.call-done = bf16[4096,512]{1,0:T(8,128)(2,1)} async-done(((bf16[256,512]{1,0:T(8,128)(2,1)}), bf16[4096,512]{1,0:T(8,128)(2,1)}) %all-gather.6.cloned.1.call-update) | async-done | bytes 4194320 | tf_op jit(solution)/shard_map/all_gather | solution.py:325
  194.7 2.2 copy-done.4
  196.8 3.8 %shard_map.134 = bf16[4,8,40,896]{3,2,1,0:T(8,128)(2,1)S(1)} custom-call(s32[8]{0:T(128)S(1)} %concatenate.3.info, bf16[1280,512]{1,0:T(8,128)(2,1)S(1)} %bitcast.30, bf16[16,256,512]{2,1,0:T(8,128)(2,1)S(1)} %bitcast.35, bf16[448,512]{1,0:T(8,128)(2,1)S(1)} %bitcast.39, bf16[448,512]{1,0:T(8,128)(2,1)S(1)} %bitcast.42, bf16[512,448]{1,0:T(8,128)(2,1)S(1)} %bitcast.34), custom_call_target="tpu_custom_call" | custom-call | flops 1800000000 | bytes 8000000 | tf_op jit(solution)/shard_map/pallas_call | solution.py:200
  200.7 31.9 %all_to_all.38.rows_ref = bf16[4,320,896]{2,1,0:T(8,128)(2,1)S(1)} all-to-all(bf16[4,320,896]{2,1,0:T(8,128)(2,1)S(1)} %bitcast.31), channel_id=1, replica_groups=mesh['y'=8,'x'=4,'z'=8,'core'=2] {'x'}, dimensions={0} | all-to-all | bytes 4587520 | tf_op jit(solution)/shard_map/all_to_all | solution.py:237
  232.6 4.4 %shard_map.135 = bf16[512,896]{1,0:T(8,128)(2,1)} custom-call(s32[8]{0:T(128)S(1)} %concatenate.3.info, bf16[8,4,64,1024]{3,2,1,0:T(8,128)(2,1)S(1)} %bitcast.26, bf16[4,320,896]{2,1,0:T(8,128)(2,1)S(1)} %all_to_all.38.rows_ref), custom_call_target="tpu_custom_call" | custom-call | flops 300000000 | bytes 3500000 | tf_op jit(solution)/shard_map/pallas_call | solution.py:200
  237.0 6.5 %all-to-all-start.4 = ((bf16[8,64,896]{2,1,0:T(8,128)(2,1)}), bf16[8,64,896]{2,1,0:T(8,128)(2,1)}, u32[]{:S(2)}, u32[]{:S(2)}) async-start(bf16[8,64,896]{2,1,0:T(8,128)(2,1)} %bitcast.14), calls=%async_computation.4 | async-start | bytes 1835008 | tf_op jit(solution)/shard_map/all_to_all | solution.py:237
  243.5 2.2 copy-done.3
  245.6 6.0 %shard_map.136 = (bf16[16,80,448]{2,1,0:T(8,128)(2,1)S(1)}, bf16[16,80,448]{2,1,0:T(8,128)(2,1)S(1)}) custom-call(s32[8]{0:T(128)S(1)} %concatenate.3.info, bf16[16,128,1024]{2,1,0:T(8,128)(2,1)S(1)} %bitcast.27), custom_call_target="tpu_custom_call" | custom-call | flops 600000000 | bytes 6500000 | tf_op jit(solution)/shard_map/pallas_call | solution.py:200
  251.7 2.2 copy-done.5
  253.9 2.5 shard_map.138
  257.3 12.6 %all-to-all-done.4 = bf16[8,64,896]{2,1,0:T(8,128)(2,1)} async-done(((bf16[8,64,896]{2,1,0:T(8,128)(2,1)}), bf16[8,64,896]{2,1,0:T(8,128)(2,1)}, u32[]{:S(2)}, u32[]{:S(2)}) %all-to-all-start.4) | async-done | bytes 917536 | tf_op jit(solution)/shard_map/all_to_all | solution.py:237
  269.9 1.3 reduce_sum.12
  (42 shorter events, 8.8 us)
Async XLA Ops:
  7.2 100.2 %all-gather.4.cloned.1.call-start = ((), (), s32[]{:S(2)}) async-start(), calls=%async_computation.7 | async-start | bytes 4325376 | tf_op jit(solution)/shard_map/all_gather | solution.py:261
  9.5 0.8 copy-start.11
  10.3 0.8 copy-start.12
  13.3 10.7 %copy-start.10 = (s32[32]{0:T(128)S(1)}, s32[32]{0:T(128)}, u32[]{:S(2)}) copy-start(s32[32]{0:T(128)} %partner.1) | copy-start | bytes 388
  13.3 13.2 %copy-start.13 = (s32[32]{0:T(128)S(1)}, s32[32]{0:T(128)}, u32[]{:S(2)}) copy-start(s32[32]{0:T(128)} %param.13) | copy-start | bytes 388
  13.3 46.2 %copy-start.6 = (bf16[1,448,512]{2,1,0:T(8,128)(2,1)S(1)}, bf16[1,448,512]{2,1,0:T(8,128)(2,1)}, u32[]{:S(2)}) copy-start(bf16[1,448,512]{2,1,0:T(8,128)(2,1)} %param.15) | copy-start | bytes 1376260
  13.3 46.2 %copy-start.8 = (bf16[1,448,512]{2,1,0:T(8,128)(2,1)S(1)}, bf16[1,448,512]{2,1,0:T(8,128)(2,1)}, u32[]{:S(2)}) copy-start(bf16[1,448,512]{2,1,0:T(8,128)(2,1)} %param.16) | copy-start | bytes 1376260
  13.3 46.2 %all-to-all-start = ((bf16[32,40,512]{2,1,0:T(8,128)(2,1)}), bf16[32,40,512]{2,1,0:T(8,128)(2,1)S(1)}, u32[]{:S(2)}, u32[]{:S(2)}) async-start(bf16[32,40,512]{2,1,0:T(8,128)(2,1)} %bitcast.5), calls=%async_computation | async-start | bytes 2621440 | tf_op jit(solution)/shard_map/all_to_all | solution.py:237
  61.2 7.4 %collective-permute-start = (bf16[8,80,1024]{2,1,0:T(8,128)(2,1)S(1)}, bf16[8,80,1024]{2,1,0:T(8,128)(2,1)S(1)}, u32[]{:S(2)}, u32[]{:S(2)}) collective-permute-start(bf16[8,80,1024]{2,1,0:T(8,128)(2,1)S(1)} %shard_map.129), channel_id=1, source_target_pairs={{0,1},{1,0},{2,3},{3,2},{4,5},{5,4},{6,7},{7,6},{8,9},{9,8},{10,11... | collective-permute-start | bytes 3932168 | tf_op jit(solution)/shard_map/ppermute | solution.py:233
  71.1 47.9 %all-to-all-start.1 = ((bf16[8,80,1024]{2,1,0:T(8,128)(2,1)}), bf16[8,80,1024]{2,1,0:T(8,128)(2,1)S(1)}, u32[]{:S(2)}, u32[]{:S(2)}) async-start(bf16[8,80,1024]{2,1,0:T(8,128)(2,1)} %shard_map.130.after_ref), calls=%async_computation.1 | async-start | bytes 2621440 | tf_op jit(solution)/shard_map/all_to_all | solution.py:237
  82.5 112.2 %all-gather.6.cloned.1.call-start = ((), (), s32[]{:S(2)}) async-start(), calls=%async_computation.8 | async-start | bytes 4456448 | tf_op jit(solution)/shard_map/all_gather | solution.py:325
  107.3 2.2 copy-start
  113.9 7.2 %collective-permute-start.1 = (bf16[8,80,512]{2,1,0:T(8,128)(2,1)}, bf16[8,80,512]{2,1,0:T(8,128)(2,1)}, u32[]{:S(2)}, u32[]{:S(2)}) collective-permute-start(bf16[8,80,512]{2,1,0:T(8,128)(2,1)} %shard_map.131), channel_id=1, source_target_pairs={{0,1},{1,0},{2,3},{3,2},{4,5},{5,4},{6,7},{7,6},{8,9},{9,8},{10,11... | collective-permute-start | bytes 1966088 | tf_op jit(solution)/shard_map/ppermute | solution.py:233
  121.1 2.2 copy-start.1
  155.3 39.3 %copy-start.7 = (bf16[1,448,512]{2,1,0:T(8,128)(2,1)S(1)}, bf16[1,448,512]{2,1,0:T(8,128)(2,1)}, u32[]{:S(2)}) copy-start(bf16[1,448,512]{2,1,0:T(8,128)(2,1)} %param.15) | copy-start | bytes 1376260
  155.3 39.3 %copy-start.9 = (bf16[1,448,512]{2,1,0:T(8,128)(2,1)S(1)}, bf16[1,448,512]{2,1,0:T(8,128)(2,1)}, u32[]{:S(2)}) copy-start(bf16[1,448,512]{2,1,0:T(8,128)(2,1)} %param.16) | copy-start | bytes 1376260
  155.4 96.4 %all-gather.8.cloned.1.call-start = ((), (), s32[]{:S(2)}) async-start(), calls=%async_computation.9 | async-start | bytes 4456448 | tf_op jit(solution)/shard_map/all_gather | solution.py:361
  194.7 2.2 copy-start.4
  200.7 31.9 %copy-start.2 = (bf16[2048,1024]{1,0:T(8,128)(2,1)S(1)}, bf16[2048,1024]{1,0:T(8,128)(2,1)}, u32[]{:S(2)}) copy-start(bf16[2048,1024]{1,0:T(8,128)(2,1)} %all-gather.4.cloned.1.call-done) | copy-start | bytes 12582916
  237.0 32.9 %all-to-all-start.4 = ((bf16[8,64,896]{2,1,0:T(8,128)(2,1)}), bf16[8,64,896]{2,1,0:T(8,128)(2,1)}, u32[]{:S(2)}, u32[]{:S(2)}) async-start(bf16[8,64,896]{2,1,0:T(8,128)(2,1)} %bitcast.14), calls=%async_computation.4 | async-start | bytes 1835008 | tf_op jit(solution)/shard_map/all_to_all | solution.py:237
  243.5 2.2 copy-start.3
  251.7 2.2 copy-start.5
Sparse Core Ops, SparseCore 0:
  13.4 93.8 all-gather.3
  155.5 39.1 all-gather.5
  196.8 43.7 all-gather.7

commit v3 on v2

v3 whole, which is shorter than its diff:
```python
import jax
import jax.numpy as jnp
from jax import lax
from jax.experimental import pallas as pl
from jax.experimental.pallas import tpu as pltpu
from jax.sharding import Mesh, PartitionSpec as P

TOK = 64
CAP = 40
FEAT = 448
WIDE = 512
HID = 512
PAIR = 2 * TOK
HALF = 2 * CAP
CHUNKS = 16
ROWS = CHUNKS * HALF
BUNDLE = 256
BF = jnp.bfloat16
F32 = jnp.float32


def dot(lhs, rhs):
    return jnp.dot(lhs, rhs, preferred_element_type=F32)


def dot_last(lhs, rhs):
    return lax.dot_general(lhs, rhs, (((1,), (1,)), ((), ())), preferred_element_type=F32)


def dot_first(lhs, rhs):
    return lax.dot_general(lhs, rhs, (((0,), (0,)), ((), ())), preferred_element_type=F32)


def as_matrix(hit):
    return jnp.where(hit, 1.0, 0.0).astype(BF)


def weight_rows(tail, experts):
    lane = lax.broadcasted_iota(jnp.int32, (8, 128), 1)
    row = lax.broadcasted_iota(jnp.int32, (8, 128), 0)
    hit = lane < 0
    for i, expert in enumerate(experts):
        hit = hit | ((row == i) & (lane == TOK + expert))
    return dot_last(as_matrix(hit), tail)


def slot_places(weights):
    count = weights.shape[1]
    routed = weights > 0.0
    source = lax.broadcasted_iota(jnp.int32, (count, count), 0)
    target = lax.broadcasted_iota(jnp.int32, (count, count), 1)
    earlier = (source < target) & ((source >> 6) == (target >> 6))
    position = dot(as_matrix(routed), as_matrix(earlier))
    group = lax.broadcasted_iota(jnp.int32, weights.shape, 1) >> 6
    return jnp.where(routed, position.astype(jnp.int32) + CAP * group, -1)


def one_hot(place, rows):
    return lax.broadcasted_iota(jnp.int32, (rows, place.shape[1]), 0) == place


def chunk_hits(tail, expert):
    weights = weight_rows(tail, (expert,))
    return one_hot(slot_places(weights)[0:1], HALF), weights[0:1]


def slot_weights(hit, weights):
    return jnp.sum(jnp.where(hit, weights, 0.0), axis=1, keepdims=True)


def prep_kernel(held, tok_ref, cot_ref, ids_ref, probs_ref, packed_ref, sent_ref):
    def weights_of(names):
        return sum(jnp.where(ids_ref[k : k + 1] == names, probs_ref[k : k + 1].astype(F32), 0.0) for k in range(8))

    names = lax.broadcasted_iota(jnp.int32, (TOK, TOK), 0)
    same = names == lax.broadcasted_iota(jnp.int32, (TOK, TOK), 1)
    dense = dot_first(weights_of(names).astype(BF), as_matrix(same)).astype(BF)
    tok, cot = tok_ref[...], cot_ref[...]
    packed_ref[:, :WIDE] = jnp.concatenate([cot, dense], axis=1)
    packed_ref[:, WIDE:] = jnp.concatenate([tok, dense], axis=1)

    slab = lax.broadcasted_iota(jnp.int32, (32, TOK), 0)
    expert = jnp.zeros((32, TOK), jnp.int32)
    for i in range(32):
        expert = jnp.where(slab == i, held[i] >> 1, expert)
    weights = weights_of(expert)
    place = slot_places(weights)
    first = lax.broadcasted_iota(jnp.int32, (HALF, TOK), 0) < CAP
    slot = lax.broadcasted_iota(jnp.int32, (HALF, TOK), 0)
    slot = jnp.where(first, slot, slot - CAP)
    for i in range(CHUNKS):
        one, two = slice(2 * i, 2 * i + 1), slice(2 * i + 1, 2 * i + 2)
        hit = slot == jnp.where(first, place[one], place[two])
        factor = slot_weights(hit, jnp.where(first, weights[one], weights[two]))
        pick = as_matrix(hit)
        rows = dot(pick, tok)
        scaled = factor * dot(pick, cot)
        sent_ref[i] = jnp.concatenate([rows, scaled], axis=1).astype(BF)


def products(rows_ref, gate_ref, up_ref, down_ref):
    count = rows_ref.shape[0]
    rows = rows_ref[...].reshape(count * HALF, 2 * FEAT)
    tok, scaled = rows[:, :FEAT], rows[:, FEAT:]
    three = dot(tok, gate_ref[...]), dot(tok, up_ref[...]), dot(scaled, down_ref[...])
    return [(slice(i * HID, (i + 1) * HID), part.reshape(count, HALF, HID)) for i, part in enumerate(three)]


def send_kernel(coords, rows_ref, gate_ref, up_ref, down_ref, out_ref):
    for lanes, part in products(rows_ref, gate_ref, up_ref, down_ref):
        out_ref[:, :, lanes] = part.astype(BF)


def keep_kernel(coords, rows_ref, gate_ref, up_ref, down_ref, got_ref, out_ref):
    for lanes, part in products(rows_ref, gate_ref, up_ref, down_ref):
        out_ref[:, :, lanes] = (part + got_ref[:, :, lanes].astype(F32)).astype(BF)


def activation_kernel(sums_ref, out_ref):
    sums = jnp.sum(sums_ref[...].astype(F32), axis=0)
    gate, up, grad = sums[:, :HID], sums[:, HID : 2 * HID], sums[:, 2 * HID :]
    sig = jax.nn.sigmoid(gate)
    activated = gate * sig
    out_ref[0:HALF] = (activated * up).astype(BF)
    out_ref[HALF : 2 * HALF] = (grad * up * sig * (1.0 + gate * (1.0 - sig))).astype(BF)
    out_ref[2 * HALF : 3 * HALF] = (grad * activated).astype(BF)
    out_ref[3 * HALF :] = jnp.zeros((BUNDLE - 3 * HALF, HID), BF)


def pick_kernel(partner, pieces_ref, out_ref):
    for j in range(32):
        out_ref[j] = pieces_ref[partner[j]]


def bundle_part(acts_ref, part):
    picked = acts_ref[:, part * HALF : (part + 1) * HALF, :]
    return picked.reshape(picked.shape[0] * HALF, HID)


def terms_kernel(coords, acts_ref, gate_ref, up_ref, down_ref, out_ref):
    out = dot_last(bundle_part(acts_ref, 0), down_ref[...])
    back = dot_last(bundle_part(acts_ref, 1), gate_ref[...]) + dot_last(bundle_part(acts_ref, 2), up_ref[...])
    both = jnp.concatenate([out, back], axis=1)
    for y in range(out_ref.shape[1]):
        for x in range(4):
            at = (4 * y + x) * CAP
            out_ref[x, y] = both[at : at + CAP].astype(BF)


def merge_kernel(held, coords, tail_ref, rows_ref, out_ref):
    weights = weight_rows(tail_ref[...].reshape(PAIR, 128), tuple(held[4 * coords[0] + i] >> 1 for i in range(4)))
    place = slot_places(weights)
    out = jnp.zeros(out_ref.shape, F32)
    back = jnp.zeros(out_ref.shape, F32)
    for i in range(4):
        hit = one_hot(place[i : i + 1], HALF)
        out = out + dot_first(jnp.where(hit, weights[i : i + 1], 0.0).astype(BF), rows_ref[i])
        back = back + dot_first(as_matrix(hit), rows_ref[i])
    lane = lax.broadcasted_iota(jnp.int32, out_ref.shape, 1)
    out_ref[...] = jnp.where(lane < FEAT, out, back).astype(BF)


def new_rows_kernel(held, partner, coords, packed_ref, rows_ref, scaled_ref):
    expert = held[partner[4 * coords[0] + coords[1]]] >> 1
    for i in range(packed_ref.shape[0]):
        hit, weights = chunk_hits(packed_ref[i, :, WIDE - 128 : WIDE], expert)
        pick = as_matrix(hit)
        rows_ref[i] = dot(pick, packed_ref[i, :, WIDE : WIDE + FEAT]).astype(BF)
        scaled_ref[i] = (slot_weights(hit, weights) * dot(pick, packed_ref[i, :, :FEAT])).astype(BF)


def slab_grad_kernel(rows_ref, scaled_ref, acts_ref, gate_ref, up_ref, down_ref):
    gate_ref[...] = dot_first(rows_ref[...], bundle_part(acts_ref, 1)).astype(BF)
    up_ref[...] = dot_first(rows_ref[...], bundle_part(acts_ref, 2)).astype(BF)
    down_ref[...] = dot_first(scaled_ref[...], bundle_part(acts_ref, 0)).astype(BF)


def shaped(*shape):
    return jax.ShapeDtypeStruct(shape, BF)


def params():
    return pltpu.CompilerParams(vmem_limit_bytes=32 * 1024 * 1024)


def cost(mflop, kbytes):
    return pl.CostEstimate(flops=mflop * 1_000_000, bytes_accessed=kbytes * 1000, transcendentals=0)


def call(kernel, grid, in_specs, out_specs, out_shape, estimate, scalars, *operands):
    return pl.pallas_call(
        kernel,
        grid_spec=pltpu.PrefetchScalarGridSpec(
            num_scalar_prefetch=len(scalars), grid=grid, in_specs=in_specs, out_specs=out_specs
        ),
        out_shape=out_shape,
        compiler_params=params(),
        cost_estimate=estimate,
    )(*scalars, *operands)


def local(kernel, out_shape, estimate, *operands):
    return pl.pallas_call(kernel, out_shape=out_shape, compiler_params=params(), cost_estimate=estimate)(*operands)


def whole(*shape):
    return pl.BlockSpec(shape, lambda i, *scalars: (0,) * len(shape))


def lead_block(*shape):
    return pl.BlockSpec(shape, lambda i, *scalars: (i,) + (0,) * (len(shape) - 1))


def core_half(count, rows, lanes, mine):
    if mine:
        return pl.BlockSpec((count, None, rows, lanes), lambda i, coords: (i, coords[2], 0, 0))
    return pl.BlockSpec((count, None, rows, lanes), lambda i, coords: (i, 1 - coords[2], 0, 0))


def in_hbm(value):
    return pltpu.with_memory_space_constraint(value, pltpu.HBM)


def swap(value):
    return lax.ppermute(value, "core", [(0, 1), (1, 0)])


def exchange(value, axes):
    return lax.all_to_all(value, axes, split_axis=0, concat_axis=0, tiled=True)


def body(tokens, cotangent, expert_ids, route_probs, held_before, partner, gate_slabs, up_slabs, down_slabs):
    gate, up, down = gate_slabs[0], up_slabs[0], down_slabs[0].T
    coords = jnp.stack([lax.axis_index("y"), lax.axis_index("x"), lax.axis_index("core")]).astype(jnp.int32)

    packed, sent = call(
        prep_kernel,
        (1,),
        [whole(TOK, FEAT), whole(TOK, FEAT), whole(8, TOK), whole(8, TOK)],
        (whole(TOK, 2 * WIDE), whole(CHUNKS, HALF, 2 * FEAT)),
        (shaped(TOK, 2 * WIDE), shaped(CHUNKS, HALF, 2 * FEAT)),
        cost(150, 2600),
        (held_before,),
        tokens,
        cotangent,
        expert_ids.T,
        route_probs.T,
    )
    everyone = lax.all_gather(packed, ("y", "x"), tiled=True)
    own_rows = exchange(sent.reshape(32, CAP, 2 * FEAT), ("y", "x"))

    rows_view = own_rows.reshape(8, 2, HALF, 2 * FEAT)
    weight_specs = [whole(FEAT, HID), whole(FEAT, HID), whole(FEAT, HID)]
    sums_block = lead_block(4, HALF, 3 * HID)
    sending = call(
        send_kernel,
        (2,),
        [core_half(4, HALF, 2 * FEAT, False)] + weight_specs,
        sums_block,
        shaped(8, HALF, 3 * HID),
        cost(900, 4500),
        (coords,),
        rows_view,
        gate,
        up,
        down,
    )
    pairs = call(
        keep_kernel,
        (2,),
        [core_half(4, HALF, 2 * FEAT, True)] + weight_specs + [sums_block],
        sums_block,
        shaped(8, HALF, 3 * HID),
        cost(900, 6500),
        (coords,),
        rows_view,
        gate,
        up,
        down,
        swap(sending),
    )
    acts = local(activation_kernel, shaped(BUNDLE, HID), cost(3, 2300), exchange(pairs, "z"))

    own_acts = lax.all_gather(acts, ("z", "core"), tiled=True).reshape(CHUNKS, BUNDLE, HID)
    pieces = exchange(acts.reshape(32, 8, HID), ("y", "x"))
    picked = call(
        pick_kernel,
        (1,),
        [whole(32, 8, HID)],
        whole(32, 8, HID),
        shaped(32, 8, HID),
        cost(1, 520),
        (partner,),
        pieces,
    )
    moved = exchange(picked, ("y", "x")).reshape(BUNDLE, HID)

    terms = call(
        terms_kernel,
        (4,),
        [
            lead_block(4, BUNDLE, HID),
            whole(FEAT, HID),
            whole(FEAT, HID),
            whole(FEAT, HID),
        ],
        pl.BlockSpec((4, 2, CAP, 2 * FEAT), lambda i, coords: (0, i, 0, 0)),
        shaped(4, 8, CAP, 2 * FEAT),
        cost(1800, 8000),
        (coords,),
        in_hbm(own_acts),
        gate,
        up,
        down,
    )
    new_acts = lax.all_gather(moved, ("z", "core"), tiled=True).reshape(CHUNKS, BUNDLE, HID)

    returned = exchange(terms.reshape(4, 8 * CAP, 2 * FEAT), "x")
    merged = call(
        merge_kernel,
        (4,),
        [
            pl.BlockSpec((2, None, TOK, 128), lambda i, held, coords: (i, coords[1], 0, 3)),
            pl.BlockSpec((4, HALF, 2 * FEAT), lambda i, held, coords: (0, i, 0)),
        ],
        lead_block(PAIR, 2 * FEAT),
        shaped(8 * TOK, 2 * FEAT),
        cost(300, 3500),
        (held_before, coords),
        in_hbm(everyone.reshape(8, 4, TOK, 2 * WIDE)),
        returned,
    )
    home = exchange(merged.reshape(8, TOK, 2 * FEAT), "y")

    rows, scaled = call(
        new_rows_kernel,
        (4,),
        [lead_block(4, PAIR, 2 * WIDE)],
        (lead_block(4, HALF, FEAT), lead_block(4, HALF, FEAT)),
        (shaped(CHUNKS, HALF, FEAT), shaped(CHUNKS, HALF, FEAT)),
        cost(600, 6500),
        (held_before, partner, coords),
        in_hbm(everyone.reshape(CHUNKS, PAIR, 2 * WIDE)),
    )
    gate_grad, up_grad, down_grad = local(
        slab_grad_kernel,
        (shaped(FEAT, HID), shaped(FEAT, HID), shaped(FEAT, HID)),
        cost(1800, 8000),
        rows.reshape(ROWS, FEAT),
        scaled.reshape(ROWS, FEAT),
        new_acts,
    )

    total = jnp.sum(home.astype(F32), axis=0).astype(BF)
    return (total[:, :FEAT], total[:, FEAT:], gate_grad[None], up_grad[None], down_grad.T[None])


def solution(mesh):
    fine = Mesh(mesh.devices.reshape(8, 4, 8, 2), ("y", "x", "z", "core"))
    expert, dp = ("y", "x"), ("z", "core")
    slab = P(expert, dp, None)
    down = P(expert, None, dp)
    return jax.shard_map(
        body,
        mesh=fine,
        in_specs=(P(expert, dp), P(expert, dp), P(expert, None), P(expert, None), P(), P(), slab, slab, down),
        out_specs=(P(expert, dp), P(expert, dp), slab, slab, down),
        check_vma=False,
    )
```

time: 280 us -> 339 us (1.21)
  waiting for transfers between devices: 80.2 us -> 174 us
  starting transfers between devices: 38.4 us -> 23.4 us
  local copies, waits for them, and re-layouts: 20.5 us -> 10.5 us
  Pallas kernels: 33.5 us -> 28.9 us
    all_gather x1, waiting for transfers between devices: 23.6 us -> 77.7 us  [body(): everyone = lax.all_gather(packed, ('y', 'x'), tiled=True)]
    all_gather x1, waiting for transfers between devices: 0.02 us -> 31.5 us  [body(): lax.all_gather(moved, ('z', 'core'), tiled=True)]
    all_to_all x3, starting transfers between devices: 28.4 us -> 18.6 us  [exchange(): return lax.all_to_all(value, axes, split_axis=0, concat_axis=0, tiled=True)]
    all_to_all x3, waiting for transfers between devices: 43.5 us -> 52.3 us  [exchange(): return lax.all_to_all(value, axes, split_axis=0, concat_axis=0, tiled=True)]
    unnamed x32 -> x30, local copies, waits for them, and re-layouts: 16.4 us -> 9.77 us
    ppermute x2 -> x1, starting transfers between devices: 9.89 us -> 4.73 us  [swap(): return lax.ppermute(value, 'core', [(0, 1), (1, 0)])]
    all_to_all x4 -> x3, blocking collectives: 88.6 us -> 87.8 us  [exchange(): return lax.all_to_all(value, axes, split_axis=0, concat_axis=0, tiled=True)]
  transfers between devices with their start and end apart: 8 -> 7, of which waited for: 6 -> 5; matrix products, arithmetic and copies ran while one was open for 2% -> 0% of each run, Pallas kernels for 9% -> 7%
where the time goes in v3:
time: 339 us; the launch traced here: 338 us
  waiting for transfers between devices  174 us (51%)
  blocking collectives  87.8 us (26%)
  Pallas kernels  28.9 us (9%)
  starting transfers between devices  23.4 us (7%)
  between operations  13.9 us (4%)
  local copies, waits for them, and re-layouts  10.5 us (3%)
    all_to_all x3, blocking collectives, exchange(): return lax.all_to_all(value, axes, split_axis=0, concat_axis=0, tiled=True)  87.8 us
    all_gather x1, waiting for transfers between devices, body(): everyone = lax.all_gather(packed, ('y', 'x'), tiled=True)  77.7 us
    all_to_all x3, waiting for transfers between devices, exchange(): return lax.all_to_all(value, axes, split_axis=0, concat_axis=0, tiled=True)  52.3 us
    all_gather x1, waiting for transfers between devices, body(): lax.all_gather(moved, ('z', 'core'), tiled=True)  31.5 us
    pallas_call x7, Pallas kernels, call(): pl.pallas_call(kernel, grid_spec=pltpu.PrefetchScalarGridSpec(num_scalar_...  25.1 us
    all_to_all x3, starting transfers between devices, exchange(): return lax.all_to_all(value, axes, split_axis=0, concat_axis=0, tiled=True)  18.6 us
    unnamed x30, local copies, waits for them, and re-layouts  9.77 us
    all_gather x1, waiting for transfers between devices, body(): lax.all_gather(acts, ('z', 'core'), tiled=True).reshape(CHUNKS, BUNDLE, HID)  7.75 us
  transfers between devices with their start and end apart: 7, of which 5 were waited for; matrix products, arithmetic and copies ran while one was open for 0% of the time, Pallas kernels for 7%

profile of v3, /device:TPU:1, one launch (start us, length us, event | category | flops | bytes accessed | tf_op | source)
XLA Modules:
  0.0 338.3 jit_solution(6750853640243213843)
XLA Ops:
  7.2 0.6 copy-done.8
  7.8 0.8 copy-done.11
  8.7 0.8 copy-done.12
  9.5 0.7 copy-done.13
  10.2 0.7 copy-done.14
  10.9 1.8 shard_map.128
  12.7 1.4 copy-done.7
  14.1 10.6 %all-to-all-start = ((bf16[32,40,896]{2,1,0:T(8,128)(2,1)}), bf16[32,40,896]{2,1,0:T(8,128)(2,1)S(1)}, u32[]{:S(2)}, u32[]{:S(2)}) async-start(bf16[32,40,896]{2,1,0:T(8,128)(2,1)} %bitcast.40), calls=%async_computation | async-start | bytes 4587520 | tf_op jit(solution)/shard_map/all_to_all | solution.py:229
  24.9 52.3 %all-to-all-done = bf16[32,40,896]{2,1,0:T(8,128)(2,1)S(1)} async-done(((bf16[32,40,896]{2,1,0:T(8,128)(2,1)}), bf16[32,40,896]{2,1,0:T(8,128)(2,1)S(1)}, u32[]{:S(2)}, u32[]{:S(2)}) %all-to-all-start) | async-done | bytes 2293792 | tf_op jit(solution)/shard_map/all_to_all | solution.py:229
  77.2 1.0 copy-done.4
  78.2 2.0 shard_map.129
  80.2 4.7 %collective-permute-start = (bf16[8,80,1536]{2,1,0:T(8,128)(2,1)S(1)}, bf16[8,80,1536]{2,1,0:T(8,128)(2,1)S(1)}, u32[]{:S(2)}, u32[]{:S(2)}) collective-permute-start(bf16[8,80,1536]{2,1,0:T(8,128)(2,1)S(1)} %shard_map.129), channel_id=1, source_target_pairs={{0,1},{1,0},{2,3},{3,2},{4,5},{5,4},{6,7},{7,6},{8,9},{9,8},{10,11... | collective-permute-start | bytes 5898248 | tf_op jit(solution)/shard_map/ppermute | solution.py:225
  85.0 3.6 %collective-permute-done.got_ref = bf16[8,80,1536]{2,1,0:T(8,128)(2,1)S(1)} collective-permute-done((bf16[8,80,1536]{2,1,0:T(8,128)(2,1)S(1)}, bf16[8,80,1536]{2,1,0:T(8,128)(2,1)S(1)}, u32[]{:S(2)}, u32[]{:S(2)}) %collective-permute-start) | collective-permute-done | bytes 1966112 | tf_op jit(solution)/shard_map/ppermute | solution.py:225
  88.6 2.0 shard_map.130
  90.6 57.4 %all_to_all.30.sums_ref = bf16[8,80,1536]{2,1,0:T(8,128)(2,1)S(1)} all-to-all(bf16[8,80,1536]{2,1,0:T(8,128)(2,1)S(1)} %shard_map.130), channel_id=1, replica_groups=mesh['y'=8,'x'=4,'z'=8,'core'=2] {'z'}, dimensions={0} | all-to-all | bytes 3932160 | tf_op jit(solution)/shard_map/all_to_all | solution.py:229
  148.0 1.0 shard_map.131
  149.1 0.7 all-gather.4.cloned.1.call-update
  149.9 16.1 %all_to_all.31.pieces_ref = bf16[32,8,512]{2,1,0:T(8,128)(2,1)S(1)} all-to-all(bf16[32,8,512]{2,1,0:T(8,128)(2,1)} %bitcast.19), channel_id=1, replica_groups=mesh['y'=8,'x'=4,'z'=8,'core'=2] {'y','x'}, dimensions={0} | all-to-all | bytes 524288 | tf_op jit(solution)/shard_map/all_to_all | solution.py:229
  166.0 0.6 shard_map.135
  166.6 14.3 %all_to_all.32 = bf16[32,8,512]{2,1,0:T(8,128)(2,1)} all-to-all(bf16[32,8,512]{2,1,0:T(8,128)(2,1)S(1)} %shard_map.135), channel_id=1, replica_groups=mesh['y'=8,'x'=4,'z'=8,'core'=2] {'y','x'}, dimensions={0} | all-to-all | bytes 524288 | tf_op jit(solution)/shard_map/all_to_all | solution.py:229
  180.9 7.8 %all-gather.6.cloned.1.call-done = bf16[4096,512]{1,0:T(8,128)(2,1)} async-done(((bf16[256,512]{1,0:T(8,128)(2,1)}), bf16[4096,512]{1,0:T(8,128)(2,1)}) %all-gather.6.cloned.1.call-update) | async-done | bytes 4194320 | tf_op jit(solution)/shard_map/all_gather | solution.py:284
  188.7 5.5 %shard_map.132 = bf16[4,8,40,896]{3,2,1,0:T(8,128)(2,1)S(1)} custom-call(s32[3]{0:T(128)S(1)} %pad_add_fusion.coords, bf16[16,256,512]{2,1,0:T(8,128)(2,1)} %bitcast.47, bf16[448,512]{1,0:T(8,128)(2,1)S(1)} %bitcast.33, bf16[448,512]{1,0:T(8,128)(2,1)S(1)} %bitcast.36, bf16[448,512]{1,0:T(8,128)(2,1)S(1)} %bitcast.39), custom_call_target="tpu_custom_call" | custom-call | flops 1800000000 | bytes 8000000 | tf_op jit(solution)/shard_map/pallas_call | solution.py:191
  194.2 1.4 copy-done
  195.6 4.1 %all-to-all-start.2 = ((bf16[4,320,896]{2,1,0:T(8,128)(2,1)}), bf16[4,320,896]{2,1,0:T(8,128)(2,1)S(1)}, u32[]{:S(2)}, u32[]{:S(2)}) async-start(bf16[4,320,896]{2,1,0:T(8,128)(2,1)} %bitcast.29), calls=%async_computation.2 | async-start | bytes 4587520 | tf_op jit(solution)/shard_map/all_to_all | solution.py:229
  199.7 77.7 %all-gather.4.cloned.1.call-done = bf16[2048,1024]{1,0:T(8,128)(2,1)} async-done(((bf16[64,1024]{1,0:T(8,128)(2,1)}), bf16[2048,1024]{1,0:T(8,128)(2,1)}) %all-gather.4.cloned.1.call-update) | async-done | bytes 4194320 | tf_op jit(solution)/shard_map/all_gather | solution.py:249
  277.4 6.0 %shard_map.133 = bf16[512,896]{1,0:T(8,128)(2,1)} custom-call(s32[32]{0:T(128)S(1)} %copy-done.9, s32[3]{0:T(128)S(1)} %pad_add_fusion.coords, bf16[8,4,64,1024]{3,2,1,0:T(8,128)(2,1)} %bitcast.45, bf16[4,320,896]{2,1,0:T(8,128)(2,1)S(1)} %all-to-all-done.2.rows_ref), custom_call_target="tpu_custom_call" | custom-call | flops 300000000 | bytes 3500000 | tf_op jit(solution)/shard_map/pallas_call | solution.py:191
  283.4 3.9 %all-to-all-start.3 = ((bf16[8,64,896]{2,1,0:T(8,128)(2,1)}), bf16[8,64,896]{2,1,0:T(8,128)(2,1)S(1)}, u32[]{:S(2)}, u32[]{:S(2)}) async-start(bf16[8,64,896]{2,1,0:T(8,128)(2,1)} %bitcast.15), calls=%async_computation.3 | async-start | bytes 1835008 | tf_op jit(solution)/shard_map/all_to_all | solution.py:229
  287.3 7.2 %shard_map.134 = (bf16[16,80,448]{2,1,0:T(8,128)(2,1)S(1)}, bf16[16,80,448]{2,1,0:T(8,128)(2,1)S(1)}) custom-call(s32[32]{0:T(128)S(1)} %copy-done.9, s32[32]{0:T(128)S(1)} %copy-done.10, s32[3]{0:T(128)S(1)} %pad_add_fusion.coords, bf16[16,128,1024]{2,1,0:T(8,128)(2,1)} %bitcast.46), custom_call_target="tpu_custom_call" | custom-call | flops 600000000 | bytes 6500000 | tf_op jit(solution)/shard_map/pallas_call | solution.py:191
  294.5 31.5 %all-gather.8.cloned.1.call-done = bf16[4096,512]{1,0:T(8,128)(2,1)} async-done(((bf16[256,512]{1,0:T(8,128)(2,1)}), bf16[4096,512]{1,0:T(8,128)(2,1)}) %all-gather.8.cloned.1.call-update) | async-done | bytes 4194320 | tf_op jit(solution)/shard_map/all_gather | solution.py:316
  326.0 2.2 copy-done.1
  328.2 2.7 shard_map.136
  331.1 0.7 fusion
  (30 shorter events, 0.4 us)
Async XLA Ops:
  7.2 0.7 copy-start.8
  7.8 0.8 copy-start.11
  8.7 0.8 copy-start.12
  9.5 0.7 copy-start.13
  10.2 0.7 copy-start.14
  12.7 1.4 copy-start.7
  14.1 63.1 %copy-start.2 = (bf16[1,448,512]{2,1,0:T(8,128)(2,1)S(1)}, bf16[1,448,512]{2,1,0:T(8,128)(2,1)}, u32[]{:S(2)}) copy-start(bf16[1,448,512]{2,1,0:T(8,128)(2,1)} %param.15) | copy-start | bytes 1376260
  14.1 63.1 %copy-start.3 = (bf16[1,448,512]{2,1,0:T(8,128)(2,1)S(1)}, bf16[1,448,512]{2,1,0:T(8,128)(2,1)}, u32[]{:S(2)}) copy-start(bf16[1,448,512]{2,1,0:T(8,128)(2,1)} %param.16) | copy-start | bytes 1376260
  14.1 63.1 %all-to-all-start = ((bf16[32,40,896]{2,1,0:T(8,128)(2,1)}), bf16[32,40,896]{2,1,0:T(8,128)(2,1)S(1)}, u32[]{:S(2)}, u32[]{:S(2)}) async-start(bf16[32,40,896]{2,1,0:T(8,128)(2,1)} %bitcast.40), calls=%async_computation | async-start | bytes 4587520 | tf_op jit(solution)/shard_map/all_to_all | solution.py:229
  24.7 163.9 %all-gather.6.cloned.1.call-start = ((), (), s32[]{:S(2)}) async-start(), calls=%async_computation.7 | async-start | bytes 4456448 | tf_op jit(solution)/shard_map/all_gather | solution.py:284
  77.2 1.0 copy-start.4
  78.2 10.4 %copy-start.5 = (bf16[1,512,448]{1,2,0:T(8,128)(2,1)S(1)}, bf16[1,512,448]{1,2,0:T(8,128)(2,1)}, u32[]{:S(2)}) copy-start(bf16[1,512,448]{1,2,0:T(8,128)(2,1)} %param.17) | copy-start | bytes 1376260
  80.2 8.3 %collective-permute-start = (bf16[8,80,1536]{2,1,0:T(8,128)(2,1)S(1)}, bf16[8,80,1536]{2,1,0:T(8,128)(2,1)S(1)}, u32[]{:S(2)}, u32[]{:S(2)}) collective-permute-start(bf16[8,80,1536]{2,1,0:T(8,128)(2,1)S(1)} %shard_map.129), channel_id=1, source_target_pairs={{0,1},{1,0},{2,3},{3,2},{4,5},{5,4},{6,7},{7,6},{8,9},{9,8},{10,11... | collective-permute-start | bytes 5898248 | tf_op jit(solution)/shard_map/ppermute | solution.py:225
  148.0 18.0 %copy-start.10 = (s32[32]{0:T(128)S(1)}, s32[32]{0:T(128)}, u32[]{:S(2)}) copy-start(s32[32]{0:T(128)} %partner.3) | copy-start | bytes 388
  148.0 40.6 %copy-start.6 = (bf16[1,512,448]{1,2,0:T(8,128)(2,1)S(1)}, bf16[1,512,448]{1,2,0:T(8,128)(2,1)}, u32[]{:S(2)}) copy-start(bf16[1,512,448]{1,2,0:T(8,128)(2,1)} %param.17) | copy-start | bytes 1376260
  149.1 128.3 %all-gather.4.cloned.1.call-start = ((), (), s32[]{:S(2)}) async-start(), calls=%async_computation.6 | async-start | bytes 4325376 | tf_op jit(solution)/shard_map/all_gather | solution.py:249
  149.8 176.2 %all-gather.8.cloned.1.call-start = ((), (), s32[]{:S(2)}) async-start(), calls=%async_computation.8 | async-start | bytes 4456448 | tf_op jit(solution)/shard_map/all_gather | solution.py:316
  194.2 1.4 copy-start
  195.6 81.8 %copy-start.9 = (s32[32]{0:T(128)S(1)}, s32[32]{0:T(128)}, u32[]{:S(2)}) copy-start(s32[32]{0:T(128)} %held.5) | copy-start | bytes 388
  195.6 81.8 %all-to-all-start.2 = ((bf16[4,320,896]{2,1,0:T(8,128)(2,1)}), bf16[4,320,896]{2,1,0:T(8,128)(2,1)S(1)}, u32[]{:S(2)}, u32[]{:S(2)}) async-start(bf16[4,320,896]{2,1,0:T(8,128)(2,1)} %bitcast.29), calls=%async_computation.2 | async-start | bytes 4587520 | tf_op jit(solution)/shard_map/all_to_all | solution.py:229
  283.4 47.5 %all-to-all-start.3 = ((bf16[8,64,896]{2,1,0:T(8,128)(2,1)}), bf16[8,64,896]{2,1,0:T(8,128)(2,1)S(1)}, u32[]{:S(2)}, u32[]{:S(2)}) async-start(bf16[8,64,896]{2,1,0:T(8,128)(2,1)} %bitcast.15), calls=%async_computation.3 | async-start | bytes 1835008 | tf_op jit(solution)/shard_map/all_to_all | solution.py:229
  326.0 2.2 copy-start.1
Sparse Core Ops, SparseCore 0:
  149.2 39.3 all-gather.5
  192.4 84.9 all-gather.3
  279.5 46.4 all-gather.7

commit v4 on v3

v4 whole, which is shorter than its diff:
```python
import jax
import jax.numpy as jnp
from jax import lax
from jax.experimental import pallas as pl
from jax.experimental.pallas import tpu as pltpu
from jax.sharding import Mesh, PartitionSpec as P

TOK = 64
CAP = 40
FEAT = 448
PACK = 2 * FEAT + TOK
HID = 512
PAIR = 2 * TOK
HALF = 2 * CAP
CHUNKS = 16
ROWS = CHUNKS * HALF
BUNDLE = 256
BF = jnp.bfloat16
F32 = jnp.float32


def dot(lhs, rhs):
    return jnp.dot(lhs, rhs, preferred_element_type=F32)


def dot_last(lhs, rhs):
    return lax.dot_general(lhs, rhs, (((1,), (1,)), ((), ())), preferred_element_type=F32)


def dot_first(lhs, rhs):
    return lax.dot_general(lhs, rhs, (((0,), (0,)), ((), ())), preferred_element_type=F32)


def as_matrix(hit):
    return jnp.where(hit, 1.0, 0.0).astype(BF)


def weight_rows(dense, experts):
    lane = lax.broadcasted_iota(jnp.int32, (8, TOK), 1)
    row = lax.broadcasted_iota(jnp.int32, (8, TOK), 0)
    hit = lane < 0
    for i, expert in enumerate(experts):
        hit = hit | ((row == i) & (lane == expert))
    return dot_last(as_matrix(hit), dense)


def slot_places(weights):
    count = weights.shape[1]
    routed = weights > 0.0
    source = lax.broadcasted_iota(jnp.int32, (count, count), 0)
    target = lax.broadcasted_iota(jnp.int32, (count, count), 1)
    earlier = (source < target) & ((source >> 6) == (target >> 6))
    position = dot(as_matrix(routed), as_matrix(earlier))
    group = lax.broadcasted_iota(jnp.int32, weights.shape, 1) >> 6
    return jnp.where(routed, position.astype(jnp.int32) + CAP * group, -1)


def one_hot(place, rows):
    return lax.broadcasted_iota(jnp.int32, (rows, place.shape[1]), 0) == place


def slot_weights(hit, weights):
    return jnp.sum(jnp.where(hit, weights, 0.0), axis=1, keepdims=True)


def two_slabs(weights, place, i):
    slot = lax.broadcasted_iota(jnp.int32, (HALF, TOK), 0)
    first = slot < CAP
    one, two = slice(2 * i, 2 * i + 1), slice(2 * i + 1, 2 * i + 2)
    hit = jnp.where(first, slot, slot - CAP) == jnp.where(first, place[one], place[two])
    return hit, jnp.where(hit, jnp.where(first, weights[one], weights[two]), 0.0)


def weights_of(names, ids_ref, probs_ref):
    return sum(jnp.where(ids_ref[k : k + 1] == names, probs_ref[k : k + 1].astype(F32), 0.0) for k in range(8))


def pack_kernel(tok_ref, cot_ref, ids_ref, probs_ref, packed_ref):
    names = lax.broadcasted_iota(jnp.int32, (TOK, TOK), 0)
    same = names == lax.broadcasted_iota(jnp.int32, (TOK, TOK), 1)
    dense = dot_first(weights_of(names, ids_ref, probs_ref).astype(BF), as_matrix(same)).astype(BF)
    packed_ref[...] = jnp.concatenate([tok_ref[...], cot_ref[...], dense], axis=1)


def slab_slots(held, ids_ref, probs_ref):
    slab = lax.broadcasted_iota(jnp.int32, (32, TOK), 0)
    expert = jnp.zeros((32, TOK), jnp.int32)
    for i in range(32):
        expert = jnp.where(slab == i, held[i] >> 1, expert)
    weights = weights_of(expert, ids_ref, probs_ref)
    return weights, slot_places(weights)


def slots_kernel(held, ids_ref, probs_ref, plain_ref, weighted_ref):
    weights, place = slab_slots(held, ids_ref, probs_ref)
    pairs = [two_slabs(weights, place, i) for i in range(CHUNKS)]
    token = lax.broadcasted_iota(jnp.int32, (TOK, TOK), 0)
    same = as_matrix(token == lax.broadcasted_iota(jnp.int32, (TOK, TOK), 1))
    plain = jnp.concatenate([as_matrix(hit) for hit, _ in pairs], axis=0)
    weighted = jnp.concatenate([factor.astype(BF) for _, factor in pairs], axis=0)
    plain_ref[...] = dot_last(same, plain).astype(BF)
    weighted_ref[...] = dot_last(same, weighted).astype(BF)


def rows_kernel(held, coords, packed_ref, after_ref, out_ref):
    weights = weight_rows(packed_ref[:, 2 * FEAT :], tuple(held[4 * coords[0] + i] >> 1 for i in range(4)))
    place = slot_places(weights)
    cot_lane = lax.broadcasted_iota(jnp.int32, (HALF, 2 * FEAT), 1) >= FEAT
    for i in range(4):
        hit = one_hot(place[i : i + 1], HALF)
        rows = dot(as_matrix(hit), packed_ref[:, : 2 * FEAT])
        out_ref[i] = (rows * jnp.where(cot_lane, slot_weights(hit, weights[i : i + 1]), 1.0)).astype(BF)


def products(rows_ref, gate_ref, up_ref, down_ref):
    count = rows_ref.shape[0]
    rows = rows_ref[...].reshape(count * HALF, 2 * FEAT)
    tok, scaled = rows[:, :FEAT], rows[:, FEAT:]
    three = dot(tok, gate_ref[...]), dot(tok, up_ref[...]), dot(scaled, down_ref[...])
    return [(slice(i * HID, (i + 1) * HID), part.reshape(count, HALF, HID)) for i, part in enumerate(three)]


def send_kernel(coords, rows_ref, gate_ref, up_ref, down_ref, out_ref):
    for lanes, part in products(rows_ref, gate_ref, up_ref, down_ref):
        out_ref[:, :, lanes] = part.astype(BF)


def keep_kernel(coords, rows_ref, gate_ref, up_ref, down_ref, got_ref, out_ref):
    for lanes, part in products(rows_ref, gate_ref, up_ref, down_ref):
        out_ref[:, :, lanes] = (part + got_ref[:, :, lanes].astype(F32)).astype(BF)


def activation_kernel(coords, sums_ref, after_ref, out_ref):
    sums = sums_ref[...].astype(F32)
    gate, up, grad = sums[:, :HID], sums[:, HID : 2 * HID], sums[:, 2 * HID :]
    sig = jax.nn.sigmoid(gate)
    activated = gate * sig
    out_ref[0:HALF] = (activated * up).astype(BF)
    out_ref[HALF : 2 * HALF] = (grad * up * sig * (1.0 + gate * (1.0 - sig))).astype(BF)
    out_ref[2 * HALF : 3 * HALF] = (grad * activated).astype(BF)
    out_ref[3 * HALF :] = jnp.zeros((BUNDLE - 3 * HALF, HID), BF)


def pick_kernel(partner, pieces_ref, out_ref):
    for j in range(32):
        out_ref[j] = pieces_ref[partner[j]]


def bundle_part(acts_ref, part):
    picked = acts_ref[:, part * HALF : (part + 1) * HALF, :]
    return picked.reshape(picked.shape[0] * HALF, HID)


def terms_kernel(coords, acts_ref, gate_ref, up_ref, down_ref, out_ref):
    out = dot_last(bundle_part(acts_ref, 0), down_ref[...])
    back = dot_last(bundle_part(acts_ref, 1), gate_ref[...]) + dot_last(bundle_part(acts_ref, 2), up_ref[...])
    both = jnp.concatenate([out, back], axis=1)
    for i in range(out_ref.shape[0]):
        out_ref[i, 0] = both[i * CAP : (i + 1) * CAP].astype(BF)


def merge_kernel(plain_ref, weighted_ref, rows_ref, out_ref, back_ref):
    out_ref[...] = dot(weighted_ref[...], rows_ref[...])[:, :FEAT].astype(BF)
    back_ref[...] = dot(plain_ref[...], rows_ref[...])[:, FEAT:].astype(BF)


def slab_grad_kernel(rows_ref, acts_ref, gate_ref, up_ref, down_ref):
    rows = rows_ref[:, :FEAT]
    gate_ref[...] = dot_first(rows, bundle_part(acts_ref, 1)).astype(BF)
    up_ref[...] = dot_first(rows, bundle_part(acts_ref, 2)).astype(BF)
    down_ref[...] = dot_first(rows_ref[:, FEAT:], bundle_part(acts_ref, 0)).astype(BF)


def shaped(*shape):
    return jax.ShapeDtypeStruct(shape, BF)


def params():
    return pltpu.CompilerParams(vmem_limit_bytes=32 * 1024 * 1024)


def cost(mflop, kbytes):
    return pl.CostEstimate(flops=mflop * 1_000_000, bytes_accessed=kbytes * 1000, transcendentals=0)


def call(kernel, grid, in_specs, out_specs, out_shape, estimate, scalars, *operands):
    return pl.pallas_call(
        kernel,
        grid_spec=pltpu.PrefetchScalarGridSpec(
            num_scalar_prefetch=len(scalars), grid=grid, in_specs=in_specs, out_specs=out_specs
        ),
        out_shape=out_shape,
        compiler_params=params(),
        cost_estimate=estimate,
    )(*scalars, *operands)


def local(kernel, out_shape, estimate, *operands):
    return pl.pallas_call(kernel, out_shape=out_shape, compiler_params=params(), cost_estimate=estimate)(*operands)


def whole(*shape):
    return pl.BlockSpec(shape, lambda i, *scalars: (0,) * len(shape))


def lead_block(*shape):
    return pl.BlockSpec(shape, lambda i, *scalars: (i,) + (0,) * (len(shape) - 1))


def core_half(count, rows, lanes, mine):
    if mine:
        return pl.BlockSpec((count, None, rows, lanes), lambda i, coords: (i, coords[2], 0, 0))
    return pl.BlockSpec((count, None, rows, lanes), lambda i, coords: (i, 1 - coords[2], 0, 0))


ANYWHERE = pl.BlockSpec(memory_space=pl.ANY)


def in_hbm(value):
    return pltpu.with_memory_space_constraint(value, pltpu.HBM)


def swap(value):
    return lax.ppermute(value, "core", [(0, 1), (1, 0)])


def exchange(value, axes):
    return lax.all_to_all(value, axes, split_axis=0, concat_axis=0, tiled=True)


def body(tokens, cotangent, expert_ids, route_probs, held_before, partner, gate_slabs, up_slabs, down_slabs):
    gate, up, down = gate_slabs[0], up_slabs[0], down_slabs[0].T
    coords = jnp.stack([lax.axis_index("y"), lax.axis_index("x"), lax.axis_index("core")]).astype(jnp.int32)

    ids, probs = expert_ids.T, route_probs.T
    packed = local(
        pack_kernel,
        shaped(TOK, PACK),
        cost(10, 300),
        in_hbm(tokens),
        in_hbm(cotangent),
        in_hbm(ids),
        in_hbm(probs),
    )
    column = lax.all_gather(packed, "y", tiled=True)

    def slab_rows(held, after):
        sent = call(
            rows_kernel,
            (4,),
            [lead_block(PAIR, PACK), ANYWHERE],
            pl.BlockSpec((4, HALF, 2 * FEAT), lambda i, held, coords: (0, i, 0)),
            pltpu.HBM((4, 4 * HALF, 2 * FEAT), BF),
            cost(600, 3500),
            (held, coords),
            column,
            in_hbm(after),
        )
        return exchange(sent, "x")

    own_rows = slab_rows(held_before, held_before)
    rows_view = own_rows.reshape(8, 2, HALF, 2 * FEAT)
    weight_specs = [whole(FEAT, HID), whole(FEAT, HID), whole(FEAT, HID)]
    sums_block = lead_block(4, HALF, 3 * HID)
    sending = call(
        send_kernel,
        (2,),
        [core_half(4, HALF, 2 * FEAT, False)] + weight_specs,
        sums_block,
        shaped(8, HALF, 3 * HID),
        cost(900, 4500),
        (coords,),
        rows_view,
        gate,
        up,
        down,
    )
    pairs = call(
        keep_kernel,
        (2,),
        [core_half(4, HALF, 2 * FEAT, True)] + weight_specs + [sums_block],
        sums_block,
        pltpu.HBM((8, HALF, 3 * HID), BF),
        cost(900, 6500),
        (coords,),
        rows_view,
        gate,
        up,
        down,
        swap(sending),
    )
    sums = lax.psum_scatter(pairs.reshape(8 * HALF, 3 * HID), "z", scatter_dimension=0, tiled=True)
    new_rows = slab_rows(jnp.take(held_before, partner), pairs)
    acts = call(
        activation_kernel,
        (1,),
        [whole(HALF, 3 * HID), ANYWHERE],
        whole(BUNDLE, HID),
        shaped(BUNDLE, HID),
        cost(3, 500),
        (coords,),
        sums,
        in_hbm(new_rows),
    )

    own_acts = lax.all_gather(acts, ("z", "core"), tiled=True).reshape(CHUNKS, BUNDLE, HID)
    pieces = exchange(acts.reshape(32, 8, HID), ("y", "x"))
    picked = call(
        pick_kernel,
        (1,),
        [whole(32, 8, HID)],
        whole(32, 8, HID),
        shaped(32, 8, HID),
        cost(1, 520),
        (partner,),
        pieces,
    )
    moved = exchange(picked, ("y", "x")).reshape(BUNDLE, HID)

    terms = call(
        terms_kernel,
        (4,),
        [
            lead_block(4, BUNDLE, HID),
            whole(FEAT, HID),
            whole(FEAT, HID),
            whole(FEAT, HID),
        ],
        pl.BlockSpec((8, 1, CAP, 2 * FEAT), lambda i, coords: (0, i, 0, 0)),
        pltpu.HBM((8, 4, CAP, 2 * FEAT), BF),
        cost(1800, 8000),
        (coords,),
        in_hbm(own_acts),
        gate,
        up,
        down,
    )
    new_acts = lax.all_gather(moved, ("z", "core"), tiled=True).reshape(CHUNKS, BUNDLE, HID)

    plain, weighted = call(
        slots_kernel,
        (1,),
        [whole(8, TOK), whole(8, TOK)],
        (whole(TOK, ROWS), whole(TOK, ROWS)),
        (shaped(TOK, ROWS), shaped(TOK, ROWS)),
        cost(20, 400),
        (held_before,),
        ids,
        probs,
    )
    layer_out, token_grad = local(
        merge_kernel,
        (shaped(TOK, FEAT), shaped(TOK, FEAT)),
        cost(300, 2400),
        plain,
        weighted,
        exchange(terms.reshape(32, CAP, 2 * FEAT), ("y", "x")).reshape(ROWS, 2 * FEAT),
    )

    gate_grad, up_grad, down_grad = local(
        slab_grad_kernel,
        (shaped(FEAT, HID), shaped(FEAT, HID), shaped(FEAT, HID)),
        cost(1800, 8000),
        new_rows.reshape(ROWS, 2 * FEAT),
        new_acts,
    )

    return (layer_out, token_grad, gate_grad[None], up_grad[None], down_grad.T[None])


def solution(mesh):
    fine = Mesh(mesh.devices.reshape(8, 4, 8, 2), ("y", "x", "z", "core"))
    expert, dp = ("y", "x"), ("z", "core")
    slab = P(expert, dp, None)
    down = P(expert, None, dp)
    return jax.shard_map(
        body,
        mesh=fine,
        in_specs=(P(expert, dp), P(expert, dp), P(expert, None), P(expert, None), P(), P(), slab, slab, down),
        out_specs=(P(expert, dp), P(expert, dp), slab, slab, down),
        check_vma=False,
    )
```

time: 339 us -> 255 us (0.75)
  waiting for transfers between devices: 174 us -> 69.4 us
  blocking collectives: 87.8 us -> 113 us
  local copies, waits for them, and re-layouts: 10.5 us -> 4.4 us
    all_gather x1 -> x0, waiting for transfers between devices: 77.7 us -> none  [body(): everyone = lax.all_gather(packed, ('y', 'x'), tiled=True)]
    all_to_all x3 -> x1, waiting for transfers between devices: 52.3 us -> 17.3 us  [exchange(): return lax.all_to_all(value, axes, split_axis=0, concat_axis=0, tiled=True)]
    all_gather x0 -> x1, blocking collectives: none -> 23.5 us  [body(): column = lax.all_gather(packed, 'y', tiled=True)]
    all_to_all x3 -> x1, starting transfers between devices: 18.6 us -> 9.52 us  [exchange(): return lax.all_to_all(value, axes, split_axis=0, concat_axis=0, tiled=True)]
    ppermute x1, starting transfers between devices: 4.73 us -> 12.6 us  [swap(): return lax.ppermute(value, 'core', [(0, 1), (1, 0)])]
    all_gather x1, waiting for transfers between devices: 7.75 us -> 14.5 us  [body(): lax.all_gather(acts, ('z', 'core'), tiled=True).reshape(CHUNKS, BUNDLE, HID)]
    unnamed x30 -> x20, local copies, waits for them, and re-layouts: 9.77 us -> 3.71 us
    reduce_scatter x0 -> x1, waiting for transfers between devices: none -> 4.9 us  [body(): lax.psum_scatter(pairs.reshape(8 * HALF, 3 * HID), 'z', scatter_dimension...]
  transfers between devices with their start and end apart: 7 -> 5, of which waited for: 5 -> 5; matrix products, arithmetic and copies ran while one was open for 0% -> 0% of each run, Pallas kernels for 7% -> 6%
where the time goes in v4:
time: 255 us; the launch traced here: 252 us
  blocking collectives  113 us (44%)
  waiting for transfers between devices  69.4 us (27%)
  Pallas kernels  29.7 us (12%)
  starting transfers between devices  22.2 us (9%)
  between operations  13.9 us (5%)
  local copies, waits for them, and re-layouts  4.4 us (2%)
    all_to_all x4, blocking collectives, exchange(): return lax.all_to_all(value, axes, split_axis=0, concat_axis=0, tiled=True)  89.3 us
    all_gather x1, waiting for transfers between devices, body(): lax.all_gather(moved, ('z', 'core'), tiled=True)  29 us
    all_gather x1, blocking collectives, body(): column = lax.all_gather(packed, 'y', tiled=True)  23.5 us
    pallas_call x8, Pallas kernels, call(): pl.pallas_call(kernel, grid_spec=pltpu.PrefetchScalarGridSpec(num_scalar_...  22.8 us
    all_to_all x1, waiting for transfers between devices, exchange(): return lax.all_to_all(value, axes, split_axis=0, concat_axis=0, tiled=True)  17.3 us
    all_gather x1, waiting for transfers between devices, body(): lax.all_gather(acts, ('z', 'core'), tiled=True).reshape(CHUNKS, BUNDLE, HID)  14.5 us
    ppermute x1, starting transfers between devices, swap(): return lax.ppermute(value, 'core', [(0, 1), (1, 0)])  12.6 us
    all_to_all x1, starting transfers between devices, exchange(): return lax.all_to_all(value, axes, split_axis=0, concat_axis=0, tiled=True)  9.52 us
  transfers between devices with their start and end apart: 5, of which 5 were waited for; matrix products, arithmetic and copies ran while one was open for 0% of the time, Pallas kernels for 6%

profile of v4, /device:TPU:1, one launch (start us, length us, event | category | flops | bytes accessed | tf_op | source)
XLA Modules:
  0.0 252.4 jit_solution(12089795799246917154)
XLA Ops:
  7.2 0.0 reduce-scatter.2.cloned.1.call-start
  7.2 1.1 shard_map.129
  8.3 23.5 %all_gather.9.packed_ref = bf16[512,960]{1,0:T(8,128)(2,1)S(1)} all-gather(bf16[64,960]{1,0:T(8,128)(2,1)S(1)} %shard_map.129), channel_id=1, replica_groups=mesh['y'=8,'x'=4,'z'=8,'core'=2] {'y'}, dimensions={0}, use_global_device_ids=true | all-gather | bytes 1105920 | tf_op jit(solution)/shard_map/all_gather | solution.py:245
  31.8 0.1 pad_add_fusion.coords
  31.8 4.2 %shard_map.130 = bf16[4,320,896]{2,1,0:T(8,128)(2,1)} custom-call(s32[32]{0:T(128)} %after_ref.1, s32[3]{0:T(128)S(1)} %pad_add_fusion.coords, bf16[512,960]{1,0:T(8,128)(2,1)S(1)} %all_gather.9.packed_ref, s32[32]{0:T(128)} %after_ref.1), custom_call_target="tpu_custom_call" | custom-call | flops 600000000 | bytes 3500000 | tf_op jit(solution)/shard_map/pallas_call | solution.py:187
  36.1 23.3 %all_to_all.25 = bf16[4,320,896]{2,1,0:T(8,128)(2,1)S(1)} all-to-all(bf16[4,320,896]{2,1,0:T(8,128)(2,1)} %shard_map.130), channel_id=1, replica_groups=mesh['y'=8,'x'=4,'z'=8,'core'=2] {'x'}, dimensions={0} | all-to-all | bytes 4587520 | tf_op jit(solution)/shard_map/all_to_all | solution.py:228
  59.4 2.1 shard_map.131
  61.4 12.6 %collective-permute-start = (bf16[8,80,1536]{2,1,0:T(8,128)(2,1)S(1)}, bf16[8,80,1536]{2,1,0:T(8,128)(2,1)S(1)}, u32[]{:S(2)}, u32[]{:S(2)}) collective-permute-start(bf16[8,80,1536]{2,1,0:T(8,128)(2,1)S(1)} %shard_map.131), channel_id=1, source_target_pairs={{0,1},{1,0},{2,3},{3,2},{4,5},{5,4},{6,7},{7,6},{8,9},{9,8},{10,11... | collective-permute-start | bytes 5898248 | tf_op jit(solution)/shard_map/ppermute | solution.py:224
  74.0 3.6 %collective-permute-done.got_ref = bf16[8,80,1536]{2,1,0:T(8,128)(2,1)S(1)} collective-permute-done((bf16[8,80,1536]{2,1,0:T(8,128)(2,1)S(1)}, bf16[8,80,1536]{2,1,0:T(8,128)(2,1)S(1)}, u32[]{:S(2)}, u32[]{:S(2)}) %collective-permute-start) | collective-permute-done | bytes 1966112 | tf_op jit(solution)/shard_map/ppermute | solution.py:224
  77.6 3.0 %shard_map.132.after_ref = bf16[8,80,1536]{2,1,0:T(8,128)(2,1)} custom-call(s32[3]{0:T(128)S(1)} %pad_add_fusion.coords, bf16[8,2,80,896]{3,2,1,0:T(8,128)(2,1)S(1)} %bitcast.25, bf16[448,512]{1,0:T(8,128)(2,1)S(1)} %bitcast.28, bf16[448,512]{1,0:T(8,128)(2,1)S(1)} %bitcast.31, bf16[448,512]{1,0:T(8,128)(2,1)S(1)} %bitcast.34, ...), custom_call_target="tpu_custom_call" | custom-call | flops 900000000 | bytes 6500000 | tf_op jit(solution)/shard_map/pallas_call | solution.py:187
  80.6 0.0 all-gather.3.cloned.1.call-start
  80.7 0.5 copy-done
  81.2 0.7 gather_fusion
  81.9 4.1 %shard_map.133 = bf16[4,320,896]{2,1,0:T(8,128)(2,1)} custom-call(s32[32]{0:T(128)S(1)} %and_select_fusion.held, s32[3]{0:T(128)S(1)} %pad_add_fusion.coords, bf16[512,960]{1,0:T(8,128)(2,1)S(1)} %all_gather.9.packed_ref, bf16[8,80,1536]{2,1,0:T(8,128)(2,1)} %shard_map.132.after_ref), custom_call_target="tpu_custom_call" | custom-call | flops 600000000 | bytes 3500000 | tf_op jit(solution)/shard_map/pallas_call | solution.py:187
  86.0 32.4 %all_to_all.26.after_ref = bf16[4,320,896]{2,1,0:T(8,128)(2,1)} all-to-all(bf16[4,320,896]{2,1,0:T(8,128)(2,1)} %shard_map.133), channel_id=1, replica_groups=mesh['y'=8,'x'=4,'z'=8,'core'=2] {'x'}, dimensions={0} | all-to-all | bytes 4587520 | tf_op jit(solution)/shard_map/all_to_all | solution.py:228
  118.5 4.9 %reduce-scatter.2.cloned.1.call-done.sums_ref = bf16[80,1536]{1,0:T(8,128)(2,1)} async-done(((bf16[640,1536]{1,0:T(8,128)(2,1)}), bf16[80,1536]{1,0:T(8,128)(2,1)}) %reduce-scatter.2.cloned.1.call-update) | async-done | bytes 245776 | tf_op jit(solution)/shard_map/reduce_scatter | solution.py:292
  123.4 0.9 copy-done.5
  124.3 1.3 shard_map.134
  125.7 0.0 all-gather.5.cloned.1.call-start
  125.7 19.4 %all_to_all.27.pieces_ref = bf16[32,8,512]{2,1,0:T(8,128)(2,1)S(1)} all-to-all(bf16[32,8,512]{2,1,0:T(8,128)(2,1)} %bitcast.16), channel_id=1, replica_groups=mesh['y'=8,'x'=4,'z'=8,'core'=2] {'y','x'}, dimensions={0} | all-to-all | bytes 524288 | tf_op jit(solution)/shard_map/all_to_all | solution.py:228
  145.1 0.6 shard_map.137
  145.7 14.2 %all_to_all.28 = bf16[32,8,512]{2,1,0:T(8,128)(2,1)} all-to-all(bf16[32,8,512]{2,1,0:T(8,128)(2,1)S(1)} %shard_map.137), channel_id=1, replica_groups=mesh['y'=8,'x'=4,'z'=8,'core'=2] {'y','x'}, dimensions={0} | all-to-all | bytes 524288 | tf_op jit(solution)/shard_map/all_to_all | solution.py:228
  159.9 0.0 all-gather.5.cloned.1.call-update
  159.9 14.5 %all-gather.3.cloned.1.call-done = bf16[4096,512]{1,0:T(8,128)(2,1)} async-done(((bf16[256,512]{1,0:T(8,128)(2,1)}), bf16[4096,512]{1,0:T(8,128)(2,1)}) %all-gather.3.cloned.1.call-update) | async-done | bytes 4194320 | tf_op jit(solution)/shard_map/all_gather | solution.py:306
  174.4 6.5 %shard_map.135 = bf16[8,4,40,896]{3,2,1,0:T(8,128)(2,1)} custom-call(s32[3]{0:T(128)S(1)} %pad_add_fusion.coords, bf16[16,256,512]{2,1,0:T(8,128)(2,1)} %bitcast.43, bf16[448,512]{1,0:T(8,128)(2,1)S(1)} %bitcast.29, bf16[448,512]{1,0:T(8,128)(2,1)S(1)} %bitcast.32, bf16[448,512]{1,0:T(8,128)(2,1)S(1)} %bitcast.35), custom_call_target="tpu_custom_call" | custom-call | flops 1800000000 | bytes 8000000 | tf_op jit(solution)/shard_map/pallas_call | solution.py:187
  180.9 9.5 %all-to-all-start.2 = ((bf16[32,40,896]{2,1,0:T(8,128)(2,1)}), bf16[32,40,896]{2,1,0:T(8,128)(2,1)}, u32[]{:S(2)}, u32[]{:S(2)}) async-start(bf16[32,40,896]{2,1,0:T(8,128)(2,1)} %bitcast.42), calls=%async_computation.3 | async-start | bytes 4587520 | tf_op jit(solution)/shard_map/all_to_all | solution.py:228
  190.5 1.1 shard_map.128
  191.5 29.0 %all-gather.5.cloned.1.call-done = bf16[4096,512]{1,0:T(8,128)(2,1)} async-done(((bf16[256,512]{1,0:T(8,128)(2,1)}), bf16[4096,512]{1,0:T(8,128)(2,1)}) %all-gather.5.cloned.1.call-update) | async-done | bytes 4194320 | tf_op jit(solution)/shard_map/all_gather | solution.py:338
  220.6 2.2 copy-done.9
  222.8 2.8 %shard_map.138 = (bf16[448,512]{1,0:T(8,128)(2,1)}, bf16[448,512]{1,0:T(8,128)(2,1)}, bf16[448,512]{1,0:T(8,128)(2,1)}) custom-call(bf16[1280,896]{1,0:T(8,128)(2,1)S(1)} %bitcast.26, bf16[16,256,512]{2,1,0:T(8,128)(2,1)S(1)} %bitcast.40), custom_call_target="tpu_custom_call" | custom-call | flops 1800000000 | bytes 8000000 | tf_op jit(solution)/shard_map/pallas_call | solution.py:199
  225.5 17.3 %all-to-all-done.2 = bf16[32,40,896]{2,1,0:T(8,128)(2,1)} async-done(((bf16[32,40,896]{2,1,0:T(8,128)(2,1)}), bf16[32,40,896]{2,1,0:T(8,128)(2,1)}, u32[]{:S(2)}, u32[]{:S(2)}) %all-to-all-start.2) | async-done | bytes 2293792 | tf_op jit(solution)/shard_map/all_to_all | solution.py:228
  242.9 3.0 %shard_map.136 = (bf16[64,448]{1,0:T(8,128)(2,1)}, bf16[64,448]{1,0:T(8,128)(2,1)}) custom-call(bf16[64,1280]{1,0:T(8,128)(2,1)S(1)} %get-tuple-element.12.plain_ref, bf16[64,1280]{1,0:T(8,128)(2,1)S(1)} %get-tuple-element.13.weighted_ref, bf16[1280,896]{1,0:T(8,128)(2,1)} %bitcast.14.rows_ref), custom_call_target="tpu_custom_call" | custom-call | flops 300000000 | bytes 2400000 | tf_op jit(solution)/shard_map/pallas_call | solution.py:199
  (22 shorter events, 0.1 us)
Async XLA Ops:
  7.2 116.2 %reduce-scatter.2.cloned.1.call-start = ((), (), s32[]{:S(2)}) async-start(), calls=%async_computation.6 | async-start | bytes 2211840 | tf_op jit(solution)/shard_map/reduce_scatter | solution.py:292
  36.0 23.3 %copy-start.2 = (bf16[1,448,512]{2,1,0:T(8,128)(2,1)S(1)}, bf16[1,448,512]{2,1,0:T(8,128)(2,1)}, u32[]{:S(2)}) copy-start(bf16[1,448,512]{2,1,0:T(8,128)(2,1)} %param.15) | copy-start | bytes 1376260
  36.0 23.3 %copy-start.3 = (bf16[1,448,512]{2,1,0:T(8,128)(2,1)S(1)}, bf16[1,448,512]{2,1,0:T(8,128)(2,1)}, u32[]{:S(2)}) copy-start(bf16[1,448,512]{2,1,0:T(8,128)(2,1)} %param.16) | copy-start | bytes 1376260
  36.0 23.3 %copy-start.4 = (bf16[1,512,448]{1,2,0:T(8,128)(2,1)S(1)}, bf16[1,512,448]{1,2,0:T(8,128)(2,1)}, u32[]{:S(2)}) copy-start(bf16[1,512,448]{1,2,0:T(8,128)(2,1)} %param.17) | copy-start | bytes 1376260
  61.4 19.2 %copy-start.8 = (s32[32]{0:T(128)S(1)}, s32[32]{0:T(128)}, u32[]{:S(2)}) copy-start(s32[32]{0:T(128)} %partner.1) | copy-start | bytes 388
  61.4 16.1 %collective-permute-start = (bf16[8,80,1536]{2,1,0:T(8,128)(2,1)S(1)}, bf16[8,80,1536]{2,1,0:T(8,128)(2,1)S(1)}, u32[]{:S(2)}, u32[]{:S(2)}) collective-permute-start(bf16[8,80,1536]{2,1,0:T(8,128)(2,1)S(1)} %shard_map.131), channel_id=1, source_target_pairs={{0,1},{1,0},{2,3},{3,2},{4,5},{5,4},{6,7},{7,6},{8,9},{9,8},{10,11... | collective-permute-start | bytes 5898248 | tf_op jit(solution)/shard_map/ppermute | solution.py:224
  80.6 0.7 copy-start
  80.6 93.8 %all-gather.3.cloned.1.call-start = ((), (), s32[]{:S(2)}) async-start(), calls=%async_computation.7 | async-start | bytes 4456448 | tf_op jit(solution)/shard_map/all_gather | solution.py:306
  123.4 0.9 copy-start.5
  125.7 94.9 %all-gather.5.cloned.1.call-start = ((), (), s32[]{:S(2)}) async-start(), calls=%async_computation.8 | async-start | bytes 4456448 | tf_op jit(solution)/shard_map/all_gather | solution.py:338
  180.9 9.5 %copy-start.6 = (s32[64,8]{0,1:T(8,128)S(1)}, s32[64,8]{0,1:T(8,128)}, u32[]{:S(2)}) copy-start(s32[64,8]{0,1:T(8,128)} %param.11) | copy-start | bytes 6148
  180.9 9.5 %copy-start.7 = (bf16[64,8]{0,1:T(8,128)(2,1)S(1)}, bf16[64,8]{0,1:T(8,128)(2,1)}, u32[]{:S(2)}) copy-start(bf16[64,8]{0,1:T(8,128)(2,1)} %param.12) | copy-start | bytes 3076
  180.9 39.7 %copy-start.1 = (bf16[4,320,896]{2,1,0:T(8,128)(2,1)S(1)}, bf16[4,320,896]{2,1,0:T(8,128)(2,1)}, u32[]{:S(2)}) copy-start(bf16[4,320,896]{2,1,0:T(8,128)(2,1)} %all_to_all.26.after_ref) | copy-start | bytes 6881284
  180.9 62.0 %all-to-all-start.2 = ((bf16[32,40,896]{2,1,0:T(8,128)(2,1)}), bf16[32,40,896]{2,1,0:T(8,128)(2,1)}, u32[]{:S(2)}, u32[]{:S(2)}) async-start(bf16[32,40,896]{2,1,0:T(8,128)(2,1)} %bitcast.42), calls=%async_computation.3 | async-start | bytes 4587520 | tf_op jit(solution)/shard_map/all_to_all | solution.py:228
  220.6 2.2 copy-start.9
Sparse Core Ops, SparseCore 0:
  80.7 42.5 reduce-scatter.1
  126.3 48.1 all-gather.2
  176.8 43.7 all-gather.4

commit v5 on v4

--- a/solution.py
+++ b/solution.py
@@ -86,7 +86,7 @@
     slab = lax.broadcasted_iota(jnp.int32, (32, TOK), 0)
     expert = jnp.zeros((32, TOK), jnp.int32)
     for i in range(32):
-        expert = jnp.where(slab == i, held[i] >> 1, expert)
+        expert = jnp.where(slab == i, held[i % 8 * 4 + i // 8] >> 1, expert)
     weights = weights_of(expert, ids_ref, probs_ref)
     return weights, slot_places(weights)
 
@@ -109,35 +109,31 @@
     for i in range(4):
         hit = one_hot(place[i : i + 1], HALF)
         rows = dot(as_matrix(hit), packed_ref[:, : 2 * FEAT])
-        out_ref[i] = (rows * jnp.where(cot_lane, slot_weights(hit, weights[i : i + 1]), 1.0)).astype(BF)
-
-
-def products(rows_ref, gate_ref, up_ref, down_ref):
+        out_ref[i, ...] = (rows * jnp.where(cot_lane, slot_weights(hit, weights[i : i + 1]), 1.0)).astype(BF).reshape(out_ref.shape[1:])
+
+
+def products_kernel(coords, rows_ref, gate_ref, up_ref, down_ref, out_ref):
     count = rows_ref.shape[0]
     rows = rows_ref[...].reshape(count * HALF, 2 * FEAT)
     tok, scaled = rows[:, :FEAT], rows[:, FEAT:]
     three = dot(tok, gate_ref[...]), dot(tok, up_ref[...]), dot(scaled, down_ref[...])
-    return [(slice(i * HID, (i + 1) * HID), part.reshape(count, HALF, HID)) for i, part in enumerate(three)]
-
-
-def send_kernel(coords, rows_ref, gate_ref, up_ref, down_ref, out_ref):
-    for lanes, part in products(rows_ref, gate_ref, up_ref, down_ref):
-        out_ref[:, :, lanes] = part.astype(BF)
-
-
-def keep_kernel(coords, rows_ref, gate_ref, up_ref, down_ref, got_ref, out_ref):
-    for lanes, part in products(rows_ref, gate_ref, up_ref, down_ref):
-        out_ref[:, :, lanes] = (part + got_ref[:, :, lanes].astype(F32)).astype(BF)
-
-
-def activation_kernel(coords, sums_ref, after_ref, out_ref):
+    for i, part in enumerate(three):
+        out_ref[:, :, i * HID : (i + 1) * HID] = part.astype(BF).reshape(count, HALF, HID)
+
+
+def add_kernel(coords, own_ref, got_ref, out_ref):
+    out_ref[...] = (own_ref[...].astype(F32) + got_ref[...].astype(F32)).astype(BF)
+
+
+def activation_kernel(coords, sums_ref, after_ref, three_ref, out_ref):
     sums = sums_ref[...].astype(F32)
     gate, up, grad = sums[:, :HID], sums[:, HID : 2 * HID], sums[:, 2 * HID :]
     sig = jax.nn.sigmoid(gate)
     activated = gate * sig
-    out_ref[0:HALF] = (activated * up).astype(BF)
-    out_ref[HALF : 2 * HALF] = (grad * up * sig * (1.0 + gate * (1.0 - sig))).astype(BF)
-    out_ref[2 * HALF : 3 * HALF] = (grad * activated).astype(BF)
+    parts = activated * up, grad * up * sig * (1.0 + gate * (1.0 - sig)), grad * activated
+    for i, part in enumerate(parts):
+        three_ref[i * HALF : (i + 1) * HALF] = part.astype(BF)
+        out_ref[i * HALF : (i + 1) * HALF] = part.astype(BF)
     out_ref[3 * HALF :] = jnp.zeros((BUNDLE - 3 * HALF, HID), BF)
 
 
@@ -154,9 +150,7 @@
 def terms_kernel(coords, acts_ref, gate_ref, up_ref, down_ref, out_ref):
     out = dot_last(bundle_part(acts_ref, 0), down_ref[...])
     back = dot_last(bundle_part(acts_ref, 1), gate_ref[...]) + dot_last(bundle_part(acts_ref, 2), up_ref[...])
-    both = jnp.concatenate([out, back], axis=1)
-    for i in range(out_ref.shape[0]):
-        out_ref[i, 0] = both[i * CAP : (i + 1) * CAP].astype(BF)
+    out_ref[...] = jnp.concatenate([out, back], axis=1).astype(BF)
 
 
 def merge_kernel(plain_ref, weighted_ref, rows_ref, out_ref, back_ref):
@@ -244,66 +238,66 @@
     )
     column = lax.all_gather(packed, "y", tiled=True)
 
-    def slab_rows(held, after):
-        sent = call(
+    def slab_rows(held, after, block, shape):
+        return call(
             rows_kernel,
             (4,),
             [lead_block(PAIR, PACK), ANYWHERE],
-            pl.BlockSpec((4, HALF, 2 * FEAT), lambda i, held, coords: (0, i, 0)),
-            pltpu.HBM((4, 4 * HALF, 2 * FEAT), BF),
+            block,
+            pltpu.HBM(shape, BF),
             cost(600, 3500),
             (held, coords),
             column,
             in_hbm(after),
         )
-        return exchange(sent, "x")
-
-    own_rows = slab_rows(held_before, held_before)
-    rows_view = own_rows.reshape(8, 2, HALF, 2 * FEAT)
-    weight_specs = [whole(FEAT, HID), whole(FEAT, HID), whole(FEAT, HID)]
-    sums_block = lead_block(4, HALF, 3 * HID)
-    sending = call(
-        send_kernel,
-        (2,),
-        [core_half(4, HALF, 2 * FEAT, False)] + weight_specs,
-        sums_block,
-        shaped(8, HALF, 3 * HID),
-        cost(900, 4500),
+
+    in_pairs = pl.BlockSpec((4, 1, HALF, 2 * FEAT), lambda i, *scalars: (0, i, 0, 0))
+    sent = slab_rows(held_before, held_before, in_pairs, (4, 4, HALF, 2 * FEAT))
+    rows_view = exchange(sent.reshape(4, 4 * HALF, 2 * FEAT), "x").reshape(8, 2, HALF, 2 * FEAT)
+
+    def products(mine):
+        return call(
+            products_kernel,
+            (2,),
+            [core_half(4, HALF, 2 * FEAT, mine)] + [whole(FEAT, HID)] * 3,
+            lead_block(4, HALF, 3 * HID),
+            shaped(8, HALF, 3 * HID),
+            cost(900, 4500),
+            (coords,),
+            rows_view,
+            gate,
+            up,
+            down,
+        )
+
+    got = swap(products(False))
+    pairs = call(
+        add_kernel,
+        (4,),
+        [lead_block(2, HALF, 3 * HID)] * 2,
+        lead_block(2, HALF, 3 * HID),
+        pltpu.HBM((8, HALF, 3 * HID), BF),
+        cost(1, 6000),
         (coords,),
-        rows_view,
-        gate,
-        up,
-        down,
-    )
-    pairs = call(
-        keep_kernel,
-        (2,),
-        [core_half(4, HALF, 2 * FEAT, True)] + weight_specs + [sums_block],
-        sums_block,
-        pltpu.HBM((8, HALF, 3 * HID), BF),
-        cost(900, 6500),
-        (coords,),
-        rows_view,
-        gate,
-        up,
-        down,
-        swap(sending),
+        products(True),
+        got,
     )
     sums = lax.psum_scatter(pairs.reshape(8 * HALF, 3 * HID), "z", scatter_dimension=0, tiled=True)
-    new_rows = slab_rows(jnp.take(held_before, partner), pairs)
-    acts = call(
+    new_sent = slab_rows(jnp.take(held_before, partner), pairs, in_pairs, (4, 4, HALF, 2 * FEAT))
+    new_rows = exchange(new_sent.reshape(4, 4 * HALF, 2 * FEAT), "x")
+    three, acts = call(
         activation_kernel,
         (1,),
         [whole(HALF, 3 * HID), ANYWHERE],
-        whole(BUNDLE, HID),
-        shaped(BUNDLE, HID),
+        (whole(3 * HALF, HID), whole(BUNDLE, HID)),
+        (shaped(3 * HALF, HID), shaped(BUNDLE, HID)),
         cost(3, 500),
         (coords,),
-        sums,
+        in_hbm(sums),
         in_hbm(new_rows),
     )
 
-    own_acts = lax.all_gather(acts, ("z", "core"), tiled=True).reshape(CHUNKS, BUNDLE, HID)
+    own_acts = lax.all_gather(three, ("z", "core"), tiled=True).reshape(CHUNKS, 3 * HALF, HID)
     pieces = exchange(acts.reshape(32, 8, HID), ("y", "x"))
     picked = call(
         pick_kernel,
@@ -319,15 +313,15 @@
 
     terms = call(
         terms_kernel,
-        (4,),
+        (2,),
         [
-            lead_block(4, BUNDLE, HID),
+            lead_block(8, 3 * HALF, HID),
             whole(FEAT, HID),
             whole(FEAT, HID),
             whole(FEAT, HID),
         ],
-        pl.BlockSpec((8, 1, CAP, 2 * FEAT), lambda i, coords: (0, i, 0, 0)),
-        pltpu.HBM((8, 4, CAP, 2 * FEAT), BF),
+        lead_block(ROWS // 2, 2 * FEAT),
+        pltpu.HBM((ROWS, 2 * FEAT), BF),
         cost(1800, 8000),
         (coords,),
         in_hbm(own_acts),
@@ -335,7 +329,7 @@
         up,
         down,
     )
-    new_acts = lax.all_gather(moved, ("z", "core"), tiled=True).reshape(CHUNKS, BUNDLE, HID)
+    new_acts = lax.all_gather(moved[: 3 * HALF], ("z", "core"), tiled=True).reshape(CHUNKS, 3 * HALF, HID)
 
     plain, weighted = call(
         slots_kernel,
@@ -354,15 +348,15 @@
         cost(300, 2400),
         plain,
         weighted,
-        exchange(terms.reshape(32, CAP, 2 * FEAT), ("y", "x")).reshape(ROWS, 2 * FEAT),
+        exchange(terms.reshape(32, CAP, 2 * FEAT), ("x", "y")).reshape(ROWS, 2 * FEAT),
     )
 
     gate_grad, up_grad, down_grad = local(
         slab_grad_kernel,
         (shaped(FEAT, HID), shaped(FEAT, HID), shaped(FEAT, HID)),
         cost(1800, 8000),
-        new_rows.reshape(ROWS, 2 * FEAT),
-        new_acts,
+        in_hbm(new_rows.reshape(ROWS, 2 * FEAT)),
+        in_hbm(new_acts),
     )
 
     return (layer_out, token_grad, gate_grad[None], up_grad[None], down_grad.T[None])

time: 255 us -> 251 us (0.984)
  Pallas kernels: 29.7 us -> 32.5 us
    unnamed x20 -> x14, local copies, waits for them, and re-layouts: 3.71 us -> 0.57 us
    pallas_call x8 -> x9, Pallas kernels: 22.8 us -> 24.6 us  [call(): pl.pallas_call(kernel, grid_spec=pltpu.PrefetchScalarGridSpec(num_scalar_...]
  transfers between devices with their start and end apart: 5 -> 5, of which waited for: 5 -> 5; matrix products, arithmetic and copies ran while one was open for 0% -> 1% of each run, Pallas kernels for 6% -> 8%
where the time goes in v5:
time: 251 us; the launch traced here: 250 us
  blocking collectives  112 us (45%)
  waiting for transfers between devices  67 us (27%)
  Pallas kernels  32.5 us (13%)
  starting transfers between devices  22.1 us (9%)
  between operations  13.9 us (6%)
    all_to_all x4, blocking collectives, exchange(): return lax.all_to_all(value, axes, split_axis=0, concat_axis=0, tiled=True)  88.7 us
    all_gather x1, waiting for transfers between devices, body(): lax.all_gather(moved[:3 * HALF], ('z', 'core'), tiled=True)  30.2 us
    pallas_call x9, Pallas kernels, call(): pl.pallas_call(kernel, grid_spec=pltpu.PrefetchScalarGridSpec(num_scalar_...  24.6 us
    all_gather x1, blocking collectives, body(): column = lax.all_gather(packed, 'y', tiled=True)  23.5 us
    all_to_all x1, waiting for transfers between devices, exchange(): return lax.all_to_all(value, axes, split_axis=0, concat_axis=0, tiled=True)  16.2 us
    all_gather x1, waiting for transfers between devices, body(): lax.all_gather(three, ('z', 'core'), tiled=True)  14.1 us
    ppermute x1, starting transfers between devices, swap(): return lax.ppermute(value, 'core', [(0, 1), (1, 0)])  12.6 us
    all_to_all x1, starting transfers between devices, exchange(): return lax.all_to_all(value, axes, split_axis=0, concat_axis=0, tiled=True)  9.39 us
  transfers between devices with their start and end apart: 5, of which 5 were waited for; matrix products, arithmetic and copies ran while one was open for 1% of the time, Pallas kernels for 8%

profile of v5, /device:TPU:1, one launch (start us, length us, event | category | flops | bytes accessed | tf_op | source)
XLA Modules:
  0.0 249.7 jit_solution(5874190449889441600)
XLA Ops:
  7.2 0.0 reduce-scatter.2.cloned.1.call-start
  7.2 1.1 shard_map.129
  8.3 23.5 %all_gather.9.packed_ref = bf16[512,960]{1,0:T(8,128)(2,1)S(1)} all-gather(bf16[64,960]{1,0:T(8,128)(2,1)S(1)} %shard_map.129), channel_id=1, replica_groups=mesh['y'=8,'x'=4,'z'=8,'core'=2] {'y'}, dimensions={0}, use_global_device_ids=true | all-gather | bytes 1105920 | tf_op jit(solution)/shard_map/all_gather | solution.py:239
  31.8 0.1 pad_add_fusion.coords
  31.8 4.2 %shard_map.130 = bf16[4,4,80,896]{3,2,1,0:T(8,128)(2,1)} custom-call(s32[32]{0:T(128)} %after_ref.1, s32[3]{0:T(128)S(1)} %pad_add_fusion.coords, bf16[512,960]{1,0:T(8,128)(2,1)S(1)} %all_gather.9.packed_ref, s32[32]{0:T(128)} %after_ref.1), custom_call_target="tpu_custom_call" | custom-call | flops 600000000 | bytes 3500000 | tf_op jit(solution)/shard_map/pallas_call | solution.py:181
  36.1 23.3 %all_to_all.25 = bf16[4,320,896]{2,1,0:T(8,128)(2,1)S(1)} all-to-all(bf16[4,320,896]{2,1,0:T(8,128)(2,1)} %bitcast.48), channel_id=1, replica_groups=mesh['y'=8,'x'=4,'z'=8,'core'=2] {'x'}, dimensions={0} | all-to-all | bytes 4587520 | tf_op jit(solution)/shard_map/all_to_all | solution.py:222
  59.4 2.1 shard_map.132
  61.4 12.6 %collective-permute-start = (bf16[8,80,1536]{2,1,0:T(8,128)(2,1)S(1)}, bf16[8,80,1536]{2,1,0:T(8,128)(2,1)S(1)}, u32[]{:S(2)}, u32[]{:S(2)}) collective-permute-start(bf16[8,80,1536]{2,1,0:T(8,128)(2,1)S(1)} %shard_map.132), channel_id=1, source_target_pairs={{0,1},{1,0},{2,3},{3,2},{4,5},{5,4},{6,7},{7,6},{8,9},{9,8},{10,11... | collective-permute-start | bytes 5898248 | tf_op jit(solution)/shard_map/ppermute | solution.py:218
  74.0 2.1 shard_map.131.own_ref
  76.1 1.5 collective-permute-done.got_ref
  77.6 2.5 %shard_map.133.after_ref = bf16[8,80,1536]{2,1,0:T(8,128)(2,1)} custom-call(s32[3]{0:T(128)S(1)} %pad_add_fusion.coords, bf16[8,80,1536]{2,1,0:T(8,128)(2,1)S(1)} %shard_map.131.own_ref, bf16[8,80,1536]{2,1,0:T(8,128)(2,1)S(1)} %collective-permute-done.got_ref), custom_call_target="tpu_custom_call" | custom-call | flops 1000000 | bytes 6000000 | tf_op jit(solution)/shard_map/pallas_call | solution.py:181
  80.1 0.0 reduce-scatter.2.cloned.1.call-update
  80.1 0.0 all-gather.3.cloned.1.call-start
  80.2 0.5 copy-done
  80.8 0.7 gather_fusion
  81.5 4.1 %shard_map.134 = bf16[4,4,80,896]{3,2,1,0:T(8,128)(2,1)} custom-call(s32[32]{0:T(128)S(1)} %and_select_fusion.held, s32[3]{0:T(128)S(1)} %pad_add_fusion.coords, bf16[512,960]{1,0:T(8,128)(2,1)S(1)} %all_gather.9.packed_ref, bf16[8,80,1536]{2,1,0:T(8,128)(2,1)} %shard_map.133.after_ref), custom_call_target="tpu_custom_call" | custom-call | flops 600000000 | bytes 3500000 | tf_op jit(solution)/shard_map/pallas_call | solution.py:181
  85.6 32.4 %all_to_all.26.after_ref = bf16[4,320,896]{2,1,0:T(8,128)(2,1)} all-to-all(bf16[4,320,896]{2,1,0:T(8,128)(2,1)} %bitcast.45), channel_id=1, replica_groups=mesh['y'=8,'x'=4,'z'=8,'core'=2] {'x'}, dimensions={0} | all-to-all | bytes 4587520 | tf_op jit(solution)/shard_map/all_to_all | solution.py:222
  118.0 4.9 %reduce-scatter.2.cloned.1.call-done.sums_ref = bf16[80,1536]{1,0:T(8,128)(2,1)} async-done(((bf16[640,1536]{1,0:T(8,128)(2,1)}), bf16[80,1536]{1,0:T(8,128)(2,1)}) %reduce-scatter.2.cloned.1.call-update) | async-done | bytes 245776 | tf_op jit(solution)/shard_map/reduce_scatter | solution.py:285
  122.9 2.3 shard_map.135
  125.2 0.0 all-gather.5.cloned.1.call-start
  125.3 19.2 %all_to_all.27.pieces_ref = bf16[32,8,512]{2,1,0:T(8,128)(2,1)S(1)} all-to-all(bf16[32,8,512]{2,1,0:T(8,128)(2,1)S(1)} %bitcast.39), channel_id=1, replica_groups=mesh['y'=8,'x'=4,'z'=8,'core'=2] {'y','x'}, dimensions={0} | all-to-all | bytes 524288 | tf_op jit(solution)/shard_map/all_to_all | solution.py:222
  144.5 0.6 shard_map.138
  145.1 13.8 %all_to_all.28 = bf16[32,8,512]{2,1,0:T(8,128)(2,1)S(1)} all-to-all(bf16[32,8,512]{2,1,0:T(8,128)(2,1)S(1)} %shard_map.138), channel_id=1, replica_groups=mesh['y'=8,'x'=4,'z'=8,'core'=2] {'y','x'}, dimensions={0} | all-to-all | bytes 524288 | tf_op jit(solution)/shard_map/all_to_all | solution.py:222
  158.9 0.7 slice_bitcast_fusion
  159.6 14.1 %all-gather.3.cloned.1.call-done = bf16[3840,512]{1,0:T(8,128)(2,1)} async-done(((bf16[240,512]{1,0:T(8,128)(2,1)}), bf16[3840,512]{1,0:T(8,128)(2,1)}) %all-gather.3.cloned.1.call-update) | async-done | bytes 3932176 | tf_op jit(solution)/shard_map/all_gather | solution.py:300
  173.7 5.7 %shard_map.136 = bf16[1280,896]{1,0:T(8,128)(2,1)} custom-call(s32[3]{0:T(128)S(1)} %pad_add_fusion.coords, bf16[16,240,512]{2,1,0:T(8,128)(2,1)} %bitcast.49, bf16[448,512]{1,0:T(8,128)(2,1)S(1)} %bitcast.32, bf16[448,512]{1,0:T(8,128)(2,1)S(1)} %bitcast.35, bf16[448,512]{1,0:T(8,128)(2,1)S(1)} %bitcast.38), custom_call_target="tpu_custom_call" | custom-call | flops 1800000000 | bytes 8000000 | tf_op jit(solution)/shard_map/pallas_call | solution.py:181
  179.4 9.4 %all-to-all-start.2 = ((bf16[32,40,896]{2,1,0:T(8,128)(2,1)}), bf16[32,40,896]{2,1,0:T(8,128)(2,1)S(1)}, u32[]{:S(2)}, u32[]{:S(2)}) async-start(bf16[32,40,896]{2,1,0:T(8,128)(2,1)} %bitcast.47), calls=%async_computation.3 | async-start | bytes 4587520 | tf_op jit(solution)/shard_map/all_to_all | solution.py:222
  188.8 1.1 shard_map.128
  189.9 30.2 %all-gather.5.cloned.1.call-done = bf16[3840,512]{1,0:T(8,128)(2,1)} async-done(((bf16[240,512]{1,0:T(8,128)(2,1)}), bf16[3840,512]{1,0:T(8,128)(2,1)}) %all-gather.5.cloned.1.call-update) | async-done | bytes 3932176 | tf_op jit(solution)/shard_map/all_gather | solution.py:332
  220.1 5.5 %shard_map.139 = (bf16[448,512]{1,0:T(8,128)(2,1)}, bf16[448,512]{1,0:T(8,128)(2,1)}, bf16[448,512]{1,0:T(8,128)(2,1)}) custom-call(bf16[1280,896]{1,0:T(8,128)(2,1)} %bitcast.46, bf16[16,240,512]{2,1,0:T(8,128)(2,1)} %bitcast.50), custom_call_target="tpu_custom_call" | custom-call | flops 1800000000 | bytes 8000000 | tf_op jit(solution)/shard_map/pallas_call | solution.py:193
  225.6 16.2 %all-to-all-done.2 = bf16[32,40,896]{2,1,0:T(8,128)(2,1)S(1)} async-done(((bf16[32,40,896]{2,1,0:T(8,128)(2,1)}), bf16[32,40,896]{2,1,0:T(8,128)(2,1)S(1)}, u32[]{:S(2)}, u32[]{:S(2)}) %all-to-all-start.2) | async-done | bytes 2293792 | tf_op jit(solution)/shard_map/all_to_all | solution.py:222
  241.8 1.3 shard_map.137
  (18 shorter events, 0.1 us)
Async XLA Ops:
  7.2 115.7 %reduce-scatter.2.cloned.1.call-start = ((), (), s32[]{:S(2)}) async-start(), calls=%async_computation.6 | async-start | bytes 2211840 | tf_op jit(solution)/shard_map/reduce_scatter | solution.py:285
  36.0 23.3 %copy-start.1 = (bf16[1,448,512]{2,1,0:T(8,128)(2,1)S(1)}, bf16[1,448,512]{2,1,0:T(8,128)(2,1)}, u32[]{:S(2)}) copy-start(bf16[1,448,512]{2,1,0:T(8,128)(2,1)} %param.15) | copy-start | bytes 1376260
  36.1 23.3 %copy-start.2 = (bf16[1,448,512]{2,1,0:T(8,128)(2,1)S(1)}, bf16[1,448,512]{2,1,0:T(8,128)(2,1)}, u32[]{:S(2)}) copy-start(bf16[1,448,512]{2,1,0:T(8,128)(2,1)} %param.16) | copy-start | bytes 1376260
  36.1 23.3 %copy-start.3 = (bf16[1,512,448]{1,2,0:T(8,128)(2,1)S(1)}, bf16[1,512,448]{1,2,0:T(8,128)(2,1)}, u32[]{:S(2)}) copy-start(bf16[1,512,448]{1,2,0:T(8,128)(2,1)} %param.17) | copy-start | bytes 1376260
  61.4 16.1 %collective-permute-start = (bf16[8,80,1536]{2,1,0:T(8,128)(2,1)S(1)}, bf16[8,80,1536]{2,1,0:T(8,128)(2,1)S(1)}, u32[]{:S(2)}, u32[]{:S(2)}) collective-permute-start(bf16[8,80,1536]{2,1,0:T(8,128)(2,1)S(1)} %shard_map.132), channel_id=1, source_target_pairs={{0,1},{1,0},{2,3},{3,2},{4,5},{5,4},{6,7},{7,6},{8,9},{9,8},{10,11... | collective-permute-start | bytes 5898248 | tf_op jit(solution)/shard_map/ppermute | solution.py:218
  76.1 4.1 %copy-start.6 = (s32[32]{0:T(128)S(1)}, s32[32]{0:T(128)}, u32[]{:S(2)}) copy-start(s32[32]{0:T(128)} %partner.1) | copy-start | bytes 388
  80.1 0.7 copy-start
  80.1 93.6 %all-gather.3.cloned.1.call-start = ((), (), s32[]{:S(2)}) async-start(), calls=%async_computation.7 | async-start | bytes 4177920 | tf_op jit(solution)/shard_map/all_gather | solution.py:300
  125.2 94.9 %all-gather.5.cloned.1.call-start = ((), (), s32[]{:S(2)}) async-start(), calls=%async_computation.8 | async-start | bytes 4177920 | tf_op jit(solution)/shard_map/all_gather | solution.py:332
  179.4 9.4 %copy-start.4 = (s32[64,8]{0,1:T(8,128)S(1)}, s32[64,8]{0,1:T(8,128)}, u32[]{:S(2)}) copy-start(s32[64,8]{0,1:T(8,128)} %param.11) | copy-start | bytes 6148
  179.4 9.4 %copy-start.5 = (bf16[64,8]{0,1:T(8,128)(2,1)S(1)}, bf16[64,8]{0,1:T(8,128)(2,1)}, u32[]{:S(2)}) copy-start(bf16[64,8]{0,1:T(8,128)(2,1)} %param.12) | copy-start | bytes 3076
  179.4 62.4 %all-to-all-start.2 = ((bf16[32,40,896]{2,1,0:T(8,128)(2,1)}), bf16[32,40,896]{2,1,0:T(8,128)(2,1)S(1)}, u32[]{:S(2)}, u32[]{:S(2)}) async-start(bf16[32,40,896]{2,1,0:T(8,128)(2,1)} %bitcast.47), calls=%async_computation.3 | async-start | bytes 4587520 | tf_op jit(solution)/shard_map/all_to_all | solution.py:222
Sparse Core Ops, SparseCore 0:
  80.3 42.5 reduce-scatter.1
  125.8 47.8 all-gather.2
  176.6 43.4 all-gather.4

commit v6 on v5

--- a/solution.py
+++ b/solution.py
@@ -103,13 +103,17 @@
 
 
 def rows_kernel(held, coords, packed_ref, after_ref, out_ref):
-    weights = weight_rows(packed_ref[:, 2 * FEAT :], tuple(held[4 * coords[0] + i] >> 1 for i in range(4)))
-    place = slot_places(weights)
+    experts = tuple(held[4 * coords[0] + i] >> 1 for i in range(4))
     cot_lane = lax.broadcasted_iota(jnp.int32, (HALF, 2 * FEAT), 1) >= FEAT
-    for i in range(4):
-        hit = one_hot(place[i : i + 1], HALF)
-        rows = dot(as_matrix(hit), packed_ref[:, : 2 * FEAT])
-        out_ref[i, ...] = (rows * jnp.where(cot_lane, slot_weights(hit, weights[i : i + 1]), 1.0)).astype(BF).reshape(out_ref.shape[1:])
+    for pair in range(out_ref.shape[1]):
+        packed = packed_ref[pair * PAIR : (pair + 1) * PAIR]
+        weights = weight_rows(packed[:, 2 * FEAT :], experts)
+        place = slot_places(weights)
+        hits = [one_hot(place[i : i + 1], HALF) for i in range(4)]
+        rows = dot(jnp.concatenate([as_matrix(hit) for hit in hits], axis=0), packed[:, : 2 * FEAT])
+        for i, hit in enumerate(hits):
+            factor = jnp.where(cot_lane, slot_weights(hit, weights[i : i + 1]), 1.0)
+            out_ref[i, pair] = (rows[i * HALF : (i + 1) * HALF] * factor).astype(BF)
 
 
 def products_kernel(coords, rows_ref, gate_ref, up_ref, down_ref, out_ref):
@@ -238,22 +242,22 @@
     )
     column = lax.all_gather(packed, "y", tiled=True)
 
-    def slab_rows(held, after, block, shape):
-        return call(
+    def slab_rows(held, after, shape):
+        sent = call(
             rows_kernel,
-            (4,),
-            [lead_block(PAIR, PACK), ANYWHERE],
-            block,
-            pltpu.HBM(shape, BF),
+            (2,),
+            [lead_block(2 * PAIR, PACK), ANYWHERE],
+            pl.BlockSpec((4, 2, HALF, 2 * FEAT), lambda i, *scalars: (0, i, 0, 0)),
+            shape,
             cost(600, 3500),
             (held, coords),
             column,
             in_hbm(after),
         )
-
-    in_pairs = pl.BlockSpec((4, 1, HALF, 2 * FEAT), lambda i, *scalars: (0, i, 0, 0))
-    sent = slab_rows(held_before, held_before, in_pairs, (4, 4, HALF, 2 * FEAT))
-    rows_view = exchange(sent.reshape(4, 4 * HALF, 2 * FEAT), "x").reshape(8, 2, HALF, 2 * FEAT)
+        return exchange(sent.reshape(4, 4 * HALF, 2 * FEAT), "x")
+
+    sent_shape = (4, 4, HALF, 2 * FEAT)
+    rows_view = slab_rows(held_before, held_before, shaped(*sent_shape)).reshape(8, 2, HALF, 2 * FEAT)
 
     def products(mine):
         return call(
@@ -273,9 +277,9 @@
     got = swap(products(False))
     pairs = call(
         add_kernel,
-        (4,),
-        [lead_block(2, HALF, 3 * HID)] * 2,
-        lead_block(2, HALF, 3 * HID),
+        (2,),
+        [lead_block(4, HALF, 3 * HID)] * 2,
+        lead_block(4, HALF, 3 * HID),
         pltpu.HBM((8, HALF, 3 * HID), BF),
         cost(1, 6000),
         (coords,),
@@ -283,8 +287,7 @@
         got,
     )
     sums = lax.psum_scatter(pairs.reshape(8 * HALF, 3 * HID), "z", scatter_dimension=0, tiled=True)
-    new_sent = slab_rows(jnp.take(held_before, partner), pairs, in_pairs, (4, 4, HALF, 2 * FEAT))
-    new_rows = exchange(new_sent.reshape(4, 4 * HALF, 2 * FEAT), "x")
+    new_rows = slab_rows(jnp.take(held_before, partner), pairs, pltpu.HBM(sent_shape, BF))
     three, acts = call(
         activation_kernel,
         (1,),

time: 251 us -> 249 us (level)
  transfers between devices with their start and end apart: 5 -> 5, of which waited for: 5 -> 5; matrix products, arithmetic and copies ran while one was open for 1% -> 1% of each run, Pallas kernels for 8% -> 7%
where the time goes in v6:
time: 249 us; the launch traced here: 248 us
  blocking collectives  113 us (45%)
  waiting for transfers between devices  67.7 us (27%)
  Pallas kernels  30.1 us (12%)
  starting transfers between devices  20.9 us (8%)
  between operations  13.9 us (6%)
    all_to_all x4, blocking collectives, exchange(): return lax.all_to_all(value, axes, split_axis=0, concat_axis=0, tiled=True)  89.5 us
    all_gather x1, waiting for transfers between devices, body(): lax.all_gather(moved[:3 * HALF], ('z', 'core'), tiled=True)  30.2 us
    all_gather x1, blocking collectives, body(): column = lax.all_gather(packed, 'y', tiled=True)  23.5 us
    pallas_call x9, Pallas kernels, call(): pl.pallas_call(kernel, grid_spec=pltpu.PrefetchScalarGridSpec(num_scalar_...  22.1 us
    all_to_all x1, waiting for transfers between devices, exchange(): return lax.all_to_all(value, axes, split_axis=0, concat_axis=0, tiled=True)  16.2 us
    all_gather x1, waiting for transfers between devices, body(): lax.all_gather(three, ('z', 'core'), tiled=True)  14.2 us
    ppermute x1, starting transfers between devices, swap(): return lax.ppermute(value, 'core', [(0, 1), (1, 0)])  11.3 us
    all_to_all x1, starting transfers between devices, exchange(): return lax.all_to_all(value, axes, split_axis=0, concat_axis=0, tiled=True)  9.39 us
  transfers between devices with their start and end apart: 5, of which 5 were waited for; matrix products, arithmetic and copies ran while one was open for 1% of the time, Pallas kernels for 7%

profile of v6, /device:TPU:1, one launch (start us, length us, event | category | flops | bytes accessed | tf_op | source)
XLA Modules:
  0.0 247.6 jit_solution(637469975908034478)
XLA Ops:
  7.2 0.0 reduce-scatter.2.cloned.1.call-start
  7.2 1.1 shard_map.129
  8.3 23.5 %all_gather.9.packed_ref = bf16[512,960]{1,0:T(8,128)(2,1)S(1)} all-gather(bf16[64,960]{1,0:T(8,128)(2,1)S(1)} %shard_map.129), channel_id=1, replica_groups=mesh['y'=8,'x'=4,'z'=8,'core'=2] {'y'}, dimensions={0}, use_global_device_ids=true | all-gather | bytes 1105920 | tf_op jit(solution)/shard_map/all_gather | solution.py:243
  31.8 0.1 pad_add_fusion.coords
  31.8 2.8 %shard_map.130 = bf16[4,4,80,896]{3,2,1,0:T(8,128)(2,1)S(1)} custom-call(s32[32]{0:T(128)} %after_ref.1, s32[3]{0:T(128)S(1)} %pad_add_fusion.coords, bf16[512,960]{1,0:T(8,128)(2,1)S(1)} %all_gather.9.packed_ref, s32[32]{0:T(128)} %after_ref.1), custom_call_target="tpu_custom_call" | custom-call | flops 600000000 | bytes 3500000 | tf_op jit(solution)/shard_map/pallas_call | solution.py:185
  34.7 24.3 %all_to_all.25 = bf16[4,320,896]{2,1,0:T(8,128)(2,1)S(1)} all-to-all(bf16[4,320,896]{2,1,0:T(8,128)(2,1)S(1)} %bitcast.30), channel_id=1, replica_groups=mesh['y'=8,'x'=4,'z'=8,'core'=2] {'x'}, dimensions={0} | all-to-all | bytes 4587520 | tf_op jit(solution)/shard_map/all_to_all | solution.py:226
  59.0 2.1 shard_map.132
  61.1 11.3 %collective-permute-start = (bf16[8,80,1536]{2,1,0:T(8,128)(2,1)S(1)}, bf16[8,80,1536]{2,1,0:T(8,128)(2,1)S(1)}, u32[]{:S(2)}, u32[]{:S(2)}) collective-permute-start(bf16[8,80,1536]{2,1,0:T(8,128)(2,1)S(1)} %shard_map.132), channel_id=1, source_target_pairs={{0,1},{1,0},{2,3},{3,2},{4,5},{5,4},{6,7},{7,6},{8,9},{9,8},{10,11... | collective-permute-start | bytes 5898248 | tf_op jit(solution)/shard_map/ppermute | solution.py:222
  72.4 2.1 shard_map.131.own_ref
  74.5 1.5 collective-permute-done.got_ref
  76.0 2.1 shard_map.133.after_ref
  78.1 0.0 reduce-scatter.2.cloned.1.call-update
  78.1 0.0 all-gather.3.cloned.1.call-start
  78.2 0.5 copy-done
  78.7 0.7 gather_fusion
  79.4 3.6 %shard_map.134 = bf16[4,4,80,896]{3,2,1,0:T(8,128)(2,1)} custom-call(s32[32]{0:T(128)S(1)} %and_select_fusion.held, s32[3]{0:T(128)S(1)} %pad_add_fusion.coords, bf16[512,960]{1,0:T(8,128)(2,1)S(1)} %all_gather.9.packed_ref, bf16[8,80,1536]{2,1,0:T(8,128)(2,1)} %shard_map.133.after_ref), custom_call_target="tpu_custom_call" | custom-call | flops 600000000 | bytes 3500000 | tf_op jit(solution)/shard_map/pallas_call | solution.py:185
  83.0 32.4 %all_to_all.26.after_ref = bf16[4,320,896]{2,1,0:T(8,128)(2,1)} all-to-all(bf16[4,320,896]{2,1,0:T(8,128)(2,1)} %bitcast.46), channel_id=1, replica_groups=mesh['y'=8,'x'=4,'z'=8,'core'=2] {'x'}, dimensions={0} | all-to-all | bytes 4587520 | tf_op jit(solution)/shard_map/all_to_all | solution.py:226
  115.4 5.5 %reduce-scatter.2.cloned.1.call-done.sums_ref = bf16[80,1536]{1,0:T(8,128)(2,1)} async-done(((bf16[640,1536]{1,0:T(8,128)(2,1)}), bf16[80,1536]{1,0:T(8,128)(2,1)}) %reduce-scatter.2.cloned.1.call-update) | async-done | bytes 245776 | tf_op jit(solution)/shard_map/reduce_scatter | solution.py:289
  120.9 2.3 shard_map.135
  123.2 0.0 all-gather.5.cloned.1.call-start
  123.3 18.9 %all_to_all.27.pieces_ref = bf16[32,8,512]{2,1,0:T(8,128)(2,1)S(1)} all-to-all(bf16[32,8,512]{2,1,0:T(8,128)(2,1)S(1)} %bitcast.40), channel_id=1, replica_groups=mesh['y'=8,'x'=4,'z'=8,'core'=2] {'y','x'}, dimensions={0} | all-to-all | bytes 524288 | tf_op jit(solution)/shard_map/all_to_all | solution.py:226
  142.2 0.6 shard_map.138
  142.8 13.9 %all_to_all.28 = bf16[32,8,512]{2,1,0:T(8,128)(2,1)S(1)} all-to-all(bf16[32,8,512]{2,1,0:T(8,128)(2,1)S(1)} %shard_map.138), channel_id=1, replica_groups=mesh['y'=8,'x'=4,'z'=8,'core'=2] {'y','x'}, dimensions={0} | all-to-all | bytes 524288 | tf_op jit(solution)/shard_map/all_to_all | solution.py:226
  156.6 0.7 slice_bitcast_fusion
  157.4 14.2 %all-gather.3.cloned.1.call-done = bf16[3840,512]{1,0:T(8,128)(2,1)} async-done(((bf16[240,512]{1,0:T(8,128)(2,1)}), bf16[3840,512]{1,0:T(8,128)(2,1)}) %all-gather.3.cloned.1.call-update) | async-done | bytes 3932176 | tf_op jit(solution)/shard_map/all_gather | solution.py:303
  171.6 5.7 %shard_map.136 = bf16[1280,896]{1,0:T(8,128)(2,1)} custom-call(s32[3]{0:T(128)S(1)} %pad_add_fusion.coords, bf16[16,240,512]{2,1,0:T(8,128)(2,1)} %bitcast.49, bf16[448,512]{1,0:T(8,128)(2,1)S(1)} %bitcast.33, bf16[448,512]{1,0:T(8,128)(2,1)S(1)} %bitcast.36, bf16[448,512]{1,0:T(8,128)(2,1)S(1)} %bitcast.39), custom_call_target="tpu_custom_call" | custom-call | flops 1800000000 | bytes 8000000 | tf_op jit(solution)/shard_map/pallas_call | solution.py:185
  177.3 9.4 %all-to-all-start.2 = ((bf16[32,40,896]{2,1,0:T(8,128)(2,1)}), bf16[32,40,896]{2,1,0:T(8,128)(2,1)S(1)}, u32[]{:S(2)}, u32[]{:S(2)}) async-start(bf16[32,40,896]{2,1,0:T(8,128)(2,1)} %bitcast.48), calls=%async_computation.3 | async-start | bytes 4587520 | tf_op jit(solution)/shard_map/all_to_all | solution.py:226
  186.7 1.1 shard_map.128
  187.8 30.2 %all-gather.5.cloned.1.call-done = bf16[3840,512]{1,0:T(8,128)(2,1)} async-done(((bf16[240,512]{1,0:T(8,128)(2,1)}), bf16[3840,512]{1,0:T(8,128)(2,1)}) %all-gather.5.cloned.1.call-update) | async-done | bytes 3932176 | tf_op jit(solution)/shard_map/all_gather | solution.py:335
  218.0 5.6 %shard_map.139 = (bf16[448,512]{1,0:T(8,128)(2,1)}, bf16[448,512]{1,0:T(8,128)(2,1)}, bf16[448,512]{1,0:T(8,128)(2,1)}) custom-call(bf16[1280,896]{1,0:T(8,128)(2,1)} %bitcast.47, bf16[16,240,512]{2,1,0:T(8,128)(2,1)} %bitcast.50), custom_call_target="tpu_custom_call" | custom-call | flops 1800000000 | bytes 8000000 | tf_op jit(solution)/shard_map/pallas_call | solution.py:197
  223.5 16.2 %all-to-all-done.2 = bf16[32,40,896]{2,1,0:T(8,128)(2,1)S(1)} async-done(((bf16[32,40,896]{2,1,0:T(8,128)(2,1)}), bf16[32,40,896]{2,1,0:T(8,128)(2,1)S(1)}, u32[]{:S(2)}, u32[]{:S(2)}) %all-to-all-start.2) | async-done | bytes 2293792 | tf_op jit(solution)/shard_map/all_to_all | solution.py:226
  239.7 1.3 shard_map.137
  (18 shorter events, 0.1 us)
Async XLA Ops:
  7.2 113.8 %reduce-scatter.2.cloned.1.call-start = ((), (), s32[]{:S(2)}) async-start(), calls=%async_computation.6 | async-start | bytes 2211840 | tf_op jit(solution)/shard_map/reduce_scatter | solution.py:289
  34.6 24.4 %copy-start.1 = (bf16[1,448,512]{2,1,0:T(8,128)(2,1)S(1)}, bf16[1,448,512]{2,1,0:T(8,128)(2,1)}, u32[]{:S(2)}) copy-start(bf16[1,448,512]{2,1,0:T(8,128)(2,1)} %param.15) | copy-start | bytes 1376260
  34.6 24.4 %copy-start.2 = (bf16[1,448,512]{2,1,0:T(8,128)(2,1)S(1)}, bf16[1,448,512]{2,1,0:T(8,128)(2,1)}, u32[]{:S(2)}) copy-start(bf16[1,448,512]{2,1,0:T(8,128)(2,1)} %param.16) | copy-start | bytes 1376260
  34.7 24.3 %copy-start.3 = (bf16[1,512,448]{1,2,0:T(8,128)(2,1)S(1)}, bf16[1,512,448]{1,2,0:T(8,128)(2,1)}, u32[]{:S(2)}) copy-start(bf16[1,512,448]{1,2,0:T(8,128)(2,1)} %param.17) | copy-start | bytes 1376260
  61.1 14.9 %collective-permute-start = (bf16[8,80,1536]{2,1,0:T(8,128)(2,1)S(1)}, bf16[8,80,1536]{2,1,0:T(8,128)(2,1)S(1)}, u32[]{:S(2)}, u32[]{:S(2)}) collective-permute-start(bf16[8,80,1536]{2,1,0:T(8,128)(2,1)S(1)} %shard_map.132), channel_id=1, source_target_pairs={{0,1},{1,0},{2,3},{3,2},{4,5},{5,4},{6,7},{7,6},{8,9},{9,8},{10,11... | collective-permute-start | bytes 5898248 | tf_op jit(solution)/shard_map/ppermute | solution.py:222
  74.5 3.7 %copy-start.6 = (s32[32]{0:T(128)S(1)}, s32[32]{0:T(128)}, u32[]{:S(2)}) copy-start(s32[32]{0:T(128)} %partner.1) | copy-start | bytes 388
  78.0 0.7 copy-start
  78.1 93.5 %all-gather.3.cloned.1.call-start = ((), (), s32[]{:S(2)}) async-start(), calls=%async_computation.7 | async-start | bytes 4177920 | tf_op jit(solution)/shard_map/all_gather | solution.py:303
  123.2 94.8 %all-gather.5.cloned.1.call-start = ((), (), s32[]{:S(2)}) async-start(), calls=%async_computation.8 | async-start | bytes 4177920 | tf_op jit(solution)/shard_map/all_gather | solution.py:335
  177.3 9.4 %copy-start.4 = (s32[64,8]{0,1:T(8,128)S(1)}, s32[64,8]{0,1:T(8,128)}, u32[]{:S(2)}) copy-start(s32[64,8]{0,1:T(8,128)} %param.11) | copy-start | bytes 6148
  177.3 9.4 %copy-start.5 = (bf16[64,8]{0,1:T(8,128)(2,1)S(1)}, bf16[64,8]{0,1:T(8,128)(2,1)}, u32[]{:S(2)}) copy-start(bf16[64,8]{0,1:T(8,128)(2,1)} %param.12) | copy-start | bytes 3076
  177.3 62.4 %all-to-all-start.2 = ((bf16[32,40,896]{2,1,0:T(8,128)(2,1)}), bf16[32,40,896]{2,1,0:T(8,128)(2,1)S(1)}, u32[]{:S(2)}, u32[]{:S(2)}) async-start(bf16[32,40,896]{2,1,0:T(8,128)(2,1)} %bitcast.48), calls=%async_computation.3 | async-start | bytes 4587520 | tf_op jit(solution)/shard_map/all_to_all | solution.py:226
Sparse Core Ops, SparseCore 0:
  78.2 42.6 reduce-scatter.1
  123.8 47.7 all-gather.2
  174.5 43.4 all-gather.4

commit v7 on v6

--- a/solution.py
+++ b/solution.py
@@ -72,7 +72,8 @@
 
 
 def weights_of(names, ids_ref, probs_ref):
-    return sum(jnp.where(ids_ref[k : k + 1] == names, probs_ref[k : k + 1].astype(F32), 0.0) for k in range(8))
+    ids, probs = ids_ref[...], probs_ref[...].astype(F32)
+    return sum(jnp.where(ids[k : k + 1] == names, probs[k : k + 1], 0.0) for k in range(8))
 
 
 def pack_kernel(tok_ref, cot_ref, ids_ref, probs_ref, packed_ref):

time: 249 us -> 249 us (level)
  no operation moved by 1% of the time
where the time goes in v7:
time: 249 us; the launch traced here: 248 us
  blocking collectives  113 us (45%)
  waiting for transfers between devices  67.7 us (27%)
  Pallas kernels  30.1 us (12%)
  starting transfers between devices  20.9 us (8%)
  between operations  13.9 us (6%)
    all_to_all x4, blocking collectives, exchange(): return lax.all_to_all(value, axes, split_axis=0, concat_axis=0, tiled=True)  89.5 us
    all_gather x1, waiting for transfers between devices, body(): lax.all_gather(moved[:3 * HALF], ('z', 'core'), tiled=True)  30.2 us
    all_gather x1, blocking collectives, body(): column = lax.all_gather(packed, 'y', tiled=True)  23.5 us
    pallas_call x9, Pallas kernels, call(): pl.pallas_call(kernel, grid_spec=pltpu.PrefetchScalarGridSpec(num_scalar_...  22.1 us
    all_to_all x1, waiting for transfers between devices, exchange(): return lax.all_to_all(value, axes, split_axis=0, concat_axis=0, tiled=True)  16.2 us
    all_gather x1, waiting for transfers between devices, body(): lax.all_gather(three, ('z', 'core'), tiled=True)  14.2 us
    ppermute x1, starting transfers between devices, swap(): return lax.ppermute(value, 'core', [(0, 1), (1, 0)])  11.3 us
    all_to_all x1, starting transfers between devices, exchange(): return lax.all_to_all(value, axes, split_axis=0, concat_axis=0, tiled=True)  9.39 us
  transfers between devices with their start and end apart: 5, of which 5 were waited for; matrix products, arithmetic and copies ran while one was open for 1% of the time, Pallas kernels for 7%

profile of v7, /device:TPU:1, one launch (start us, length us, event | category | flops | bytes accessed | tf_op | source)
XLA Modules:
  0.0 247.6 jit_solution(9361464048330025071)
XLA Ops:
  7.2 0.0 reduce-scatter.2.cloned.1.call-start
  7.2 1.1 shard_map.129
  8.3 23.5 %all_gather.9.packed_ref = bf16[512,960]{1,0:T(8,128)(2,1)S(1)} all-gather(bf16[64,960]{1,0:T(8,128)(2,1)S(1)} %shard_map.129), channel_id=1, replica_groups=mesh['y'=8,'x'=4,'z'=8,'core'=2] {'y'}, dimensions={0}, use_global_device_ids=true | all-gather | bytes 1105920 | tf_op jit(solution)/shard_map/all_gather | solution.py:244
  31.8 0.1 pad_add_fusion.coords
  31.8 2.8 %shard_map.130 = bf16[4,4,80,896]{3,2,1,0:T(8,128)(2,1)S(1)} custom-call(s32[32]{0:T(128)} %after_ref.1, s32[3]{0:T(128)S(1)} %pad_add_fusion.coords, bf16[512,960]{1,0:T(8,128)(2,1)S(1)} %all_gather.9.packed_ref, s32[32]{0:T(128)} %after_ref.1), custom_call_target="tpu_custom_call" | custom-call | flops 600000000 | bytes 3500000 | tf_op jit(solution)/shard_map/pallas_call | solution.py:186
  34.7 24.3 %all_to_all.25 = bf16[4,320,896]{2,1,0:T(8,128)(2,1)S(1)} all-to-all(bf16[4,320,896]{2,1,0:T(8,128)(2,1)S(1)} %bitcast.30), channel_id=1, replica_groups=mesh['y'=8,'x'=4,'z'=8,'core'=2] {'x'}, dimensions={0} | all-to-all | bytes 4587520 | tf_op jit(solution)/shard_map/all_to_all | solution.py:227
  59.0 2.1 shard_map.132
  61.1 11.3 %collective-permute-start = (bf16[8,80,1536]{2,1,0:T(8,128)(2,1)S(1)}, bf16[8,80,1536]{2,1,0:T(8,128)(2,1)S(1)}, u32[]{:S(2)}, u32[]{:S(2)}) collective-permute-start(bf16[8,80,1536]{2,1,0:T(8,128)(2,1)S(1)} %shard_map.132), channel_id=1, source_target_pairs={{0,1},{1,0},{2,3},{3,2},{4,5},{5,4},{6,7},{7,6},{8,9},{9,8},{10,11... | collective-permute-start | bytes 5898248 | tf_op jit(solution)/shard_map/ppermute | solution.py:223
  72.4 2.1 shard_map.131.own_ref
  74.5 1.5 collective-permute-done.got_ref
  76.0 2.1 shard_map.133.after_ref
  78.1 0.0 reduce-scatter.2.cloned.1.call-update
  78.1 0.0 all-gather.3.cloned.1.call-start
  78.2 0.5 copy-done
  78.7 0.7 gather_fusion
  79.4 3.6 %shard_map.134 = bf16[4,4,80,896]{3,2,1,0:T(8,128)(2,1)} custom-call(s32[32]{0:T(128)S(1)} %and_select_fusion.held, s32[3]{0:T(128)S(1)} %pad_add_fusion.coords, bf16[512,960]{1,0:T(8,128)(2,1)S(1)} %all_gather.9.packed_ref, bf16[8,80,1536]{2,1,0:T(8,128)(2,1)} %shard_map.133.after_ref), custom_call_target="tpu_custom_call" | custom-call | flops 600000000 | bytes 3500000 | tf_op jit(solution)/shard_map/pallas_call | solution.py:186
  83.0 32.4 %all_to_all.26.after_ref = bf16[4,320,896]{2,1,0:T(8,128)(2,1)} all-to-all(bf16[4,320,896]{2,1,0:T(8,128)(2,1)} %bitcast.46), channel_id=1, replica_groups=mesh['y'=8,'x'=4,'z'=8,'core'=2] {'x'}, dimensions={0} | all-to-all | bytes 4587520 | tf_op jit(solution)/shard_map/all_to_all | solution.py:227
  115.4 5.5 %reduce-scatter.2.cloned.1.call-done.sums_ref = bf16[80,1536]{1,0:T(8,128)(2,1)} async-done(((bf16[640,1536]{1,0:T(8,128)(2,1)}), bf16[80,1536]{1,0:T(8,128)(2,1)}) %reduce-scatter.2.cloned.1.call-update) | async-done | bytes 245776 | tf_op jit(solution)/shard_map/reduce_scatter | solution.py:290
  120.9 2.3 shard_map.135
  123.2 0.0 all-gather.5.cloned.1.call-start
  123.3 18.9 %all_to_all.27.pieces_ref = bf16[32,8,512]{2,1,0:T(8,128)(2,1)S(1)} all-to-all(bf16[32,8,512]{2,1,0:T(8,128)(2,1)S(1)} %bitcast.40), channel_id=1, replica_groups=mesh['y'=8,'x'=4,'z'=8,'core'=2] {'y','x'}, dimensions={0} | all-to-all | bytes 524288 | tf_op jit(solution)/shard_map/all_to_all | solution.py:227
  142.2 0.6 shard_map.138
  142.8 13.9 %all_to_all.28 = bf16[32,8,512]{2,1,0:T(8,128)(2,1)S(1)} all-to-all(bf16[32,8,512]{2,1,0:T(8,128)(2,1)S(1)} %shard_map.138), channel_id=1, replica_groups=mesh['y'=8,'x'=4,'z'=8,'core'=2] {'y','x'}, dimensions={0} | all-to-all | bytes 524288 | tf_op jit(solution)/shard_map/all_to_all | solution.py:227
  156.6 0.7 slice_bitcast_fusion
  157.4 14.2 %all-gather.3.cloned.1.call-done = bf16[3840,512]{1,0:T(8,128)(2,1)} async-done(((bf16[240,512]{1,0:T(8,128)(2,1)}), bf16[3840,512]{1,0:T(8,128)(2,1)}) %all-gather.3.cloned.1.call-update) | async-done | bytes 3932176 | tf_op jit(solution)/shard_map/all_gather | solution.py:304
  171.6 5.7 %shard_map.136 = bf16[1280,896]{1,0:T(8,128)(2,1)} custom-call(s32[3]{0:T(128)S(1)} %pad_add_fusion.coords, bf16[16,240,512]{2,1,0:T(8,128)(2,1)} %bitcast.49, bf16[448,512]{1,0:T(8,128)(2,1)S(1)} %bitcast.33, bf16[448,512]{1,0:T(8,128)(2,1)S(1)} %bitcast.36, bf16[448,512]{1,0:T(8,128)(2,1)S(1)} %bitcast.39), custom_call_target="tpu_custom_call" | custom-call | flops 1800000000 | bytes 8000000 | tf_op jit(solution)/shard_map/pallas_call | solution.py:186
  177.3 9.4 %all-to-all-start.2 = ((bf16[32,40,896]{2,1,0:T(8,128)(2,1)}), bf16[32,40,896]{2,1,0:T(8,128)(2,1)S(1)}, u32[]{:S(2)}, u32[]{:S(2)}) async-start(bf16[32,40,896]{2,1,0:T(8,128)(2,1)} %bitcast.48), calls=%async_computation.3 | async-start | bytes 4587520 | tf_op jit(solution)/shard_map/all_to_all | solution.py:227
  186.7 1.1 shard_map.128
  187.8 30.2 %all-gather.5.cloned.1.call-done = bf16[3840,512]{1,0:T(8,128)(2,1)} async-done(((bf16[240,512]{1,0:T(8,128)(2,1)}), bf16[3840,512]{1,0:T(8,128)(2,1)}) %all-gather.5.cloned.1.call-update) | async-done | bytes 3932176 | tf_op jit(solution)/shard_map/all_gather | solution.py:336
  218.0 5.6 %shard_map.139 = (bf16[448,512]{1,0:T(8,128)(2,1)}, bf16[448,512]{1,0:T(8,128)(2,1)}, bf16[448,512]{1,0:T(8,128)(2,1)}) custom-call(bf16[1280,896]{1,0:T(8,128)(2,1)} %bitcast.47, bf16[16,240,512]{2,1,0:T(8,128)(2,1)} %bitcast.50), custom_call_target="tpu_custom_call" | custom-call | flops 1800000000 | bytes 8000000 | tf_op jit(solution)/shard_map/pallas_call | solution.py:198
  223.5 16.2 %all-to-all-done.2 = bf16[32,40,896]{2,1,0:T(8,128)(2,1)S(1)} async-done(((bf16[32,40,896]{2,1,0:T(8,128)(2,1)}), bf16[32,40,896]{2,1,0:T(8,128)(2,1)S(1)}, u32[]{:S(2)}, u32[]{:S(2)}) %all-to-all-start.2) | async-done | bytes 2293792 | tf_op jit(solution)/shard_map/all_to_all | solution.py:227
  239.7 1.3 shard_map.137
  (18 shorter events, 0.1 us)
Async XLA Ops:
  7.2 113.8 %reduce-scatter.2.cloned.1.call-start = ((), (), s32[]{:S(2)}) async-start(), calls=%async_computation.6 | async-start | bytes 2211840 | tf_op jit(solution)/shard_map/reduce_scatter | solution.py:290
  34.6 24.4 %copy-start.1 = (bf16[1,448,512]{2,1,0:T(8,128)(2,1)S(1)}, bf16[1,448,512]{2,1,0:T(8,128)(2,1)}, u32[]{:S(2)}) copy-start(bf16[1,448,512]{2,1,0:T(8,128)(2,1)} %param.15) | copy-start | bytes 1376260
  34.6 24.4 %copy-start.2 = (bf16[1,448,512]{2,1,0:T(8,128)(2,1)S(1)}, bf16[1,448,512]{2,1,0:T(8,128)(2,1)}, u32[]{:S(2)}) copy-start(bf16[1,448,512]{2,1,0:T(8,128)(2,1)} %param.16) | copy-start | bytes 1376260
  34.7 24.3 %copy-start.3 = (bf16[1,512,448]{1,2,0:T(8,128)(2,1)S(1)}, bf16[1,512,448]{1,2,0:T(8,128)(2,1)}, u32[]{:S(2)}) copy-start(bf16[1,512,448]{1,2,0:T(8,128)(2,1)} %param.17) | copy-start | bytes 1376260
  61.1 14.9 %collective-permute-start = (bf16[8,80,1536]{2,1,0:T(8,128)(2,1)S(1)}, bf16[8,80,1536]{2,1,0:T(8,128)(2,1)S(1)}, u32[]{:S(2)}, u32[]{:S(2)}) collective-permute-start(bf16[8,80,1536]{2,1,0:T(8,128)(2,1)S(1)} %shard_map.132), channel_id=1, source_target_pairs={{0,1},{1,0},{2,3},{3,2},{4,5},{5,4},{6,7},{7,6},{8,9},{9,8},{10,11... | collective-permute-start | bytes 5898248 | tf_op jit(solution)/shard_map/ppermute | solution.py:223
  74.5 3.7 %copy-start.6 = (s32[32]{0:T(128)S(1)}, s32[32]{0:T(128)}, u32[]{:S(2)}) copy-start(s32[32]{0:T(128)} %partner.1) | copy-start | bytes 388
  78.0 0.7 copy-start
  78.1 93.5 %all-gather.3.cloned.1.call-start = ((), (), s32[]{:S(2)}) async-start(), calls=%async_computation.7 | async-start | bytes 4177920 | tf_op jit(solution)/shard_map/all_gather | solution.py:304
  123.2 94.8 %all-gather.5.cloned.1.call-start = ((), (), s32[]{:S(2)}) async-start(), calls=%async_computation.8 | async-start | bytes 4177920 | tf_op jit(solution)/shard_map/all_gather | solution.py:336
  177.3 9.4 %copy-start.4 = (s32[64,8]{0,1:T(8,128)S(1)}, s32[64,8]{0,1:T(8,128)}, u32[]{:S(2)}) copy-start(s32[64,8]{0,1:T(8,128)} %param.11) | copy-start | bytes 6148
  177.3 9.4 %copy-start.5 = (bf16[64,8]{0,1:T(8,128)(2,1)S(1)}, bf16[64,8]{0,1:T(8,128)(2,1)}, u32[]{:S(2)}) copy-start(bf16[64,8]{0,1:T(8,128)(2,1)} %param.12) | copy-start | bytes 3076
  177.3 62.4 %all-to-all-start.2 = ((bf16[32,40,896]{2,1,0:T(8,128)(2,1)}), bf16[32,40,896]{2,1,0:T(8,128)(2,1)S(1)}, u32[]{:S(2)}, u32[]{:S(2)}) async-start(bf16[32,40,896]{2,1,0:T(8,128)(2,1)} %bitcast.48), calls=%async_computation.3 | async-start | bytes 4587520 | tf_op jit(solution)/shard_map/all_to_all | solution.py:227
Sparse Core Ops, SparseCore 0:
  78.2 42.6 reduce-scatter.1
  123.8 47.7 all-gather.2
  174.5 43.4 all-gather.4
